TPU v7x, 32 devices: a whole 2x2x4 slice. The times are simulated.
32 devices in a mesh: wide: 16 (over z, y, x), narrow: 2 (over core).
Axes of the slice: x: 2, y: 2, z: 4, core: 2. Of those that a mesh axis runs over, the one named last changes fastest.
Arguments:
- integrals: bfloat16 [4096, 65536], P('wide', 'narrow'), may hold values from -0.03125 to 0.03125
- amp_tiles: bfloat16 [2, 3145728], P('narrow', 'wide'), may hold values from -6 to 6
- row_orbitals: int32 [4096, 2], P('wide'), may hold values from 0 to 511
- orb_irrep: int32 [512], replicated, may hold values from 0 to 3
- occ_pairs: int32 [96, 2], replicated, may hold values from 0 to 15
- occ_irrep: int32 [16], replicated, may hold values from 0 to 3
Outputs:
- residual: float32 [4096, 96], P(('wide', 'narrow'))
All inputs are finite; a program needn't handle non-finite values.
Results may differ from a plain program's by a relative error of at most 0.0003.
Values may be sent and summed in bfloat16 or wider, within the bound.
No kernel may reach another device: no remote copies, remote signals or barrier semaphores. Data moves between devices by JAX's collectives and lax.ppermute only.
A program may use at most 64 MiB of HBM per device.

v0:
```python
import jax
import jax.numpy as jnp
from jax import lax
from jax.sharding import PartitionSpec as P


def lookup_irrep(orbitals, table):
    hits = orbitals[..., None] == jnp.arange(table.shape[0], dtype=jnp.int32)
    return jnp.sum(jnp.where(hits, table, 0), axis=-1)


def shards(integrals, amp_tiles, row_orbitals, orb_irrep, occ_pairs, occ_irrep):
    pair_count = occ_pairs.shape[0]
    column_count = integrals.shape[1]
    row_labels = lookup_irrep(row_orbitals, orb_irrep)
    pair_labels = lookup_irrep(occ_pairs, occ_irrep)
    row_sym = jnp.bitwise_xor(row_labels[:, 0], row_labels[:, 1])
    pair_sym = jnp.bitwise_xor(pair_labels[:, 0], pair_labels[:, 1])
    keep = row_sym[:, None] == pair_sym[None, :]
    gathered = lax.all_gather(amp_tiles, "wide", axis=1, tiled=True)
    amplitudes = gathered.reshape(column_count, pair_count)
    block = jnp.dot(integrals, amplitudes, preferred_element_type=jnp.float32)
    return lax.psum_scatter(
        jnp.where(keep, block, jnp.zeros_like(block)), "narrow", scatter_dimension=0, tiled=True
    )


def solution(mesh):
    in_specs = (P("wide", "narrow"), P("narrow", "wide"), P("wide", None), P(), P(), P())
    out_specs = P(("wide", "narrow"), None)
    return jax.shard_map(shards, mesh=mesh, in_specs=in_specs, out_specs=out_specs, check_vma=False)
```

profile of v0, /device:TPU:0, one launch (start us, length us, event | category | flops | bytes accessed | tf_op | source)
XLA Modules:
  0.0 336.5 jit_solution(854828648305792995)
XLA Ops:
  6.5 0.0 all-gather.2.cloned.1.call-start
  6.5 0.7 all-gather.2.cloned.1.call-update
  7.3 0.0 reduce-scatter.2.cloned.1.call-start
  7.3 0.8 select_reduce_fusion.1
  8.1 1.0 select_reduce_fusion
  9.1 155.8 %all-gather.2.cloned.1.call-done = bf16[1,3145728]{1,0:T(2,128)(2,1)} async-done(((bf16[1,196608]{1,0:T(2,128)(2,1)}), bf16[1,3145728]{1,0:T(2,128)(2,1)}) %all-gather.2.cloned.1.call-update) | async-done | bytes 6291472 | tf_op jit(solution)/shard_map/all_gather | solution.py:20
  164.9 134.2 %reduce = bf16[3145728]{0:T(1024)(128)(2,1)} reduce(bf16[1,3145728]{1,0:T(2,128)(2,1)} %all-gather.2.cloned.1.call-done, bf16[]{:T(256)} %constant.5), dimensions={0}, to_apply=%all_gather.3.reduce_sub_computation | reduce | bytes 12582914 | tf_op jit(solution)/shard_map/all_gather | solution.py:20
  299.1 13.2 %reshape.15 = bf16[32768,96]{1,0:T(8,128)(2,1)} reshape(bf16[3145728]{0:T(1024)(128)(2,1)} %reduce) | data formatting | bytes 12582912 | tf_op jit(solution)/shard_map/reshape | solution.py:21
  312.3 11.5 %convolution_select_fusion = f32[256,96]{0,1:T(8,128)} fusion(bf16[256,32768]{1,0:T(8,128)(2,1)} %param.6, bf16[32768,96]{1,0:T(8,128)(2,1)} %reshape.15, s32[256]{0:T(256)S(1)} %bitcast.5, s32[96]{0:T(128)S(1)} %xor_bitcast_fusion), kind=kOutput, calls=%fused_computation | convolution fusion | flops 1610661888 | bytes 23168384 | tf_op jit(solution)/shard_map/dot_general | solution.py:22
  323.8 0.0 reduce-scatter.2.cloned.1.call-update
  323.8 5.8 %reduce-scatter.2.cloned.1.call-done = f32[128,96]{0,1:T(8,128)} async-done(((f32[256,96]{0,1:T(8,128)}), f32[128,96]{0,1:T(8,128)}) %reduce-scatter.2.cloned.1.call-update) | async-done | bytes 49168 | tf_op jit(solution)/shard_map/reduce_scatter | solution.py:23
  (2 shorter events, 0.0 us)
Async XLA Ops:
  6.5 158.3 %all-gather.2.cloned.1.call-start = ((), (), s32[]{:S(2)}) async-start(), calls=%async_computation.1 | async-start | bytes 13369344 | tf_op jit(solution)/shard_map/all_gather | solution.py:20
  7.3 322.4 %reduce-scatter.2.cloned.1.call-start = ((), (), s32[]{:S(2)}) async-start(), calls=%async_computation.2 | async-start | bytes 147456 | tf_op jit(solution)/shard_map/reduce_scatter | solution.py:23
Sparse Core Ops, SparseCore 0:
  10.1 154.6 all-gather.1
  324.0 5.6 reduce-scatter.1
where the time goes:
time: 337 us
  waiting for transfers between devices  162 us (48%)
  other arithmetic  136 us (40%)
  between operations  13.4 us (4%)
  local copies, waits for them, and re-layouts  13.2 us (4%)
  matrix products  11.5 us (3%)
    all_gather x1, waiting for transfers between devices, shards(): gathered = lax.all_gather(amp_tiles, 'wide', axis=1, tiled=True)  156 us
    all_gather x1, other arithmetic, shards(): gathered = lax.all_gather(amp_tiles, 'wide', axis=1, tiled=True)  134 us
    reshape x1, local copies, waits for them, and re-layouts, shards(): amplitudes = gathered.reshape(column_count, pair_count)  13.2 us
    dot_general x1, matrix products, shards(): block = jnp.dot(integrals, amplitudes, preferred_element_type=jnp.float32)  11.5 us
  transfers between devices with their start and end apart: 2, of which 2 were waited for; matrix products, arithmetic and copies ran while one was open for 1% of the time, Pallas kernels for 0%

commit v1 on v0

v1 whole, which is shorter than its diff:
```python
import functools

import jax
import jax.numpy as jnp
from jax import lax
from jax.experimental import pallas as pl
from jax.experimental.pallas import tpu as pltpu
from jax.sharding import PartitionSpec as P

LANES = 128
X, Y, Z1, Z2 = 1, 2, 4, 8
STEPS = (
    ("A", Z1, "O"), ("XO", X, "O"), ("YO", Y, "O"), ("B", Z2, "O"),
    ("DO", X, "YO"), ("YA", Y, "A"), ("C", Z1, "B"), ("XB", X, "B"), ("YB", Y, "B"),
    ("DA", Z1, "DO"), ("XA", X, "A"), ("DB", Y, "XB"), ("YC", Y, "C"), ("XC", X, "C"),
    ("DC", Z1, "DB"),
)
GROUPS = (("O",), ("A", "XO", "YO", "B"), ("DO", "YA", "C"), ("XB", "YB", "DA"), ("XA", "DB", "YC"), ("XC", "DC"))


def lookup_irrep(orbitals, table):
    hits = orbitals[..., None] == jnp.arange(table.shape[0], dtype=jnp.int32)
    return jnp.sum(jnp.where(hits, table, 0), axis=-1)


def transpose_kernel(pairs, tile_ref, out_ref, flat, rows):
    depth = flat.shape[0] // 3
    flat[...] = tile_ref[...].astype(jnp.float32).reshape(flat.shape)
    x0, x1, x2 = [flat[pl.ds(s, depth, stride=3), :] for s in range(3)]
    lane = lax.broadcasted_iota(jnp.int32, x0.shape, 1)
    rows[pl.ds(0, depth, stride=4), :] = x0
    rows[pl.ds(1, depth, stride=4), :] = jnp.where(lane < 32, pltpu.roll(x0, 32, 1), pltpu.roll(x1, 32, 1))
    rows[pl.ds(2, depth, stride=4), :] = jnp.where(lane < 64, pltpu.roll(x1, 64, 1), pltpu.roll(x2, 64, 1))
    rows[pl.ds(3, depth, stride=4), :] = pltpu.roll(x2, 96, 1)
    out_ref[...] = rows[...].T[:pairs].astype(out_ref.dtype)


def transposed_tile(tile, pairs):
    size = tile.shape[1]
    return pl.pallas_call(
        functools.partial(transpose_kernel, pairs),
        out_shape=jax.ShapeDtypeStruct((pairs, size // pairs), tile.dtype),
        scratch_shapes=[
            pltpu.VMEM((size // LANES, LANES), jnp.float32),
            pltpu.VMEM((size // pairs, LANES), jnp.float32),
        ],
        name="transpose_tile",
    )(tile)


def product(left, right):
    return lax.dot_general(left, right, (((1,), (1,)), ((), ())), preferred_element_type=jnp.float32)


def group_kernel(count, has_total, columns_ref, integrals_ref, *refs):
    chunks, out_ref = refs[:count], refs[-1]
    step = pl.program_id(0)

    @pl.when(step == 0)
    def _():
        out_ref[...] = refs[count][...] if has_total else jnp.zeros_like(out_ref)

    for k in range(count):
        @pl.when(step == k)
        def _():
            out_ref[...] += product(integrals_ref[...], chunks[k][...])


def add_group(integrals, chunks, columns, total):
    rows = integrals.shape[0]
    pairs, depth = chunks[0].shape
    whole = lambda shape: pl.BlockSpec(shape, lambda i, c: (0, 0))
    extra = [] if total is None else [total]
    return pl.pallas_call(
        functools.partial(group_kernel, len(chunks), total is not None),
        out_shape=jax.ShapeDtypeStruct((rows, pairs), jnp.float32),
        grid_spec=pltpu.PrefetchScalarGridSpec(
            num_scalar_prefetch=1,
            grid=(len(chunks),),
            in_specs=[pl.BlockSpec((rows, depth), lambda i, c: (0, c[i]))]
            + [whole((pairs, depth))] * len(chunks) + [whole((rows, pairs))] * len(extra),
            out_specs=whole((rows, pairs)),
        ),
        cost_estimate=pl.CostEstimate(
            flops=2 * rows * depth * pairs * len(chunks), bytes_accessed=2 * rows * depth * len(chunks), transcendentals=0
        ),
        compiler_params=pltpu.CompilerParams(vmem_limit_bytes=16 * 2**20),
        name="add_group",
    )(columns, integrals, *chunks, *extra)


def ring_kernel(integrals_ref, chunk_ref, out_ref):
    @pl.when(pl.program_id(0) == 0)
    def _():
        out_ref[...] = jnp.zeros_like(out_ref)

    out_ref[...] += product(integrals_ref[...], chunk_ref[0])


def gathered_product(integrals, own, axis_size):
    rows, (pairs, depth) = integrals.shape[0], own.shape
    gathered = lax.all_gather(own, "wide", axis=0)
    return pl.pallas_call(
        ring_kernel,
        out_shape=jax.ShapeDtypeStruct((rows, pairs), jnp.float32),
        grid=(axis_size,),
        in_specs=[
            pl.BlockSpec((rows, depth), lambda i: (0, i)),
            pl.BlockSpec((1, pairs, depth), lambda i: (i, 0, 0)),
        ],
        out_specs=pl.BlockSpec((rows, pairs), lambda i: (0, 0)),
        name="gathered_product",
    )(integrals, gathered)


def exchanged_product(integrals, own):
    me = lax.axis_index("wide")
    held, distance = {"O": own}, {"O": 0}
    for name, step, source in STEPS:
        held[name] = lax.ppermute(held[source], "wide", [(i, i ^ step) for i in range(16)])
        distance[name] = distance[source] ^ step
    total = None
    for group in GROUPS:
        columns = jnp.stack([me ^ distance[name] for name in group]).astype(jnp.int32)
        total = add_group(integrals, [held[name] for name in group], columns, total)
    return total


def shards(wide, narrow, integrals, amp_tiles, row_orbitals, orb_irrep, occ_pairs, occ_irrep):
    pairs = occ_pairs.shape[0]
    part = integrals.shape[0] // narrow
    row_labels = lookup_irrep(row_orbitals, orb_irrep)
    pair_labels = lookup_irrep(occ_pairs, occ_irrep)
    row_sym = jnp.bitwise_xor(row_labels[:, 0], row_labels[:, 1])
    pair_sym = jnp.bitwise_xor(pair_labels[:, 0], pair_labels[:, 1])
    own = transposed_tile(amp_tiles, pairs)
    if (wide, narrow) != (16, 2):
        block = gathered_product(integrals, own, wide)
        block = jnp.where(row_sym[:, None] == pair_sym[None, :], block, jnp.zeros_like(block))
        return lax.psum_scatter(block, "narrow", scatter_dimension=0, tiled=True)
    total = exchanged_product(integrals, own)
    core = lax.axis_index("narrow")
    mine = lax.dynamic_slice_in_dim(total, core * part, part, 0)
    other = lax.dynamic_slice_in_dim(total, (1 - core) * part, part, 0)
    sym = lax.dynamic_slice_in_dim(row_sym, core * part, part, 0)
    summed = mine + lax.ppermute(other, "narrow", [(0, 1), (1, 0)])
    return jnp.where(sym[:, None] == pair_sym[None, :], summed, jnp.zeros_like(summed))


def solution(mesh):
    in_specs = (P("wide", "narrow"), P("narrow", "wide"), P("wide", None), P(), P(), P())
    out_specs = P(("wide", "narrow"), None)
    body = functools.partial(shards, mesh.shape["wide"], mesh.shape["narrow"])
    return jax.shard_map(body, mesh=mesh, in_specs=in_specs, out_specs=out_specs, check_vma=False)
```

time: 337 us -> 87.6 us (0.26)
  other arithmetic: 136 us -> 3.9 us
  waiting for transfers between devices: 162 us -> 31.5 us
  starting transfers between devices: 0.04 us -> 21.4 us
  Pallas kernels: 0 us -> 16.7 us
  between operations: 13.4 us -> 0.17 us
  matrix products: 11.5 us -> 0 us
    all_gather x1 -> x0, waiting for transfers between devices: 156 us -> none  [shards(): gathered = lax.all_gather(amp_tiles, 'wide', axis=1, tiled=True)]
    all_gather x1 -> x0, other arithmetic: 134 us -> none  [shards(): gathered = lax.all_gather(amp_tiles, 'wide', axis=1, tiled=True)]
    ppermute x0 -> x16, waiting for transfers between devices: none -> 31.5 us  [the longest x15 30.3 us: exchanged_product(): lax.ppermute(held[source], 'wide', [(i, i ^ step) for i in range(16)])]
    ppermute x0 -> x16, starting transfers between devices: none -> 21.4 us  [the longest x15 21.3 us: exchanged_product(): lax.ppermute(held[source], 'wide', [(i, i ^ step) for i in range(16)])]
    pallas_call x0 -> x7, Pallas kernels: none -> 16.7 us  [the longest x6 14.1 us: add_group(): pl.pallas_call(functools.partial(group_kernel, len(chunks), total is not...]
    reshape x1 -> x0, local copies, waits for them, and re-layouts: 13.2 us -> none  [shards(): amplitudes = gathered.reshape(column_count, pair_count)]
    unnamed x0 -> x16, local copies, waits for them, and re-layouts: none -> 12.9 us
    dot_general x1 -> x0, matrix products: 11.5 us -> none  [shards(): block = jnp.dot(integrals, amplitudes, preferred_element_type=jnp.float32)]
  transfers between devices with their start and end apart: 2 -> 16, of which waited for: 2 -> 6; matrix products, arithmetic and copies ran while one was open for 1% -> 4% of each run, Pallas kernels for 0% -> 14%
where the time goes in v1:
time: 87.6 us; the launch traced here: 87.2 us
  waiting for transfers between devices  31.5 us (36%)
  starting transfers between devices  21.4 us (24%)
  Pallas kernels  16.7 us (19%)
  local copies, waits for them, and re-layouts  13.6 us (16%)
  other arithmetic  3.9 us (4%)
    ppermute x15, waiting for transfers between devices, exchanged_product(): lax.ppermute(held[source], 'wide', [(i, i ^ step) for i in range(16)])  30.3 us
    ppermute x15, starting transfers between devices, exchanged_product(): lax.ppermute(held[source], 'wide', [(i, i ^ step) for i in range(16)])  21.3 us
    pallas_call x6, Pallas kernels, add_group(): pl.pallas_call(functools.partial(group_kernel, len(chunks), total is not...  14.1 us
    unnamed x16, local copies, waits for them, and re-layouts  12.9 us
    pallas_call x1, Pallas kernels, transposed_tile(): pl.pallas_call(functools.partial(transpose_kernel, pairs), out_shape=jax....  2.57 us
    reduce_sum x2, other arithmetic, lookup_irrep(): return jnp.sum(jnp.where(hits, table, 0), axis=-1)  2.32 us
  transfers between devices with their start and end apart: 16, of which 6 were waited for; matrix products, arithmetic and copies ran while one was open for 4% of the time, Pallas kernels for 14%

profile of v1, /device:TPU:0, one launch (start us, length us, event | category | flops | bytes accessed | tf_op | source)
XLA Modules:
  0.0 87.2 jit_solution(17907167976815207318)
XLA Ops:
  0.0 2.6 %transpose_tile.1.refs_0_ = bf16[96,2048]{1,0:T(8,128)(2,1)} custom-call(bf16[1,196608]{1,0:T(2,128)(2,1)} %tile_ref.1), custom_call_target="tpu_custom_call" | custom-call | tf_op jit(solution)/shard_map/transpose_tile/pallas_call | solution.py:40
  2.6 4.0 %collective-permute-start = (bf16[96,2048]{1,0:T(8,128)(2,1)}, bf16[96,2048]{1,0:T(8,128)(2,1)S(1)}, u32[]{:S(2)}, u32[]{:S(2)}) collective-permute-start(bf16[96,2048]{1,0:T(8,128)(2,1)} %transpose_tile.1.refs_0_), channel_id=1, source_target_pairs={{0,16},{2,18},{4,20},{6,22},{8,24},{10,26},{12,28},{14,30},{16,0},... | collective-permute-start | bytes 1179656 | tf_op jit(solution)/shard_map/ppermute | solution.py:120
  6.6 1.6 %collective-permute-start.6 = (bf16[96,2048]{1,0:T(8,128)(2,1)}, bf16[96,2048]{1,0:T(8,128)(2,1)S(1)}, u32[]{:S(2)}, u32[]{:S(2)}) collective-permute-start(bf16[96,2048]{1,0:T(8,128)(2,1)} %transpose_tile.1.refs_0_), channel_id=1, source_target_pairs={{0,8},{2,10},{4,12},{6,14},{8,0},{10,2},{12,4},{14,6},{16,24},{18,... | collective-permute-start | bytes 1179656 | tf_op jit(solution)/shard_map/ppermute | solution.py:120
  8.2 1.5 %collective-permute-start.10 = (bf16[96,2048]{1,0:T(8,128)(2,1)}, bf16[96,2048]{1,0:T(8,128)(2,1)S(1)}, u32[]{:S(2)}, u32[]{:S(2)}) collective-permute-start(bf16[96,2048]{1,0:T(8,128)(2,1)} %transpose_tile.1.refs_0_), channel_id=1, source_target_pairs={{0,4},{2,6},{4,0},{6,2},{8,12},{10,14},{12,8},{14,10},{16,20},{18,... | collective-permute-start | bytes 1179656 | tf_op jit(solution)/shard_map/ppermute | solution.py:120
  9.7 1.5 %collective-permute-start.14 = (bf16[96,2048]{1,0:T(8,128)(2,1)}, bf16[96,2048]{1,0:T(8,128)(2,1)S(1)}, u32[]{:S(2)}, u32[]{:S(2)}) collective-permute-start(bf16[96,2048]{1,0:T(8,128)(2,1)} %transpose_tile.1.refs_0_), channel_id=1, source_target_pairs={{0,2},{2,0},{4,6},{6,4},{8,10},{10,8},{12,14},{14,12},{16,18},{18,... | collective-permute-start | bytes 1179656 | tf_op jit(solution)/shard_map/ppermute | solution.py:120
  11.2 13.3 %collective-permute-done.refs_3_ = bf16[96,2048]{1,0:T(8,128)(2,1)S(1)} collective-permute-done((bf16[96,2048]{1,0:T(8,128)(2,1)}, bf16[96,2048]{1,0:T(8,128)(2,1)S(1)}, u32[]{:S(2)}, u32[]{:S(2)}) %collective-permute-start) | collective-permute-done | bytes 393248 | tf_op jit(solution)/shard_map/ppermute | solution.py:120
  24.5 1.5 %collective-permute-start.3 = (bf16[96,2048]{1,0:T(8,128)(2,1)S(1)}, bf16[96,2048]{1,0:T(8,128)(2,1)S(1)}, u32[]{:S(2)}, u32[]{:S(2)}) collective-permute-start(bf16[96,2048]{1,0:T(8,128)(2,1)S(1)} %collective-permute-done.refs_3_), channel_id=1, source_target_pairs={{0,2},{2,0},{4,6},{6,4},{8,10},{10,8},{12,14},{14,12},{16,18},{18,... | collective-permute-start | bytes 1179656 | tf_op jit(solution)/shard_map/ppermute | solution.py:120
  26.7 0.8 select_reduce_fusion.1
  27.5 0.7 collective-permute-start.1
  28.3 1.5 %collective-permute-start.9 = (bf16[96,2048]{1,0:T(8,128)(2,1)S(1)}, bf16[96,2048]{1,0:T(8,128)(2,1)S(1)}, u32[]{:S(2)}, u32[]{:S(2)}) collective-permute-start(bf16[96,2048]{1,0:T(8,128)(2,1)S(1)} %collective-permute-done.refs_3_), channel_id=1, source_target_pairs={{0,4},{2,6},{4,0},{6,2},{8,12},{10,14},{12,8},{14,10},{16,20},{18,... | collective-permute-start | bytes 1179656 | tf_op jit(solution)/shard_map/ppermute | solution.py:120
  30.8 5.7 %collective-permute-done.3.refs_0_ = bf16[96,2048]{1,0:T(8,128)(2,1)S(1)} collective-permute-done((bf16[96,2048]{1,0:T(8,128)(2,1)S(1)}, bf16[96,2048]{1,0:T(8,128)(2,1)S(1)}, u32[]{:S(2)}, u32[]{:S(2)}) %collective-permute-start.3) | collective-permute-done | bytes 393248 | tf_op jit(solution)/shard_map/ppermute | solution.py:120
  36.5 1.6 %collective-permute-start.4 = (bf16[96,2048]{1,0:T(8,128)(2,1)S(1)}, bf16[96,2048]{1,0:T(8,128)(2,1)}, u32[]{:S(2)}, u32[]{:S(2)}) collective-permute-start(bf16[96,2048]{1,0:T(8,128)(2,1)S(1)} %collective-permute-done.3.refs_0_), channel_id=1, source_target_pairs={{0,4},{2,6},{4,0},{6,2},{8,12},{10,14},{12,8},{14,10},{16,20},{18,... | collective-permute-start | bytes 1179656 | tf_op jit(solution)/shard_map/ppermute | solution.py:120
  38.2 1.5 %select_reduce_fusion = s32[256,2]{0,1:T(2,128)} fusion(s32[512]{0:T(512)} %param.9, s32[256,2]{0,1:T(2,128)} %param.8), kind=kLoop, calls=%fused_computation | loop fusion | flops 785920 | bytes 6144 | tf_op jit(solution)/shard_map/reduce_sum | solution.py:23
  39.7 0.6 xor_bitcast_fusion
  40.3 1.5 %collective-permute-start.7 = (bf16[96,2048]{1,0:T(8,128)(2,1)S(1)}, bf16[96,2048]{1,0:T(8,128)(2,1)}, u32[]{:S(2)}, u32[]{:S(2)}) collective-permute-start(bf16[96,2048]{1,0:T(8,128)(2,1)S(1)} %collective-permute-done.6.refs_0_), channel_id=1, source_target_pairs={{0,2},{2,0},{4,6},{6,4},{8,10},{10,8},{12,14},{14,12},{16,18},{18,... | collective-permute-start | bytes 1179656 | tf_op jit(solution)/shard_map/ppermute | solution.py:120
  41.8 3.3 %collective-permute-done.11.refs_0_ = bf16[96,2048]{1,0:T(8,128)(2,1)} collective-permute-done((bf16[96,2048]{1,0:T(8,128)(2,1)S(1)}, bf16[96,2048]{1,0:T(8,128)(2,1)}, u32[]{:S(2)}, u32[]{:S(2)}) %collective-permute-start.11) | collective-permute-done | bytes 393248 | tf_op jit(solution)/shard_map/ppermute | solution.py:120
  45.0 1.6 %collective-permute-start.8 = (bf16[96,2048]{1,0:T(8,128)(2,1)S(1)}, bf16[96,2048]{1,0:T(8,128)(2,1)}, u32[]{:S(2)}, u32[]{:S(2)}) collective-permute-start(bf16[96,2048]{1,0:T(8,128)(2,1)S(1)} %collective-permute-done.1.refs_2_), channel_id=1, source_target_pairs={{0,4},{2,6},{4,0},{6,2},{8,12},{10,14},{12,8},{14,10},{16,20},{18,... | collective-permute-start | bytes 1179656 | tf_op jit(solution)/shard_map/ppermute | solution.py:120
  46.6 2.1 %collective-permute-done.13.refs_1_ = bf16[96,2048]{1,0:T(8,128)(2,1)S(1)} collective-permute-done((bf16[96,2048]{1,0:T(8,128)(2,1)S(1)}, bf16[96,2048]{1,0:T(8,128)(2,1)S(1)}, u32[]{:S(2)}, u32[]{:S(2)}) %collective-permute-start.13) | collective-permute-done | bytes 393248 | tf_op jit(solution)/shard_map/ppermute | solution.py:120
  48.7 0.8 copy-done.3
  50.0 1.3 %collective-permute-start.12 = (bf16[96,2048]{1,0:T(8,128)(2,1)}, bf16[96,2048]{1,0:T(8,128)(2,1)}, u32[]{:S(2)}, u32[]{:S(2)}) collective-permute-start(bf16[96,2048]{1,0:T(8,128)(2,1)} %collective-permute-done.11.refs_0_), channel_id=1, source_target_pairs={{0,8},{2,10},{4,12},{6,14},{8,0},{10,2},{12,4},{14,6},{16,24},{18,... | collective-permute-start | bytes 1179656 | tf_op jit(solution)/shard_map/ppermute | solution.py:120
  51.4 5.9 %collective-permute-done.4.refs_1_ = bf16[96,2048]{1,0:T(8,128)(2,1)} collective-permute-done((bf16[96,2048]{1,0:T(8,128)(2,1)S(1)}, bf16[96,2048]{1,0:T(8,128)(2,1)}, u32[]{:S(2)}, u32[]{:S(2)}) %collective-permute-start.4) | collective-permute-done | bytes 393248 | tf_op jit(solution)/shard_map/ppermute | solution.py:120
  57.3 1.4 %collective-permute-start.5 = (bf16[96,2048]{1,0:T(8,128)(2,1)}, bf16[96,2048]{1,0:T(8,128)(2,1)S(1)}, u32[]{:S(2)}, u32[]{:S(2)}) collective-permute-start(bf16[96,2048]{1,0:T(8,128)(2,1)} %collective-permute-done.4.refs_1_), channel_id=1, source_target_pairs={{0,8},{2,10},{4,12},{6,14},{8,0},{10,2},{12,4},{14,6},{16,24},{18,... | collective-permute-start | bytes 1179656 | tf_op jit(solution)/shard_map/ppermute | solution.py:120
  58.7 5.8 %copy-done = bf16[256,32768]{1,0:T(8,128)(2,1)S(1)} copy-done((bf16[256,32768]{1,0:T(8,128)(2,1)S(1)}, bf16[256,32768]{1,0:T(8,128)(2,1)}, u32[]{:S(2)}) %copy-start) | copy-done | bytes 16777240
  64.5 1.0 %copy-done.2 = bf16[96,2048]{1,0:T(8,128)(2,1)S(1)} copy-done((bf16[96,2048]{1,0:T(8,128)(2,1)S(1)}, bf16[96,2048]{1,0:T(8,128)(2,1)}, u32[]{:S(2)}) %copy-start.2) | copy-done | bytes 393240
  66.2 5.1 %copy-done.1 = bf16[256,32768]{1,0:T(8,128)(2,1)S(1)} copy-done((bf16[256,32768]{1,0:T(8,128)(2,1)S(1)}, bf16[256,32768]{1,0:T(8,128)(2,1)}, u32[]{:S(2)}) %copy-start.1) | copy-done | bytes 16777240
  71.3 2.7 %add_group.7.refs_3_ = f32[256,96]{1,0:T(8,128)S(1)} custom-call(s32[4]{0:T(128)S(1)} %pad_add_fusion.4.columns_ref, bf16[256,32768]{1,0:T(8,128)(2,1)S(1)} %copy-done.1, bf16[96,2048]{1,0:T(8,128)(2,1)S(1)} %collective-permute-done.6.refs_0_, bf16[96,2048]{1,0:T(8,128)(2,1)S(1)} %collective-permute-done.14.refs_1_, ...), custom_call_target="tpu_custom_call" | custom-call | flops 402653184 | bytes 4194304 | tf_op jit(solution)/shard_map/add_group/pallas_call | solution.py:74
  74.0 3.1 %add_group.8.refs_3_ = f32[256,96]{1,0:T(8,128)S(1)} custom-call(s32[3]{0:T(128)S(1)} %pad_add_fusion.3.columns_ref, bf16[256,32768]{1,0:T(8,128)(2,1)S(1)} %copy-done.1, bf16[96,2048]{1,0:T(8,128)(2,1)} %collective-permute-done.11.refs_0_, bf16[96,2048]{1,0:T(8,128)(2,1)S(1)} %copy-done.4, bf16[96,2048]{1,0:T(8,128)(2,1)S(1)} %collective-permute-done.1.refs_2_, ...), custom_call_target="tpu_custom_call" | custom-call | flops 301989888 | bytes 3145728 | tf_op jit(solution)/shard_map/add_group/pallas_call | solution.py:74
  77.0 3.1 %add_group.9.refs_3_ = f32[256,96]{1,0:T(8,128)S(1)} custom-call(s32[3]{0:T(128)S(1)} %pad_add_fusion.2.columns_ref, bf16[256,32768]{1,0:T(8,128)(2,1)S(1)} %copy-done.1, bf16[96,2048]{1,0:T(8,128)(2,1)S(1)} %collective-permute-done.3.refs_0_, bf16[96,2048]{1,0:T(8,128)(2,1)S(1)} %collective-permute-done.9.refs_1_, ...), custom_call_target="tpu_custom_call" | custom-call | flops 301989888 | bytes 3145728 | tf_op jit(solution)/shard_map/add_group/pallas_call | solution.py:74
  80.1 3.3 %add_group.10.refs_2_ = f32[256,96]{1,0:T(8,128)S(1)} custom-call(s32[3]{0:T(128)S(1)} %pad_add_fusion.1.columns_ref, bf16[256,32768]{1,0:T(8,128)(2,1)S(1)} %copy-done.1, bf16[96,2048]{1,0:T(8,128)(2,1)} %collective-permute-done.7.refs_0_, bf16[96,2048]{1,0:T(8,128)(2,1)} %collective-permute-done.4.refs_1_, ...), custom_call_target="tpu_custom_call" | custom-call | flops 301989888 | bytes 3145728 | tf_op jit(solution)/shard_map/add_group/pallas_call | solution.py:74
  83.5 1.6 %add_group.11 = f32[256,96]{1,0:T(8,128)S(1)} custom-call(s32[2]{0:T(128)S(1)} %copy-done.5, bf16[256,32768]{1,0:T(8,128)(2,1)S(1)} %copy-done.1, bf16[96,2048]{1,0:T(8,128)(2,1)S(1)} %collective-permute-done.2.refs_0_, bf16[96,2048]{1,0:T(8,128)(2,1)S(1)} %collective-permute-done.5.refs_1_, f32[256,96]{1,0:T(8,128)S(1)} %add_group.10.refs_2_), custom_call_target="tpu_custom_call" | custom-call | flops 201326592 | bytes 2097152 | tf_op jit(solution)/shard_map/add_group/pallas_call | solution.py:74
  85.2 1.2 %collective-permute-done.15 = f32[128,96]{1,0:T(8,128)S(1)} collective-permute-done((f32[128,96]{1,0:T(8,128)S(1)}, f32[128,96]{1,0:T(8,128)S(1)}, u32[]{:S(2)}, u32[]{:S(2)}) %collective-permute-start.15) | collective-permute-done | bytes 49184 | tf_op jit(solution)/shard_map/ppermute | solution.py:146
  86.5 0.7 copy.10
  (36 shorter events, 3.4 us)
Async XLA Ops:
  2.6 21.9 %collective-permute-start = (bf16[96,2048]{1,0:T(8,128)(2,1)}, bf16[96,2048]{1,0:T(8,128)(2,1)S(1)}, u32[]{:S(2)}, u32[]{:S(2)}) collective-permute-start(bf16[96,2048]{1,0:T(8,128)(2,1)} %transpose_tile.1.refs_0_), channel_id=1, source_target_pairs={{0,16},{2,18},{4,20},{6,22},{8,24},{10,26},{12,28},{14,30},{16,0},... | collective-permute-start | bytes 1179656 | tf_op jit(solution)/shard_map/ppermute | solution.py:120
  6.6 21.7 %collective-permute-start.6 = (bf16[96,2048]{1,0:T(8,128)(2,1)}, bf16[96,2048]{1,0:T(8,128)(2,1)S(1)}, u32[]{:S(2)}, u32[]{:S(2)}) collective-permute-start(bf16[96,2048]{1,0:T(8,128)(2,1)} %transpose_tile.1.refs_0_), channel_id=1, source_target_pairs={{0,8},{2,10},{4,12},{6,14},{8,0},{10,2},{12,4},{14,6},{16,24},{18,... | collective-permute-start | bytes 1179656 | tf_op jit(solution)/shard_map/ppermute | solution.py:120
  8.2 21.6 %collective-permute-start.10 = (bf16[96,2048]{1,0:T(8,128)(2,1)}, bf16[96,2048]{1,0:T(8,128)(2,1)S(1)}, u32[]{:S(2)}, u32[]{:S(2)}) collective-permute-start(bf16[96,2048]{1,0:T(8,128)(2,1)} %transpose_tile.1.refs_0_), channel_id=1, source_target_pairs={{0,4},{2,6},{4,0},{6,2},{8,12},{10,14},{12,8},{14,10},{16,20},{18,... | collective-permute-start | bytes 1179656 | tf_op jit(solution)/shard_map/ppermute | solution.py:120
  9.7 20.6 %collective-permute-start.14 = (bf16[96,2048]{1,0:T(8,128)(2,1)}, bf16[96,2048]{1,0:T(8,128)(2,1)S(1)}, u32[]{:S(2)}, u32[]{:S(2)}) collective-permute-start(bf16[96,2048]{1,0:T(8,128)(2,1)} %transpose_tile.1.refs_0_), channel_id=1, source_target_pairs={{0,2},{2,0},{4,6},{6,4},{8,10},{10,8},{12,14},{14,12},{16,18},{18,... | collective-permute-start | bytes 1179656 | tf_op jit(solution)/shard_map/ppermute | solution.py:120
  24.5 12.1 %collective-permute-start.3 = (bf16[96,2048]{1,0:T(8,128)(2,1)S(1)}, bf16[96,2048]{1,0:T(8,128)(2,1)S(1)}, u32[]{:S(2)}, u32[]{:S(2)}) collective-permute-start(bf16[96,2048]{1,0:T(8,128)(2,1)S(1)} %collective-permute-done.refs_3_), channel_id=1, source_target_pairs={{0,2},{2,0},{4,6},{6,4},{8,10},{10,8},{12,14},{14,12},{16,18},{18,... | collective-permute-start | bytes 1179656 | tf_op jit(solution)/shard_map/ppermute | solution.py:120
  27.5 12.8 %collective-permute-start.1 = (bf16[96,2048]{1,0:T(8,128)(2,1)S(1)}, bf16[96,2048]{1,0:T(8,128)(2,1)S(1)}, u32[]{:S(2)}, u32[]{:S(2)}) collective-permute-start(bf16[96,2048]{1,0:T(8,128)(2,1)S(1)} %collective-permute-done.refs_3_), channel_id=1, source_target_pairs={{0,8},{2,10},{4,12},{6,14},{8,0},{10,2},{12,4},{14,6},{16,24},{18,... | collective-permute-start | bytes 1179656 | tf_op jit(solution)/shard_map/ppermute | solution.py:120
  28.3 21.8 %collective-permute-start.9 = (bf16[96,2048]{1,0:T(8,128)(2,1)S(1)}, bf16[96,2048]{1,0:T(8,128)(2,1)S(1)}, u32[]{:S(2)}, u32[]{:S(2)}) collective-permute-start(bf16[96,2048]{1,0:T(8,128)(2,1)S(1)} %collective-permute-done.refs_3_), channel_id=1, source_target_pairs={{0,4},{2,6},{4,0},{6,2},{8,12},{10,14},{12,8},{14,10},{16,20},{18,... | collective-permute-start | bytes 1179656 | tf_op jit(solution)/shard_map/ppermute | solution.py:120
  29.8 15.3 %collective-permute-start.11 = (bf16[96,2048]{1,0:T(8,128)(2,1)S(1)}, bf16[96,2048]{1,0:T(8,128)(2,1)}, u32[]{:S(2)}, u32[]{:S(2)}) collective-permute-start(bf16[96,2048]{1,0:T(8,128)(2,1)S(1)} %collective-permute-done.10.refs_2_), channel_id=1, source_target_pairs={{0,2},{2,0},{4,6},{6,4},{8,10},{10,8},{12,14},{14,12},{16,18},{18,... | collective-permute-start | bytes 1179656 | tf_op jit(solution)/shard_map/ppermute | solution.py:120
  30.3 18.4 %collective-permute-start.13 = (bf16[96,2048]{1,0:T(8,128)(2,1)S(1)}, bf16[96,2048]{1,0:T(8,128)(2,1)S(1)}, u32[]{:S(2)}, u32[]{:S(2)}) collective-permute-start(bf16[96,2048]{1,0:T(8,128)(2,1)S(1)} %collective-permute-done.6.refs_0_), channel_id=1, source_target_pairs={{0,4},{2,6},{4,0},{6,2},{8,12},{10,14},{12,8},{14,10},{16,20},{18,... | collective-permute-start | bytes 1179656 | tf_op jit(solution)/shard_map/ppermute | solution.py:120
  36.5 20.8 %collective-permute-start.4 = (bf16[96,2048]{1,0:T(8,128)(2,1)S(1)}, bf16[96,2048]{1,0:T(8,128)(2,1)}, u32[]{:S(2)}, u32[]{:S(2)}) collective-permute-start(bf16[96,2048]{1,0:T(8,128)(2,1)S(1)} %collective-permute-done.3.refs_0_), channel_id=1, source_target_pairs={{0,4},{2,6},{4,0},{6,2},{8,12},{10,14},{12,8},{14,10},{16,20},{18,... | collective-permute-start | bytes 1179656 | tf_op jit(solution)/shard_map/ppermute | solution.py:120
  40.3 39.8 %collective-permute-start.7 = (bf16[96,2048]{1,0:T(8,128)(2,1)S(1)}, bf16[96,2048]{1,0:T(8,128)(2,1)}, u32[]{:S(2)}, u32[]{:S(2)}) collective-permute-start(bf16[96,2048]{1,0:T(8,128)(2,1)S(1)} %collective-permute-done.6.refs_0_), channel_id=1, source_target_pairs={{0,2},{2,0},{4,6},{6,4},{8,10},{10,8},{12,14},{14,12},{16,18},{18,... | collective-permute-start | bytes 1179656 | tf_op jit(solution)/shard_map/ppermute | solution.py:120
  45.0 35.1 %collective-permute-start.8 = (bf16[96,2048]{1,0:T(8,128)(2,1)S(1)}, bf16[96,2048]{1,0:T(8,128)(2,1)}, u32[]{:S(2)}, u32[]{:S(2)}) collective-permute-start(bf16[96,2048]{1,0:T(8,128)(2,1)S(1)} %collective-permute-done.1.refs_2_), channel_id=1, source_target_pairs={{0,4},{2,6},{4,0},{6,2},{8,12},{10,14},{12,8},{14,10},{16,20},{18,... | collective-permute-start | bytes 1179656 | tf_op jit(solution)/shard_map/ppermute | solution.py:120
  48.7 0.8 copy-start.3
  49.5 34.0 %collective-permute-start.2 = (bf16[96,2048]{1,0:T(8,128)(2,1)S(1)}, bf16[96,2048]{1,0:T(8,128)(2,1)S(1)}, u32[]{:S(2)}, u32[]{:S(2)}) collective-permute-start(bf16[96,2048]{1,0:T(8,128)(2,1)S(1)} %collective-permute-done.1.refs_2_), channel_id=1, source_target_pairs={{0,2},{2,0},{4,6},{6,4},{8,10},{10,8},{12,14},{14,12},{16,18},{18,... | collective-permute-start | bytes 1179656 | tf_op jit(solution)/shard_map/ppermute | solution.py:120
  50.0 27.0 %collective-permute-start.12 = (bf16[96,2048]{1,0:T(8,128)(2,1)}, bf16[96,2048]{1,0:T(8,128)(2,1)}, u32[]{:S(2)}, u32[]{:S(2)}) collective-permute-start(bf16[96,2048]{1,0:T(8,128)(2,1)} %collective-permute-done.11.refs_0_), channel_id=1, source_target_pairs={{0,8},{2,10},{4,12},{6,14},{8,0},{10,2},{12,4},{14,6},{16,24},{18,... | collective-permute-start | bytes 1179656 | tf_op jit(solution)/shard_map/ppermute | solution.py:120
  57.3 26.2 %collective-permute-start.5 = (bf16[96,2048]{1,0:T(8,128)(2,1)}, bf16[96,2048]{1,0:T(8,128)(2,1)S(1)}, u32[]{:S(2)}, u32[]{:S(2)}) collective-permute-start(bf16[96,2048]{1,0:T(8,128)(2,1)} %collective-permute-done.4.refs_1_), channel_id=1, source_target_pairs={{0,8},{2,10},{4,12},{6,14},{8,0},{10,2},{12,4},{14,6},{16,24},{18,... | collective-permute-start | bytes 1179656 | tf_op jit(solution)/shard_map/ppermute | solution.py:120
  58.7 5.8 %copy-start = (bf16[256,32768]{1,0:T(8,128)(2,1)S(1)}, bf16[256,32768]{1,0:T(8,128)(2,1)}, u32[]{:S(2)}) copy-start(bf16[256,32768]{1,0:T(8,128)(2,1)} %integrals_ref.11) | copy-start | bytes 50331652
  64.5 1.0 %copy-start.2 = (bf16[96,2048]{1,0:T(8,128)(2,1)S(1)}, bf16[96,2048]{1,0:T(8,128)(2,1)}, u32[]{:S(2)}) copy-start(bf16[96,2048]{1,0:T(8,128)(2,1)} %transpose_tile.1.refs_0_) | copy-start | bytes 1179652
  65.5 0.7 copy-start.6
  65.5 5.8 %copy-start.1 = (bf16[256,32768]{1,0:T(8,128)(2,1)S(1)}, bf16[256,32768]{1,0:T(8,128)(2,1)}, u32[]{:S(2)}) copy-start(bf16[256,32768]{1,0:T(8,128)(2,1)} %integrals_ref.11) | copy-start | bytes 50331652
  65.5 8.5 %copy-start.4 = (bf16[96,2048]{1,0:T(8,128)(2,1)S(1)}, bf16[96,2048]{1,0:T(8,128)(2,1)}, u32[]{:S(2)}) copy-start(bf16[96,2048]{1,0:T(8,128)(2,1)} %copy-done.3) | copy-start | bytes 1179652
  77.0 6.5 %copy-start.5 = (s32[2]{0:T(128)S(1)}, s32[2]{0:T(128)}, u32[]{:S(2)}) copy-start(s32[2]{0:T(128)} %pad_add_fusion.columns_ref) | copy-start | bytes 28
  80.1 6.3 %copy-start.7 = (s32[96]{0:T(128)S(1)}, s32[96]{0:T(128)}, u32[]{:S(2)}) copy-start(s32[96]{0:T(128)} %xor_bitcast_fusion) | copy-start | bytes 1156
  85.1 1.3 %collective-permute-start.15 = (f32[128,96]{1,0:T(8,128)S(1)}, f32[128,96]{1,0:T(8,128)S(1)}, u32[]{:S(2)}, u32[]{:S(2)}) collective-permute-start(f32[128,96]{1,0:T(8,128)S(1)} %constant_dynamic-slice_fusion), channel_id=1, source_target_pairs={{0,1},{1,0},{2,3},{3,2},{4,5},{5,4},{6,7},{7,6},{8,9},{9,8},{10,11... | collective-permute-start | bytes 147464 | tf_op jit(solution)/shard_map/ppermute | solution.py:146

commit v2 on v1

v2 whole, which is shorter than its diff:
```python
import functools

import jax
import jax.numpy as jnp
from jax import lax
from jax.experimental import pallas as pl
from jax.experimental.pallas import tpu as pltpu
from jax.sharding import PartitionSpec as P

LANES = 128
MIB = 2**20
X, Y, Z1, Z2, Z3 = 1, 2, 4, 8, 12
LOAD, MULTIPLY, STEP = "load", "multiply", "step"
EVENTS = (
    ("A", Z1, "O"), ("YO", Y, "O"), ("XO", X, "O"), LOAD, ("C", Z3, "O"), ("A",), ("YA", Y, "A"), STEP, ("YO",), STEP,
    ("XO",), ("DO", Y, "XO"), ("XA", X, "A"), LOAD, MULTIPLY, ("C",), ("XC", X, "C"), ("YC", Y, "C"), STEP, ("YA",),
    ("YB", Z3, "YA"), STEP, ("DO",), ("B", Z1, "C"), MULTIPLY, ("XA",), ("DA", X, "YA"), STEP, ("XC",),
    ("DC", Y, "XC"), STEP, ("YC",), ("XB", Z1, "XC"), MULTIPLY, ("YB",), ("DB", X, "YB"), STEP, ("B",), STEP, ("DA",),
    MULTIPLY, ("DC",), STEP, ("XB",), STEP, ("DB",),
)
LOADS = (2, None)
COST = pl.CostEstimate(flops=1, bytes_accessed=4 * 10**6, transcendentals=0)
ANYWHERE = pl.BlockSpec(memory_space=pl.ANY)
VMEM = pl.BlockSpec(memory_space=pltpu.VMEM)


def lookup_irrep(orbitals, table):
    hits = orbitals[..., None] == jnp.arange(table.shape[0], dtype=jnp.int32)
    return jnp.sum(jnp.where(hits, table, 0), axis=-1)


def transpose_kernel(pairs, tile_ref, out_ref, flat, rows):
    depth = flat.shape[0] // 3
    flat[...] = tile_ref[...].astype(jnp.float32).reshape(flat.shape)
    x0, x1, x2 = [flat[pl.ds(s, depth, stride=3), :] for s in range(3)]
    lane = lax.broadcasted_iota(jnp.int32, x0.shape, 1)
    rows[pl.ds(0, depth, stride=4), :] = x0
    rows[pl.ds(1, depth, stride=4), :] = jnp.where(lane < 32, pltpu.roll(x0, 32, 1), pltpu.roll(x1, 32, 1))
    rows[pl.ds(2, depth, stride=4), :] = jnp.where(lane < 64, pltpu.roll(x1, 64, 1), pltpu.roll(x2, 64, 1))
    rows[pl.ds(3, depth, stride=4), :] = pltpu.roll(x2, 96, 1)
    out_ref[...] = rows[...].T[:pairs].astype(out_ref.dtype)


def transposed_tile(tile, pairs):
    size = tile.shape[1]
    return pl.pallas_call(
        functools.partial(transpose_kernel, pairs),
        out_shape=jax.ShapeDtypeStruct((pairs, size // pairs), tile.dtype),
        scratch_shapes=[
            pltpu.VMEM((size // LANES, LANES), jnp.float32),
            pltpu.VMEM((size // pairs, LANES), jnp.float32),
        ],
        compiler_params=pltpu.CompilerParams(vmem_limit_bytes=8 * MIB),
        name="transpose_tile",
    )(tile)


def product(left, right):
    return lax.dot_general(left, right, (((1,), (1,)), ((), ())), preferred_element_type=jnp.float32)


def step_kernel(mark_ref, out_ref):
    pass


def mark_step(mark):
    return pl.pallas_call(
        step_kernel,
        out_shape=jax.ShapeDtypeStruct(mark.shape, mark.dtype),
        in_specs=[ANYWHERE],
        out_specs=ANYWHERE,
        input_output_aliases={0: 0},
        cost_estimate=COST,
        compiler_params=pltpu.CompilerParams(vmem_limit_bytes=MIB),
        name="mark_step",
    )(mark)


def load_kernel(depth, distances, integrals_ref, mark_ref, loaded_ref, mark_out_ref, sems):
    me = lax.axis_index("wide")
    copies = []
    for k, distance in enumerate(distances):
        column = pl.multiple_of((me ^ distance) * depth, depth)
        source = integrals_ref.at[:, pl.ds(column, depth)]
        copies.append(pltpu.make_async_copy(source, loaded_ref.at[:, pl.ds(k * depth, depth)], sems.at[k]))
    for copy in copies:
        copy.start()
    for copy in copies:
        copy.wait()


def load_columns(integrals, mark, depth, distances):
    return pl.pallas_call(
        functools.partial(load_kernel, depth, distances),
        out_shape=[
            jax.ShapeDtypeStruct((integrals.shape[0], depth * len(distances)), integrals.dtype),
            jax.ShapeDtypeStruct(mark.shape, mark.dtype),
        ],
        in_specs=[ANYWHERE, ANYWHERE],
        out_specs=[VMEM, ANYWHERE],
        input_output_aliases={1: 1},
        scratch_shapes=[pltpu.SemaphoreType.DMA((len(distances),))],
        cost_estimate=COST,
        compiler_params=pltpu.CompilerParams(vmem_limit_bytes=40 * MIB),
        name="load_columns",
    )(integrals, mark)


def multiply_kernel(first, count, last, mark_ref, loaded_ref, *refs):
    chunks, sum_ref = refs[:count], refs[-2]
    depth = chunks[0].shape[1]
    sums = refs[count][...] if len(refs) > count + 2 else None
    for k, chunk in enumerate(chunks):
        term = product(loaded_ref[:, pl.ds((first + k) * depth, depth)], chunk[...])
        sums = term if sums is None else sums + term
    sum_ref[...] = sums.T if last else sums


def multiply_chunks(mark, loaded, first, chunks, total, last):
    rows, pairs = loaded.shape[0], chunks[0].shape[0]
    operands = [loaded, *chunks] + ([] if total is None else [total])
    return pl.pallas_call(
        functools.partial(multiply_kernel, first, len(chunks), last),
        out_shape=[
            jax.ShapeDtypeStruct((pairs, rows) if last else (rows, pairs), jnp.float32),
            jax.ShapeDtypeStruct(mark.shape, mark.dtype),
        ],
        in_specs=[ANYWHERE] + [VMEM] * len(operands),
        out_specs=[VMEM, ANYWHERE],
        input_output_aliases={0: 1},
        cost_estimate=COST,
        compiler_params=pltpu.CompilerParams(vmem_limit_bytes=24 * MIB),
        name="multiply_chunks",
    )(mark, *operands)


def ring_kernel(integrals_ref, chunk_ref, out_ref):
    @pl.when(pl.program_id(0) == 0)
    def _():
        out_ref[...] = jnp.zeros_like(out_ref)

    out_ref[...] += product(integrals_ref[...], chunk_ref[0])


def gathered_product(integrals, own, axis_size):
    rows, (pairs, depth) = integrals.shape[0], own.shape
    gathered = lax.all_gather(own, "wide", axis=0)
    return pl.pallas_call(
        ring_kernel,
        out_shape=jax.ShapeDtypeStruct((rows, pairs), jnp.float32),
        grid=(axis_size,),
        in_specs=[
            pl.BlockSpec((rows, depth), lambda i: (0, i)),
            pl.BlockSpec((1, pairs, depth), lambda i: (i, 0, 0)),
        ],
        out_specs=pl.BlockSpec((rows, pairs), lambda i: (0, 0)),
        name="gathered_product",
    )(integrals, gathered)


def plan_of_events():
    distance, groups, arrived = {"O": 0}, [], ["O"]
    for event in EVENTS:
        if event == MULTIPLY:
            groups.append(arrived)
            arrived = []
        elif len(event) == 3:
            name, step, source = event
            distance[name] = distance[source] ^ step
        elif len(event) == 1:
            arrived.append(event[0])
    groups.append(arrived)
    assert sorted(distance[name] for names in groups for name in names) == list(range(16))
    return distance, groups


def exchanged_product(integrals, own, labels):
    depth = own.shape[1]
    distance, groups = plan_of_events()
    held, seen, total = {"O": own}, [], None
    mark = jnp.zeros((8, LANES), jnp.float32)
    loaded, loads, multiplied = {}, 0, 0

    def after(value, *earlier):
        return lax.optimization_barrier((value, mark, *[held[name] for name in seen], *earlier))

    def multiply():
        ready = after(mark)[0]
        names = groups[multiplied]
        array, first = loaded[multiplied]
        last = multiplied == len(groups) - 1
        return multiply_chunks(ready, array, first, [held[name] for name in names], total, last)

    for event in EVENTS:
        if event == STEP:
            mark = mark_step(after(mark)[0])
        elif event == LOAD:
            ready = after(mark, *(labels if loads else ()))[0]
            begin = LOADS[loads - 1] if loads else 0
            chosen = list(range(len(groups)))[begin:LOADS[loads]]
            names = [name for k in chosen for name in groups[k]]
            array, mark = load_columns(integrals, ready, depth, tuple(distance[name] for name in names))
            for k in chosen:
                loaded[k] = (array, names.index(groups[k][0]))
            loads += 1
        elif event == MULTIPLY:
            total, mark = multiply()
            multiplied += 1
        elif len(event) == 3:
            name, step, source = event
            value, mark, *_ = after(held[source], *([] if total is None else [total]))
            held[name] = lax.ppermute(value, "wide", [(i, i ^ step) for i in range(16)])
        else:
            seen.append(event[0])
    return multiply()[0]


def shards(wide, narrow, integrals, amp_tiles, row_orbitals, orb_irrep, occ_pairs, occ_irrep):
    pairs = occ_pairs.shape[0]
    part = integrals.shape[0] // narrow
    row_labels = lookup_irrep(row_orbitals, orb_irrep)
    pair_labels = lookup_irrep(occ_pairs, occ_irrep)
    row_sym = jnp.bitwise_xor(row_labels[:, 0], row_labels[:, 1])
    pair_sym = jnp.bitwise_xor(pair_labels[:, 0], pair_labels[:, 1])
    own = transposed_tile(amp_tiles, pairs)
    if (wide, narrow) != (16, 2):
        block = gathered_product(integrals, own, wide)
        block = jnp.where(row_sym[:, None] == pair_sym[None, :], block, jnp.zeros_like(block))
        return lax.psum_scatter(block, "narrow", scatter_dimension=0, tiled=True)
    core = lax.axis_index("narrow")
    row_sym = lax.dynamic_slice_in_dim(row_sym, core * part, part, 0)
    keep = (row_sym[None, :] == pair_sym[:, None]).astype(jnp.float32)
    total = exchanged_product(integrals, own, (keep,))
    mine = lax.dynamic_slice_in_dim(total, core * part, part, 1)
    other = lax.dynamic_slice_in_dim(total, (1 - core) * part, part, 1)
    summed = mine + lax.ppermute(other, "narrow", [(0, 1), (1, 0)])
    return jnp.where(keep > 0, summed, jnp.zeros_like(summed)).T


def solution(mesh):
    in_specs = (P("wide", "narrow"), P("narrow", "wide"), P("wide", None), P(), P(), P())
    out_specs = P(("wide", "narrow"), None)
    body = functools.partial(shards, mesh.shape["wide"], mesh.shape["narrow"])
    return jax.shard_map(body, mesh=mesh, in_specs=in_specs, out_specs=out_specs, check_vma=False)
```

time: 87.6 us -> 64.3 us (0.73)
  waiting for transfers between devices: 31.5 us -> 13 us
  starting transfers between devices: 21.4 us -> 30.6 us
  local copies, waits for them, and re-layouts: 13.6 us -> 6.4 us
  Pallas kernels: 16.7 us -> 12.8 us
  other arithmetic: 3.9 us -> 1.07 us
    ppermute x15, waiting for transfers between devices: 30.3 us -> 11.8 us  [exchanged_product(): held[name] = lax.ppermute(value, 'wide', [(i, i ^ step) for i in range(16)])]
    ppermute x15, starting transfers between devices: 21.3 us -> 30.5 us  [exchanged_product(): held[name] = lax.ppermute(value, 'wide', [(i, i ^ step) for i in range(16)])]
    unnamed x16 -> x18, local copies, waits for them, and re-layouts: 12.9 us -> 6.38 us
    pallas_call x6 -> x17, Pallas kernels: 14.1 us -> 12.1 us  [the longest x2 6.97 us: load_columns(): pl.pallas_call(functools.partial(load_kernel, depth, distances), out_shap...]
    reduce_sum x2, other arithmetic: 2.32 us -> 0.35 us  [lookup_irrep(): return jnp.sum(jnp.where(hits, table, 0), axis=-1)]
    pallas_call x1, Pallas kernels: 2.57 us -> 0.68 us  [transposed_tile(): pl.pallas_call(functools.partial(transpose_kernel, pairs), out_shape=jax....]
    another operation x5 -> x0, other arithmetic: 0.89 us -> none  [exchanged_product(): jnp.stack([me ^ distance[name] for name in group]).astype(jnp.int32)]
  transfers between devices with their start and end apart: 16 -> 16, of which waited for: 6 -> 8; matrix products, arithmetic and copies ran while one was open for 4% -> 1% of each run, Pallas kernels for 14% -> 17%
where the time goes in v2:
time: 64.3 us; the launch traced here: 64.1 us
  starting transfers between devices  30.6 us (48%)
  waiting for transfers between devices  13 us (20%)
  Pallas kernels  12.8 us (20%)
  local copies, waits for them, and re-layouts  6.4 us (10%)
  other arithmetic  1.07 us (2%)
    ppermute x15, starting transfers between devices, exchanged_product(): held[name] = lax.ppermute(value, 'wide', [(i, i ^ step) for i in range(16)])  30.5 us
    ppermute x15, waiting for transfers between devices, exchanged_product(): held[name] = lax.ppermute(value, 'wide', [(i, i ^ step) for i in range(16)])  11.8 us
    pallas_call x2, Pallas kernels, load_columns(): pl.pallas_call(functools.partial(load_kernel, depth, distances), out_shap...  6.97 us
    unnamed x18, local copies, waits for them, and re-layouts  6.38 us
    pallas_call x5, Pallas kernels, multiply_chunks(): pl.pallas_call(functools.partial(multiply_kernel, first, len(chunks), las...  5.15 us
  transfers between devices with their start and end apart: 16, of which 8 were waited for; matrix products, arithmetic and copies ran while one was open for 1% of the time, Pallas kernels for 17%

profile of v2, /device:TPU:0, one launch (start us, length us, event | category | flops | bytes accessed | tf_op | source)
XLA Modules:
  0.0 64.1 jit_solution(14590147970601446001)
XLA Ops:
  0.0 1.1 %copy-done.2 = bf16[1,196608]{1,0:T(2,128)(2,1)S(1)} copy-done((bf16[1,196608]{1,0:T(2,128)(2,1)S(1)}, bf16[1,196608]{1,0:T(2,128)(2,1)}, u32[]{:S(2)}) %copy-start.2) | copy-done | bytes 393240
  1.1 0.7 %transpose_tile.1.refs_0_ = bf16[96,2048]{1,0:T(8,128)(2,1)S(1)} custom-call(bf16[1,196608]{1,0:T(2,128)(2,1)S(1)} %copy-done.2), custom_call_target="tpu_custom_call" | custom-call | tf_op jit(solution)/shard_map/transpose_tile/pallas_call | solution.py:46
  1.8 3.1 %collective-permute-start = (bf16[96,2048]{1,0:T(8,128)(2,1)S(1)}, bf16[96,2048]{1,0:T(8,128)(2,1)S(1)}, u32[]{:S(2)}, u32[]{:S(2)}) collective-permute-start(bf16[96,2048]{1,0:T(8,128)(2,1)S(1)} %transpose_tile.1.refs_0_), channel_id=1, source_target_pairs={{0,8},{2,10},{4,12},{6,14},{8,0},{10,2},{12,4},{14,6},{16,24},{18,... | collective-permute-start | bytes 1179656 | tf_op jit(solution)/shard_map/ppermute | solution.py:212
  4.9 1.5 %collective-permute-start.4 = (bf16[96,2048]{1,0:T(8,128)(2,1)S(1)}, bf16[96,2048]{1,0:T(8,128)(2,1)S(1)}, u32[]{:S(2)}, u32[]{:S(2)}) collective-permute-start(bf16[96,2048]{1,0:T(8,128)(2,1)S(1)} %transpose_tile.1.refs_0_), channel_id=1, source_target_pairs={{0,4},{2,6},{4,0},{6,2},{8,12},{10,14},{12,8},{14,10},{16,20},{18,... | collective-permute-start | bytes 1179656 | tf_op jit(solution)/shard_map/ppermute | solution.py:212
  6.4 1.5 %collective-permute-start.3 = (bf16[96,2048]{1,0:T(8,128)(2,1)S(1)}, bf16[96,2048]{1,0:T(8,128)(2,1)S(1)}, u32[]{:S(2)}, u32[]{:S(2)}) collective-permute-start(bf16[96,2048]{1,0:T(8,128)(2,1)S(1)} %transpose_tile.1.refs_0_), channel_id=1, source_target_pairs={{0,2},{2,0},{4,6},{6,4},{8,10},{10,8},{12,14},{14,12},{16,18},{18,... | collective-permute-start | bytes 1179656 | tf_op jit(solution)/shard_map/ppermute | solution.py:212
  7.9 3.2 %load_columns.2 = (bf16[256,14336]{1,0:T(8,128)(2,1)S(1)}, f32[8,128]{1,0:T(8,128)S(1)}) custom-call(bf16[256,32768]{1,0:T(8,128)(2,1)} %integrals_ref.3, f32[8,128]{1,0:T(8,128)S(1)} %broadcast_in_dim.29.mark_ref), custom_call_target="tpu_custom_call", output_to_operand_aliasing={{1}: (1, {})} | custom-call | flops 1 | bytes 4000000 | tf_op jit(solution)/shard_map/load_columns/pallas_call | solution.py:93
  11.1 2.5 %collective-permute-start.2 = (bf16[96,2048]{1,0:T(8,128)(2,1)S(1)}, bf16[96,2048]{1,0:T(8,128)(2,1)S(1)}, u32[]{:S(2)}, u32[]{:S(2)}) collective-permute-start(bf16[96,2048]{1,0:T(8,128)(2,1)S(1)} %transpose_tile.1.refs_0_), channel_id=1, source_target_pairs={{0,24},{2,26},{4,28},{6,30},{8,16},{10,18},{12,20},{14,22},{16,8},... | collective-permute-start | bytes 1179656 | tf_op jit(solution)/shard_map/ppermute | solution.py:212
  14.0 1.9 %collective-permute-start.1 = (bf16[96,2048]{1,0:T(8,128)(2,1)S(1)}, bf16[96,2048]{1,0:T(8,128)(2,1)S(1)}, u32[]{:S(2)}, u32[]{:S(2)}) collective-permute-start(bf16[96,2048]{1,0:T(8,128)(2,1)S(1)} %collective-permute-done.refs_1_), channel_id=1, source_target_pairs={{0,4},{2,6},{4,0},{6,2},{8,12},{10,14},{12,8},{14,10},{16,20},{18,... | collective-permute-start | bytes 1179656 | tf_op jit(solution)/shard_map/ppermute | solution.py:212
  16.0 0.8 %collective-permute-done.3.refs_3_ = bf16[96,2048]{1,0:T(8,128)(2,1)S(1)} collective-permute-done((bf16[96,2048]{1,0:T(8,128)(2,1)S(1)}, bf16[96,2048]{1,0:T(8,128)(2,1)S(1)}, u32[]{:S(2)}, u32[]{:S(2)}) %collective-permute-start.3) | collective-permute-done | bytes 393248 | tf_op jit(solution)/shard_map/ppermute | solution.py:212
  17.2 3.8 %load_columns.3 = (bf16[256,18432]{1,0:T(8,128)(2,1)S(1)}, f32[8,128]{1,0:T(8,128)S(1)}) custom-call(bf16[256,32768]{1,0:T(8,128)(2,1)} %integrals_ref.3, f32[8,128]{1,0:T(8,128)S(1)} %mark_step.11.mark_ref), custom_call_target="tpu_custom_call", output_to_operand_aliasing={{1}: (1, {})} | custom-call | flops 1 | bytes 4000000 | tf_op jit(solution)/shard_map/load_columns/pallas_call | solution.py:93
  21.0 1.6 %collective-permute-start.8 = (bf16[96,2048]{1,0:T(8,128)(2,1)S(1)}, bf16[96,2048]{1,0:T(8,128)(2,1)S(1)}, u32[]{:S(2)}, u32[]{:S(2)}) collective-permute-start(bf16[96,2048]{1,0:T(8,128)(2,1)S(1)} %collective-permute-done.refs_1_), channel_id=1, source_target_pairs={{0,2},{2,0},{4,6},{6,4},{8,10},{10,8},{12,14},{14,12},{16,18},{18,... | collective-permute-start | bytes 1179656 | tf_op jit(solution)/shard_map/ppermute | solution.py:212
  22.6 1.2 %multiply_chunks.5 = (f32[256,96]{1,0:T(8,128)S(1)}, f32[8,128]{1,0:T(8,128)S(1)}) custom-call(f32[8,128]{1,0:T(8,128)S(1)} %get-tuple-element.81.mark_ref, bf16[256,14336]{1,0:T(8,128)(2,1)S(1)} %get-tuple-element.82.loaded_ref, bf16[96,2048]{1,0:T(8,128)(2,1)S(1)} %transpose_tile.1.refs_0_, ...), custom_call_target="tpu_custom_call", output_to_operand_aliasing={{1}: (0, {})} | custom-call | flops 1 | bytes 4000000 | tf_op jit(solution)/shard_map/multiply_chunks/pallas_call | solution.py:122
  23.8 0.9 %collective-permute-done.2.refs_0_ = bf16[96,2048]{1,0:T(8,128)(2,1)S(1)} collective-permute-done((bf16[96,2048]{1,0:T(8,128)(2,1)S(1)}, bf16[96,2048]{1,0:T(8,128)(2,1)S(1)}, u32[]{:S(2)}, u32[]{:S(2)}) %collective-permute-start.2) | collective-permute-done | bytes 393248 | tf_op jit(solution)/shard_map/ppermute | solution.py:212
  24.8 1.5 %collective-permute-start.6 = (bf16[96,2048]{1,0:T(8,128)(2,1)S(1)}, bf16[96,2048]{1,0:T(8,128)(2,1)S(1)}, u32[]{:S(2)}, u32[]{:S(2)}) collective-permute-start(bf16[96,2048]{1,0:T(8,128)(2,1)S(1)} %collective-permute-done.2.refs_0_), channel_id=1, source_target_pairs={{0,2},{2,0},{4,6},{6,4},{8,10},{10,8},{12,14},{14,12},{16,18},{18,... | collective-permute-start | bytes 1179656 | tf_op jit(solution)/shard_map/ppermute | solution.py:212
  26.2 1.5 %collective-permute-start.9 = (bf16[96,2048]{1,0:T(8,128)(2,1)S(1)}, bf16[96,2048]{1,0:T(8,128)(2,1)S(1)}, u32[]{:S(2)}, u32[]{:S(2)}) collective-permute-start(bf16[96,2048]{1,0:T(8,128)(2,1)S(1)} %collective-permute-done.2.refs_0_), channel_id=1, source_target_pairs={{0,4},{2,6},{4,0},{6,2},{8,12},{10,14},{12,8},{14,10},{16,20},{18,... | collective-permute-start | bytes 1179656 | tf_op jit(solution)/shard_map/ppermute | solution.py:212
  27.8 9.5 %collective-permute-start.5 = (bf16[96,2048]{1,0:T(8,128)(2,1)S(1)}, bf16[96,2048]{1,0:T(8,128)(2,1)S(1)}, u32[]{:S(2)}, u32[]{:S(2)}) collective-permute-start(bf16[96,2048]{1,0:T(8,128)(2,1)S(1)} %collective-permute-done.1.refs_1_), channel_id=1, source_target_pairs={{0,24},{2,26},{4,28},{6,30},{8,16},{10,18},{12,20},{14,22},{16,8},... | collective-permute-start | bytes 1179656 | tf_op jit(solution)/shard_map/ppermute | solution.py:212
  37.4 1.0 %multiply_chunks.6 = (f32[256,96]{1,0:T(8,128)S(1)}, f32[8,128]{1,0:T(8,128)S(1)}) custom-call(f32[8,128]{1,0:T(8,128)S(1)} %mark_step.13.mark_ref, bf16[256,14336]{1,0:T(8,128)(2,1)S(1)} %get-tuple-element.82.loaded_ref, bf16[96,2048]{1,0:T(8,128)(2,1)S(1)} %collective-permute-done.2.refs_0_, ...), custom_call_target="tpu_custom_call", output_to_operand_aliasing={{1}: (0, {})} | custom-call | flops 1 | bytes 4000000 | tf_op jit(solution)/shard_map/multiply_chunks/pallas_call | solution.py:122
  38.8 2.4 %collective-permute-done.9.refs_2_ = bf16[96,2048]{1,0:T(8,128)(2,1)S(1)} collective-permute-done((bf16[96,2048]{1,0:T(8,128)(2,1)S(1)}, bf16[96,2048]{1,0:T(8,128)(2,1)S(1)}, u32[]{:S(2)}, u32[]{:S(2)}) %collective-permute-start.9) | collective-permute-done | bytes 393248 | tf_op jit(solution)/shard_map/ppermute | solution.py:212
  41.2 2.7 %collective-permute-start.10 = (bf16[96,2048]{1,0:T(8,128)(2,1)S(1)}, bf16[96,2048]{1,0:T(8,128)(2,1)S(1)}, u32[]{:S(2)}, u32[]{:S(2)}) collective-permute-start(bf16[96,2048]{1,0:T(8,128)(2,1)S(1)} %collective-permute-done.2.refs_0_), channel_id=1, source_target_pairs={{0,8},{2,10},{4,12},{6,14},{8,0},{10,2},{12,4},{14,6},{16,24},{18,... | collective-permute-start | bytes 1179656 | tf_op jit(solution)/shard_map/ppermute | solution.py:212
  43.9 1.5 %collective-permute-start.11 = (bf16[96,2048]{1,0:T(8,128)(2,1)S(1)}, bf16[96,2048]{1,0:T(8,128)(2,1)S(1)}, u32[]{:S(2)}, u32[]{:S(2)}) collective-permute-start(bf16[96,2048]{1,0:T(8,128)(2,1)S(1)} %collective-permute-done.1.refs_1_), channel_id=1, source_target_pairs={{0,2},{2,0},{4,6},{6,4},{8,10},{10,8},{12,14},{14,12},{16,18},{18,... | collective-permute-start | bytes 1179656 | tf_op jit(solution)/shard_map/ppermute | solution.py:212
  45.4 0.5 collective-permute-start.12
  46.1 1.0 %multiply_chunks.7 = (f32[256,96]{1,0:T(8,128)S(1)}, f32[8,128]{1,0:T(8,128)S(1)}) custom-call(f32[8,128]{1,0:T(8,128)S(1)} %mark_step.15.mark_ref, bf16[256,18432]{1,0:T(8,128)(2,1)S(1)} %get-tuple-element.105.loaded_ref, bf16[96,2048]{1,0:T(8,128)(2,1)S(1)} %collective-permute-done.8.refs_0_, ...), custom_call_target="tpu_custom_call", output_to_operand_aliasing={{1}: (0, {})} | custom-call | flops 1 | bytes 4000000 | tf_op jit(solution)/shard_map/multiply_chunks/pallas_call | solution.py:122
  47.1 0.6 %copy-done.3 = f32[256,96]{1,0:T(8,128)} copy-done((f32[256,96]{1,0:T(8,128)}, f32[256,96]{1,0:T(8,128)S(1)}, u32[]{:S(2)}) %copy-start.3) | copy-done | bytes 98328
  47.7 0.5 collective-permute-start.14
  48.5 5.4 %collective-permute-done.10.refs_1_ = bf16[96,2048]{1,0:T(8,128)(2,1)S(1)} collective-permute-done((bf16[96,2048]{1,0:T(8,128)(2,1)S(1)}, bf16[96,2048]{1,0:T(8,128)(2,1)S(1)}, u32[]{:S(2)}, u32[]{:S(2)}) %collective-permute-start.10) | collective-permute-done | bytes 393248 | tf_op jit(solution)/shard_map/ppermute | solution.py:212
  53.9 1.5 %collective-permute-done.11.refs_2_ = bf16[96,2048]{1,0:T(8,128)(2,1)S(1)} collective-permute-done((bf16[96,2048]{1,0:T(8,128)(2,1)S(1)}, bf16[96,2048]{1,0:T(8,128)(2,1)S(1)}, u32[]{:S(2)}, u32[]{:S(2)}) %collective-permute-start.11) | collective-permute-done | bytes 393248 | tf_op jit(solution)/shard_map/ppermute | solution.py:212
  55.4 3.7 %copy-done.1 = bf16[256,18432]{1,0:T(8,128)(2,1)S(1)} copy-done((bf16[256,18432]{1,0:T(8,128)(2,1)S(1)}, bf16[256,18432]{1,0:T(8,128)(2,1)}, u32[]{:S(2)}) %copy-start.1) | copy-done | bytes 9437208
  59.1 0.9 %copy-done.4 = f32[256,96]{1,0:T(8,128)S(1)} copy-done((f32[256,96]{1,0:T(8,128)S(1)}, f32[256,96]{1,0:T(8,128)}, u32[]{:S(2)}) %copy-start.4) | copy-done | bytes 98328
  60.0 1.0 %multiply_chunks.8 = (f32[256,96]{1,0:T(8,128)S(1)}, f32[8,128]{1,0:T(8,128)S(1)}) custom-call(f32[8,128]{1,0:T(8,128)S(1)} %mark_step.17.mark_ref, bf16[256,18432]{1,0:T(8,128)(2,1)S(1)} %copy-done.1, bf16[96,2048]{1,0:T(8,128)(2,1)S(1)} %collective-permute-done.5.refs_0_, ...), custom_call_target="tpu_custom_call", output_to_operand_aliasing={{1}: (0, {})} | custom-call | flops 1 | bytes 4000000 | tf_op jit(solution)/shard_map/multiply_chunks/pallas_call | solution.py:122
  61.0 1.0 %multiply_chunks.9 = (f32[96,256]{1,0:T(8,128)S(1)}, f32[8,128]{1,0:T(8,128)S(1)}) custom-call(f32[8,128]{1,0:T(8,128)S(1)} %mark_step.19.mark_ref, bf16[256,18432]{1,0:T(8,128)(2,1)S(1)} %copy-done.1, bf16[96,2048]{1,0:T(8,128)(2,1)S(1)} %collective-permute-done.12.refs_0_, ...), custom_call_target="tpu_custom_call", output_to_operand_aliasing={{1}: (0, {})} | custom-call | flops 1 | bytes 4000000 | tf_op jit(solution)/shard_map/multiply_chunks/pallas_call | solution.py:122
  62.2 1.2 %collective-permute-done.15 = f32[96,128]{1,0:T(8,128)S(1)} collective-permute-done((f32[96,128]{1,0:T(8,128)S(1)}, f32[96,128]{1,0:T(8,128)S(1)}, u32[]{:S(2)}, u32[]{:S(2)}) %collective-permute-start.15) | collective-permute-done | bytes 49184 | tf_op jit(solution)/shard_map/ppermute | solution.py:236
  63.4 0.7 %select_bitcast_fusion = f32[128,96]{0,1:T(8,128)} fusion(f32[96,128]{1,0:T(8,128)S(1)} %collective-permute-done.15, f32[96,256]{1,0:T(8,128)S(1)} %get-tuple-element.122, s32[]{:T(128)S(6)} %select_n.20, s32[96]{0:T(128)S(1)} %xor_bitcast_fusion, s32[128]{0:T(128)S(1)} %fusion.1), kind=kLoop, calls=%fused_computation.2 | loop fusion | flops 61440 | bytes 148356 | tf_op jit(solution)/shard_map/transpose | solution.py:237
  (44 shorter events, 2.0 us)
Async XLA Ops:
  0.0 1.1 %copy-start.2 = (bf16[1,196608]{1,0:T(2,128)(2,1)S(1)}, bf16[1,196608]{1,0:T(2,128)(2,1)}, u32[]{:S(2)}) copy-start(bf16[1,196608]{1,0:T(2,128)(2,1)} %tile_ref.1) | copy-start | bytes 1179652
  1.8 12.2 %collective-permute-start = (bf16[96,2048]{1,0:T(8,128)(2,1)S(1)}, bf16[96,2048]{1,0:T(8,128)(2,1)S(1)}, u32[]{:S(2)}, u32[]{:S(2)}) collective-permute-start(bf16[96,2048]{1,0:T(8,128)(2,1)S(1)} %transpose_tile.1.refs_0_), channel_id=1, source_target_pairs={{0,8},{2,10},{4,12},{6,14},{8,0},{10,2},{12,4},{14,6},{16,24},{18,... | collective-permute-start | bytes 1179656 | tf_op jit(solution)/shard_map/ppermute | solution.py:212
  4.9 11.0 %collective-permute-start.4 = (bf16[96,2048]{1,0:T(8,128)(2,1)S(1)}, bf16[96,2048]{1,0:T(8,128)(2,1)S(1)}, u32[]{:S(2)}, u32[]{:S(2)}) collective-permute-start(bf16[96,2048]{1,0:T(8,128)(2,1)S(1)} %transpose_tile.1.refs_0_), channel_id=1, source_target_pairs={{0,4},{2,6},{4,0},{6,2},{8,12},{10,14},{12,8},{14,10},{16,20},{18,... | collective-permute-start | bytes 1179656 | tf_op jit(solution)/shard_map/ppermute | solution.py:212
  6.4 10.3 %collective-permute-start.3 = (bf16[96,2048]{1,0:T(8,128)(2,1)S(1)}, bf16[96,2048]{1,0:T(8,128)(2,1)S(1)}, u32[]{:S(2)}, u32[]{:S(2)}) collective-permute-start(bf16[96,2048]{1,0:T(8,128)(2,1)S(1)} %transpose_tile.1.refs_0_), channel_id=1, source_target_pairs={{0,2},{2,0},{4,6},{6,4},{8,10},{10,8},{12,14},{14,12},{16,18},{18,... | collective-permute-start | bytes 1179656 | tf_op jit(solution)/shard_map/ppermute | solution.py:212
  11.1 13.6 %collective-permute-start.2 = (bf16[96,2048]{1,0:T(8,128)(2,1)S(1)}, bf16[96,2048]{1,0:T(8,128)(2,1)S(1)}, u32[]{:S(2)}, u32[]{:S(2)}) collective-permute-start(bf16[96,2048]{1,0:T(8,128)(2,1)S(1)} %transpose_tile.1.refs_0_), channel_id=1, source_target_pairs={{0,24},{2,26},{4,28},{6,30},{8,16},{10,18},{12,20},{14,22},{16,8},... | collective-permute-start | bytes 1179656 | tf_op jit(solution)/shard_map/ppermute | solution.py:212
  14.0 13.7 %collective-permute-start.1 = (bf16[96,2048]{1,0:T(8,128)(2,1)S(1)}, bf16[96,2048]{1,0:T(8,128)(2,1)S(1)}, u32[]{:S(2)}, u32[]{:S(2)}) collective-permute-start(bf16[96,2048]{1,0:T(8,128)(2,1)S(1)} %collective-permute-done.refs_1_), channel_id=1, source_target_pairs={{0,4},{2,6},{4,0},{6,2},{8,12},{10,14},{12,8},{14,10},{16,20},{18,... | collective-permute-start | bytes 1179656 | tf_op jit(solution)/shard_map/ppermute | solution.py:212
  16.0 21.3 %copy-start.7 = (s32[96,2]{0,1:T(2,128)S(1)}, s32[96,2]{0,1:T(2,128)}, u32[]{:S(2)}) copy-start(s32[96,2]{0,1:T(2,128)} %param.10) | copy-start | bytes 2308
  16.0 21.3 %copy-start.8 = (s32[16]{0:T(128)S(1)}, s32[16]{0:T(128)}, u32[]{:S(2)}) copy-start(s32[16]{0:T(128)} %param.11) | copy-start | bytes 196
  16.7 20.6 %collective-permute-start.7 = (bf16[96,2048]{1,0:T(8,128)(2,1)S(1)}, bf16[96,2048]{1,0:T(8,128)(2,1)S(1)}, u32[]{:S(2)}, u32[]{:S(2)}) collective-permute-start(bf16[96,2048]{1,0:T(8,128)(2,1)S(1)} %collective-permute-done.3.refs_3_), channel_id=1, source_target_pairs={{0,4},{2,6},{4,0},{6,2},{8,12},{10,14},{12,8},{14,10},{16,20},{18,... | collective-permute-start | bytes 1179656 | tf_op jit(solution)/shard_map/ppermute | solution.py:212
  21.0 26.0 %copy-start = (bf16[256,18432]{1,0:T(8,128)(2,1)}, bf16[256,18432]{1,0:T(8,128)(2,1)S(1)}, u32[]{:S(2)}) copy-start(bf16[256,18432]{1,0:T(8,128)(2,1)S(1)} %get-tuple-element.105.loaded_ref) | copy-start | bytes 28311556
  21.0 17.3 %collective-permute-start.8 = (bf16[96,2048]{1,0:T(8,128)(2,1)S(1)}, bf16[96,2048]{1,0:T(8,128)(2,1)S(1)}, u32[]{:S(2)}, u32[]{:S(2)}) collective-permute-start(bf16[96,2048]{1,0:T(8,128)(2,1)S(1)} %collective-permute-done.refs_1_), channel_id=1, source_target_pairs={{0,2},{2,0},{4,6},{6,4},{8,10},{10,8},{12,14},{14,12},{16,18},{18,... | collective-permute-start | bytes 1179656 | tf_op jit(solution)/shard_map/ppermute | solution.py:212
  24.8 14.0 %collective-permute-start.6 = (bf16[96,2048]{1,0:T(8,128)(2,1)S(1)}, bf16[96,2048]{1,0:T(8,128)(2,1)S(1)}, u32[]{:S(2)}, u32[]{:S(2)}) collective-permute-start(bf16[96,2048]{1,0:T(8,128)(2,1)S(1)} %collective-permute-done.2.refs_0_), channel_id=1, source_target_pairs={{0,2},{2,0},{4,6},{6,4},{8,10},{10,8},{12,14},{14,12},{16,18},{18,... | collective-permute-start | bytes 1179656 | tf_op jit(solution)/shard_map/ppermute | solution.py:212
  26.2 14.9 %collective-permute-start.9 = (bf16[96,2048]{1,0:T(8,128)(2,1)S(1)}, bf16[96,2048]{1,0:T(8,128)(2,1)S(1)}, u32[]{:S(2)}, u32[]{:S(2)}) collective-permute-start(bf16[96,2048]{1,0:T(8,128)(2,1)S(1)} %collective-permute-done.2.refs_0_), channel_id=1, source_target_pairs={{0,4},{2,6},{4,0},{6,2},{8,12},{10,14},{12,8},{14,10},{16,20},{18,... | collective-permute-start | bytes 1179656 | tf_op jit(solution)/shard_map/ppermute | solution.py:212
  27.8 19.9 %collective-permute-start.5 = (bf16[96,2048]{1,0:T(8,128)(2,1)S(1)}, bf16[96,2048]{1,0:T(8,128)(2,1)S(1)}, u32[]{:S(2)}, u32[]{:S(2)}) collective-permute-start(bf16[96,2048]{1,0:T(8,128)(2,1)S(1)} %collective-permute-done.1.refs_1_), channel_id=1, source_target_pairs={{0,24},{2,26},{4,28},{6,30},{8,16},{10,18},{12,20},{14,22},{16,8},... | collective-permute-start | bytes 1179656 | tf_op jit(solution)/shard_map/ppermute | solution.py:212
  37.3 10.9 %copy-start.5 = (s32[512]{0:T(512)S(1)}, s32[512]{0:T(512)}, u32[]{:S(2)}) copy-start(s32[512]{0:T(512)} %param.9) | copy-start | bytes 6148
  37.3 10.9 %copy-start.6 = (s32[256,2]{0,1:T(2,128)S(1)}, s32[256,2]{0,1:T(2,128)}, u32[]{:S(2)}) copy-start(s32[256,2]{0,1:T(2,128)} %param.8) | copy-start | bytes 6148
  41.2 12.8 %collective-permute-start.10 = (bf16[96,2048]{1,0:T(8,128)(2,1)S(1)}, bf16[96,2048]{1,0:T(8,128)(2,1)S(1)}, u32[]{:S(2)}, u32[]{:S(2)}) collective-permute-start(bf16[96,2048]{1,0:T(8,128)(2,1)S(1)} %collective-permute-done.2.refs_0_), channel_id=1, source_target_pairs={{0,8},{2,10},{4,12},{6,14},{8,0},{10,2},{12,4},{14,6},{16,24},{18,... | collective-permute-start | bytes 1179656 | tf_op jit(solution)/shard_map/ppermute | solution.py:212
  43.9 11.5 %collective-permute-start.11 = (bf16[96,2048]{1,0:T(8,128)(2,1)S(1)}, bf16[96,2048]{1,0:T(8,128)(2,1)S(1)}, u32[]{:S(2)}, u32[]{:S(2)}) collective-permute-start(bf16[96,2048]{1,0:T(8,128)(2,1)S(1)} %collective-permute-done.1.refs_1_), channel_id=1, source_target_pairs={{0,2},{2,0},{4,6},{6,4},{8,10},{10,8},{12,14},{14,12},{16,18},{18,... | collective-permute-start | bytes 1179656 | tf_op jit(solution)/shard_map/ppermute | solution.py:212
  45.4 15.6 %collective-permute-start.12 = (bf16[96,2048]{1,0:T(8,128)(2,1)S(1)}, bf16[96,2048]{1,0:T(8,128)(2,1)S(1)}, u32[]{:S(2)}, u32[]{:S(2)}) collective-permute-start(bf16[96,2048]{1,0:T(8,128)(2,1)S(1)} %collective-permute-done.6.refs_1_), channel_id=1, source_target_pairs={{0,4},{2,6},{4,0},{6,2},{8,12},{10,14},{12,8},{14,10},{16,20},{18,... | collective-permute-start | bytes 1179656 | tf_op jit(solution)/shard_map/ppermute | solution.py:212
  45.9 15.1 %collective-permute-start.13 = (bf16[96,2048]{1,0:T(8,128)(2,1)S(1)}, bf16[96,2048]{1,0:T(8,128)(2,1)S(1)}, u32[]{:S(2)}, u32[]{:S(2)}) collective-permute-start(bf16[96,2048]{1,0:T(8,128)(2,1)S(1)} %collective-permute-done.6.refs_1_), channel_id=1, source_target_pairs={{0,8},{2,10},{4,12},{6,14},{8,0},{10,2},{12,4},{14,6},{16,24},{18,... | collective-permute-start | bytes 1179656 | tf_op jit(solution)/shard_map/ppermute | solution.py:212
  47.1 0.7 %copy-start.3 = (f32[256,96]{1,0:T(8,128)}, f32[256,96]{1,0:T(8,128)S(1)}, u32[]{:S(2)}) copy-start(f32[256,96]{1,0:T(8,128)S(1)} %get-tuple-element.107.refs_3_) | copy-start | bytes 294916
  47.7 13.3 %collective-permute-start.14 = (bf16[96,2048]{1,0:T(8,128)(2,1)S(1)}, bf16[96,2048]{1,0:T(8,128)(2,1)S(1)}, u32[]{:S(2)}, u32[]{:S(2)}) collective-permute-start(bf16[96,2048]{1,0:T(8,128)(2,1)S(1)} %collective-permute-done.5.refs_0_), channel_id=1, source_target_pairs={{0,2},{2,0},{4,6},{6,4},{8,10},{10,8},{12,14},{14,12},{16,18},{18,... | collective-permute-start | bytes 1179656 | tf_op jit(solution)/shard_map/ppermute | solution.py:212
  55.4 3.7 %copy-start.1 = (bf16[256,18432]{1,0:T(8,128)(2,1)S(1)}, bf16[256,18432]{1,0:T(8,128)(2,1)}, u32[]{:S(2)}) copy-start(bf16[256,18432]{1,0:T(8,128)(2,1)} %copy-done) | copy-start | bytes 28311556
  59.1 0.9 %copy-start.4 = (f32[256,96]{1,0:T(8,128)S(1)}, f32[256,96]{1,0:T(8,128)}, u32[]{:S(2)}) copy-start(f32[256,96]{1,0:T(8,128)} %copy-done.3) | copy-start | bytes 294916
  62.1 1.3 %collective-permute-start.15 = (f32[96,128]{1,0:T(8,128)S(1)}, f32[96,128]{1,0:T(8,128)S(1)}, u32[]{:S(2)}, u32[]{:S(2)}) collective-permute-start(f32[96,128]{1,0:T(8,128)S(1)} %constant_dynamic-slice_fusion), channel_id=1, source_target_pairs={{0,1},{1,0},{2,3},{3,2},{4,5},{5,4},{6,7},{7,6},{8,9},{9,8},{10,11... | collective-permute-start | bytes 147464 | tf_op jit(solution)/shard_map/ppermute | solution.py:236

commit v3 on v2

v3 whole, which is shorter than its diff:
```python
import functools

import jax
import jax.numpy as jnp
from jax import lax
from jax.experimental import pallas as pl
from jax.experimental.pallas import tpu as pltpu
from jax.sharding import PartitionSpec as P

LANES = 128
MIB = 2**20
X, Y, Z1, Z2, Z3 = 1, 2, 4, 8, 12
INNER, OUTER = (1, 2), (0, 3)
LOAD, MULTIPLY, STEP, PICK = "load", "multiply", "step", "pick"
EVENTS = (
    ("A", Z1, "O"), ("C1", Z3, "O", INNER), ("XO", X, "O"), ("YO", Y, "O"), LOAD, ("A",), STEP, ("C1",),
    ("C2", Z3, "O", OUTER), ("YA", Y, "A"), ("YO",), ("DO", X, "YO"), ("XO",), MULTIPLY, ("C2",), (PICK, "C"),
    ("XC", X, "C"), ("B", Z1, "C"), ("YC", Y, "C"), ("YA",), ("DO",), MULTIPLY, ("XC",), ("XB", Z1, "XC"), ("B",),
    ("YB", Y, "B"), ("YC",), ("XA", X, "A"), ("DC", X, "YC"), MULTIPLY, ("XB",), ("DB", Y, "XB"), ("DA", Z1, "DO"),
    ("YB",), ("XA",), MULTIPLY, ("DA",), ("DC",), ("DB",),
)
LOADS = {0: (1, 3), 1: (3, None)}
KEEP_AT = 2
COST = pl.CostEstimate(flops=1, bytes_accessed=4 * 10**6, transcendentals=0)
ANYWHERE = pl.BlockSpec(memory_space=pl.ANY)
VMEM = pl.BlockSpec(memory_space=pltpu.VMEM)


def lookup_irrep(orbitals, table):
    hits = orbitals[..., None] == jnp.arange(table.shape[0], dtype=jnp.int32)
    return jnp.sum(jnp.where(hits, table, 0), axis=-1)


def transpose_kernel(pairs, tile_ref, out_ref, flat, rows):
    depth = flat.shape[0] // 3
    flat[...] = tile_ref[...].astype(jnp.float32).reshape(flat.shape)
    x0, x1, x2 = [flat[pl.ds(s, depth, stride=3), :] for s in range(3)]
    lane = lax.broadcasted_iota(jnp.int32, x0.shape, 1)
    rows[pl.ds(0, depth, stride=4), :] = x0
    rows[pl.ds(1, depth, stride=4), :] = jnp.where(lane < 32, pltpu.roll(x0, 32, 1), pltpu.roll(x1, 32, 1))
    rows[pl.ds(2, depth, stride=4), :] = jnp.where(lane < 64, pltpu.roll(x1, 64, 1), pltpu.roll(x2, 64, 1))
    rows[pl.ds(3, depth, stride=4), :] = pltpu.roll(x2, 96, 1)
    out_ref[...] = rows[...].T[:pairs].astype(out_ref.dtype)


def transposed_tile(tile, pairs):
    size = tile.shape[1]
    return pl.pallas_call(
        functools.partial(transpose_kernel, pairs),
        out_shape=jax.ShapeDtypeStruct((pairs, size // pairs), tile.dtype),
        scratch_shapes=[
            pltpu.VMEM((size // LANES, LANES), jnp.float32),
            pltpu.VMEM((size // pairs, LANES), jnp.float32),
        ],
        compiler_params=pltpu.CompilerParams(vmem_limit_bytes=8 * MIB),
        name="transpose_tile",
    )(tile)


def product(left, right):
    return lax.dot_general(left, right, (((1,), (1,)), ((), ())), preferred_element_type=jnp.float32)


def step_kernel(mark_ref, out_ref):
    pass


def mark_step(mark):
    return pl.pallas_call(
        step_kernel,
        out_shape=jax.ShapeDtypeStruct(mark.shape, mark.dtype),
        in_specs=[ANYWHERE],
        out_specs=ANYWHERE,
        input_output_aliases={0: 0},
        cost_estimate=COST,
        compiler_params=pltpu.CompilerParams(vmem_limit_bytes=MIB),
        name="mark_step",
    )(mark)


def pick_kernel(inner_ref, outer_ref, mark_ref, out_ref, mark_out_ref):
    z = lax.axis_index("wide") // 4
    inner = jnp.logical_and(z > 0, z < 3)

    @pl.when(inner)
    def _():
        out_ref[...] = inner_ref[...]

    @pl.when(jnp.logical_not(inner))
    def _():
        out_ref[...] = outer_ref[...]


def pick_level(inner, outer, mark):
    return pl.pallas_call(
        pick_kernel,
        out_shape=[jax.ShapeDtypeStruct(inner.shape, inner.dtype), jax.ShapeDtypeStruct(mark.shape, mark.dtype)],
        in_specs=[VMEM, VMEM, ANYWHERE],
        out_specs=[VMEM, ANYWHERE],
        input_output_aliases={2: 1},
        cost_estimate=COST,
        compiler_params=pltpu.CompilerParams(vmem_limit_bytes=2 * MIB),
        name="pick_level",
    )(inner, outer, mark)


def keep_of(rows, pairs, pair_count, orbital_table, pair_table):
    columns = jnp.concatenate([orbital_table, orbital_table]).astype(jnp.float32).T
    row_labels = [jnp.zeros((1, rows.shape[1]), jnp.float32) for _ in range(2)]
    for block in range(orbital_table.shape[0]):
        ids = lax.broadcasted_iota(jnp.int32, (LANES, rows.shape[1]), 0) + block * LANES
        for k in range(2):
            hits = jnp.where(ids == rows[k:k + 1], columns[:, block:block + 1], 0.0)
            row_labels[k] += jnp.sum(hits, axis=0, keepdims=True)
    row_sym = jnp.bitwise_xor(*[label.astype(jnp.int32) for label in row_labels]).astype(jnp.float32)
    pair_labels = jnp.zeros(pairs.shape, jnp.int32)
    for k in range(pair_table.shape[0]):
        pair_labels = jnp.where(pairs == k, pair_table[k], pair_labels)
    pair_sym = jnp.bitwise_xor(pair_labels[0:1], pair_labels[1:2]).astype(jnp.float32)
    pair_sym = jnp.concatenate([pair_sym, jnp.zeros((1, -pair_count % LANES), jnp.float32)], axis=1)
    pair_sym = jnp.broadcast_to(pair_sym, (8, pair_sym.shape[1])).T[:pair_count, 0:1]
    return (pair_sym == row_sym).astype(jnp.float32)


def work_kernel(parts, depth, mark_ref, *refs):
    refs = list(refs)
    take = lambda count: [refs.pop(0) for _ in range(count)]
    me = lax.axis_index("wide")
    integrals = take(1) if parts["loads"] else []
    tables = take(4 if parts["pairs"] else 0)
    loaded = take(1 if parts["chunks"] else 0)
    chunks = take(parts["chunks"])
    total = take(parts["total"])
    keeps = take(1 if parts["pairs"] else 0)
    fetched = take(len(parts["loads"]))
    sums_out = take(2 if parts["last"] else 1 if parts["chunks"] else 0)
    copies = []
    for target, distances in zip(fetched, parts["loads"]):
        for k, distance in enumerate(distances):
            column = pl.multiple_of((me ^ distance) * depth, depth)
            source = integrals[0].at[:, pl.ds(column, depth)]
            copies.append(pltpu.make_async_copy(source, target.at[:, pl.ds(k * depth, depth)], refs[-1].at[len(copies)]))
    for copy in copies:
        copy.start()
    if chunks:
        sums = total[0][...] if total else None
        for k, chunk in enumerate(chunks):
            term = product(loaded[0][:, pl.ds(k * depth, depth)], chunk[...])
            sums = term if sums is None else sums + term
        if parts["last"]:
            part = parts["last"]
            mine = pl.multiple_of(lax.axis_index("narrow") * part, part)
            whole = refs.pop()
            whole[...] = sums.T
            sums_out[0][...] = whole[:, pl.ds(mine, part)]
            sums_out[1][...] = whole[:, pl.ds(part - mine, part)]
        else:
            sums_out[0][...] = sums
    if tables:
        part = keeps[0].shape[1]
        rows = tables[0][:, pl.ds(pl.multiple_of(lax.axis_index("narrow") * part, part), part)]
        keeps[0][...] = keep_of(rows, tables[1][...], parts["pairs"], tables[2][...], tables[3])
    for copy in copies:
        copy.wait()


def work(mark, depth, integrals=None, loads=(), loaded=None, chunks=(), total=None, last=0, tables=(), keep_shape=None):
    parts = {
        "loads": loads, "chunks": len(chunks), "total": 0 if total is None else 1, "last": last,
        "pairs": keep_shape[0] if tables else 0,
    }
    operands, specs, outs = [], [], []
    if loads:
        operands.append(integrals)
        specs.append(ANYWHERE)
    if tables:
        operands += tables
        specs += [VMEM, VMEM, VMEM, pl.BlockSpec(memory_space=pltpu.SMEM)]
        outs.append(jax.ShapeDtypeStruct(keep_shape, jnp.float32))
    for distances in loads:
        outs.append(jax.ShapeDtypeStruct((integrals.shape[0], depth * len(distances)), integrals.dtype))
    if chunks:
        operands += [loaded, *chunks] + ([] if total is None else [total])
        specs += [VMEM] * (len(operands) - len(specs))
        rows, pairs = loaded.shape[0], chunks[0].shape[0]
        outs += [jax.ShapeDtypeStruct(shape, jnp.float32) for shape in ([(pairs, last)] * 2 if last else [(rows, pairs)])]
    count = sum(len(distances) for distances in loads)
    *result, mark = pl.pallas_call(
        functools.partial(work_kernel, parts, depth),
        out_shape=outs + [jax.ShapeDtypeStruct(mark.shape, mark.dtype)],
        in_specs=[ANYWHERE] + specs,
        out_specs=[VMEM] * len(outs) + [ANYWHERE],
        input_output_aliases={0: len(outs)},
        scratch_shapes=(
            [pltpu.SemaphoreType.DMA((count,))] if count else [pltpu.VMEM((pairs, rows), jnp.float32)] if last else []
        ),
        cost_estimate=COST,
        compiler_params=pltpu.CompilerParams(vmem_limit_bytes=(20 if not loads else 30 if chunks else 40) * MIB),
        name="work",
    )(mark, *operands)
    keep = result.pop(0) if tables else None
    fetched = [result.pop(0) for _ in loads]
    return mark, fetched, (result if last else result.pop(0) if chunks else total), keep


def ring_kernel(integrals_ref, chunk_ref, out_ref):
    @pl.when(pl.program_id(0) == 0)
    def _():
        out_ref[...] = jnp.zeros_like(out_ref)

    out_ref[...] += product(integrals_ref[...], chunk_ref[0])


def gathered_product(integrals, own, axis_size):
    rows, (pairs, depth) = integrals.shape[0], own.shape
    gathered = lax.all_gather(own, "wide", axis=0)
    return pl.pallas_call(
        ring_kernel,
        out_shape=jax.ShapeDtypeStruct((rows, pairs), jnp.float32),
        grid=(axis_size,),
        in_specs=[
            pl.BlockSpec((rows, depth), lambda i: (0, i)),
            pl.BlockSpec((1, pairs, depth), lambda i: (i, 0, 0)),
        ],
        out_specs=pl.BlockSpec((rows, pairs), lambda i: (0, 0)),
        name="gathered_product",
    )(integrals, gathered)


def plan_of_events():
    distance, groups, arrived = {"O": 0}, [], ["O"]
    for event in EVENTS:
        if event in (LOAD, STEP):
            continue
        if event == MULTIPLY:
            groups.append(arrived)
            arrived = []
        elif event[0] == PICK:
            arrived.append(event[1])
        elif len(event) == 4:
            distance[event[0][:-1]] = distance[event[2]] ^ event[1]
        elif len(event) == 3:
            name, step, source = event
            distance[name] = distance[source] ^ step
        elif event[0] in distance:
            arrived.append(event[0])
    groups.append(arrived)
    assert sorted(distance[name] for names in groups for name in names) == list(range(16))
    return distance, groups


def exchanged_product(integrals, own, tables, keep_shape):
    depth = own.shape[1]
    distance, groups = plan_of_events()
    wanted = [tuple(distance[name] for name in names) for names in groups]
    held, fresh, loaded, total, keep, multiplied = {"O": own}, [], [], None, None, 0
    mark = jnp.zeros((8, LANES), jnp.float32)

    def ready():
        arrived = [held[name] for name in fresh]
        fresh.clear()
        return lax.optimization_barrier((mark, *arrived))[0]

    def multiply(**more):
        chunks = [held[name] for name in groups[multiplied]]
        return work(ready(), depth, loaded=loaded[multiplied], chunks=chunks, total=total, **more)

    for event in EVENTS:
        if event == STEP:
            mark = mark_step(ready())
        elif event == LOAD:
            mark, loaded, *_ = work(ready(), depth, integrals=integrals, loads=tuple(wanted[:1]))
        elif event == MULTIPLY:
            more = {}
            if multiplied in LOADS:
                more = {"integrals": integrals, "loads": tuple(wanted[slice(*LOADS[multiplied])])}
            if multiplied == KEEP_AT:
                more |= {"tables": tables, "keep_shape": keep_shape}
            mark, fetched, total, keeps = multiply(**more)
            loaded = loaded + fetched
            keep = keep if keeps is None else keeps
            multiplied += 1
        elif event[0] == PICK:
            name = event[1]
            held[name], mark = pick_level(held[name + "1"], held[name + "2"], ready())
        elif len(event) >= 3:
            name, step, source = event[:3]
            levels = event[3] if len(event) == 4 else range(4)
            value, mark, *_ = lax.optimization_barrier((held[source], mark, *[held[n] for n in fresh]))
            held[name] = lax.ppermute(value, "wide", [(i, i ^ step) for i in range(16) if i // 4 in levels])
        else:
            fresh.append(event[0])
    return *multiply(last=keep_shape[1])[2], keep


def masked_block(integrals, own, wide, row_orbitals, orb_irrep, occ_pairs, occ_irrep):
    row_labels = lookup_irrep(row_orbitals, orb_irrep)
    pair_labels = lookup_irrep(occ_pairs, occ_irrep)
    row_sym = jnp.bitwise_xor(row_labels[:, 0], row_labels[:, 1])
    pair_sym = jnp.bitwise_xor(pair_labels[:, 0], pair_labels[:, 1])
    block = gathered_product(integrals, own, wide)
    return jnp.where(row_sym[:, None] == pair_sym[None, :], block, jnp.zeros_like(block))


def shards(wide, narrow, integrals, amp_tiles, row_orbitals, orb_irrep, occ_pairs, occ_irrep):
    pairs = occ_pairs.shape[0]
    part = integrals.shape[0] // narrow
    own = transposed_tile(amp_tiles, pairs)
    if (wide, narrow) != (16, 2):
        block = masked_block(integrals, own, wide, row_orbitals, orb_irrep, occ_pairs, occ_irrep)
        return lax.psum_scatter(block, "narrow", scatter_dimension=0, tiled=True)
    tables = (row_orbitals.T, occ_pairs.T, orb_irrep.reshape(-1, LANES), occ_irrep)
    mine, other, keep = exchanged_product(integrals, own, tables, (pairs, part))
    summed = mine + lax.ppermute(other, "narrow", [(0, 1), (1, 0)])
    return jnp.where(keep > 0, summed, jnp.zeros_like(summed)).T


def solution(mesh):
    in_specs = (P("wide", "narrow"), P("narrow", "wide"), P("wide", None), P(), P(), P())
    out_specs = P(("wide", "narrow"), None)
    body = functools.partial(shards, mesh.shape["wide"], mesh.shape["narrow"])
    return jax.shard_map(body, mesh=mesh, in_specs=in_specs, out_specs=out_specs, check_vma=False)
```

time: 64.3 us -> 60 us (0.933)
  waiting for transfers between devices: 13 us -> 18.7 us
  starting transfers between devices: 30.6 us -> 25.1 us
  local copies, waits for them, and re-layouts: 6.4 us -> 1.15 us
  Pallas kernels: 12.8 us -> 14.1 us
    ppermute x15 -> x16, waiting for transfers between devices: 11.8 us -> 17.5 us  [exchanged_product(): lax.ppermute(value, 'wide', [(i, i ^ step) for i in range(16) if i // 4 i...]
    ppermute x15 -> x16, starting transfers between devices: 30.5 us -> 25 us  [exchanged_product(): lax.ppermute(value, 'wide', [(i, i ^ step) for i in range(16) if i // 4 i...]
    unnamed x18 -> x10, local copies, waits for them, and re-layouts: 6.38 us -> 1.15 us
    pallas_call x7, Pallas kernels: 12.1 us -> 13.4 us  [the longest x6 13.4 us: work(): pl.pallas_call(functools.partial(work_kernel, parts, depth), out_shape=ou...]
  transfers between devices with their start and end apart: 16 -> 17, of which waited for: 8 -> 9; matrix products, arithmetic and copies ran while one was open for 1% -> 0% of each run, Pallas kernels for 17% -> 21%
where the time goes in v3:
time: 60 us; the launch traced here: 59.8 us
  starting transfers between devices  25.1 us (42%)
  waiting for transfers between devices  18.7 us (31%)
  Pallas kernels  14.1 us (24%)
  local copies, waits for them, and re-layouts  1.15 us (2%)
  other arithmetic  0.63 us (1%)
    ppermute x16, starting transfers between devices, exchanged_product(): lax.ppermute(value, 'wide', [(i, i ^ step) for i in range(16) if i // 4 i...  25 us
    ppermute x16, waiting for transfers between devices, exchanged_product(): lax.ppermute(value, 'wide', [(i, i ^ step) for i in range(16) if i // 4 i...  17.5 us
    pallas_call x6, Pallas kernels, work(): pl.pallas_call(functools.partial(work_kernel, parts, depth), out_shape=ou...  13.4 us
    ppermute x1, waiting for transfers between devices, shards(): summed = mine + lax.ppermute(other, 'narrow', [(0, 1), (1, 0)])  1.22 us
  transfers between devices with their start and end apart: 17, of which 9 were waited for; matrix products, arithmetic and copies ran while one was open for 0% of the time, Pallas kernels for 21%

profile of v3, /device:TPU:0, one launch (start us, length us, event | category | flops | bytes accessed | tf_op | source)
XLA Modules:
  0.0 59.8 jit_solution(13306316407134443128)
XLA Ops:
  0.0 1.1 %copy-done = bf16[1,196608]{1,0:T(2,128)(2,1)S(1)} copy-done((bf16[1,196608]{1,0:T(2,128)(2,1)S(1)}, bf16[1,196608]{1,0:T(2,128)(2,1)}, u32[]{:S(2)}) %copy-start) | copy-done | bytes 393240
  1.1 0.7 %transpose_tile.1.refs_2_ = bf16[96,2048]{1,0:T(8,128)(2,1)S(1)} custom-call(bf16[1,196608]{1,0:T(2,128)(2,1)S(1)} %copy-done), custom_call_target="tpu_custom_call" | custom-call | tf_op jit(solution)/shard_map/transpose_tile/pallas_call | solution.py:48
  1.8 3.1 %collective-permute-start.1 = (bf16[96,2048]{1,0:T(8,128)(2,1)S(1)}, bf16[96,2048]{1,0:T(8,128)(2,1)S(1)}, u32[]{:S(2)}, u32[]{:S(2)}) collective-permute-start(bf16[96,2048]{1,0:T(8,128)(2,1)S(1)} %transpose_tile.1.refs_2_), channel_id=1, source_target_pairs={{0,8},{2,10},{4,12},{6,14},{8,0},{10,2},{12,4},{14,6},{16,24},{18,... | collective-permute-start | bytes 1179656 | tf_op jit(solution)/shard_map/ppermute | solution.py:290
  4.9 0.7 %collective-permute-start = (bf16[96,2048]{1,0:T(8,128)(2,1)S(1)}, bf16[96,2048]{1,0:T(8,128)(2,1)S(1)}, u32[]{:S(2)}, u32[]{:S(2)}) collective-permute-start(bf16[96,2048]{1,0:T(8,128)(2,1)S(1)} %transpose_tile.1.refs_2_), channel_id=1, source_target_pairs={{8,16},{10,18},{12,20},{14,22},{16,8},{18,10},{20,12},{22,14},{9,1... | collective-permute-start | bytes 1179656 | tf_op jit(solution)/shard_map/ppermute | solution.py:290
  5.6 1.6 %collective-permute-start.3 = (bf16[96,2048]{1,0:T(8,128)(2,1)S(1)}, bf16[96,2048]{1,0:T(8,128)(2,1)S(1)}, u32[]{:S(2)}, u32[]{:S(2)}) collective-permute-start(bf16[96,2048]{1,0:T(8,128)(2,1)S(1)} %transpose_tile.1.refs_2_), channel_id=1, source_target_pairs={{0,4},{2,6},{4,0},{6,2},{8,12},{10,14},{12,8},{14,10},{16,20},{18,... | collective-permute-start | bytes 1179656 | tf_op jit(solution)/shard_map/ppermute | solution.py:290
  7.2 1.5 %collective-permute-start.4 = (bf16[96,2048]{1,0:T(8,128)(2,1)S(1)}, bf16[96,2048]{1,0:T(8,128)(2,1)S(1)}, u32[]{:S(2)}, u32[]{:S(2)}) collective-permute-start(bf16[96,2048]{1,0:T(8,128)(2,1)S(1)} %transpose_tile.1.refs_2_), channel_id=1, source_target_pairs={{0,2},{2,0},{4,6},{6,4},{8,10},{10,8},{12,14},{14,12},{16,18},{18,... | collective-permute-start | bytes 1179656 | tf_op jit(solution)/shard_map/ppermute | solution.py:290
  8.7 2.2 %work.6 = (bf16[256,8192]{1,0:T(8,128)(2,1)S(1)}, f32[8,128]{1,0:T(8,128)S(1)}) custom-call(f32[8,128]{1,0:T(8,128)S(1)} %broadcast_in_dim.3.mark_ref, bf16[256,32768]{1,0:T(8,128)(2,1)} %refs_0_.5), custom_call_target="tpu_custom_call", output_to_operand_aliasing={{1}: (0, {})} | custom-call | flops 1 | bytes 4000000 | tf_op jit(solution)/shard_map/work/pallas_call | solution.py:188
  10.9 3.1 %collective-permute-done.1.refs_3_ = bf16[96,2048]{1,0:T(8,128)(2,1)S(1)} collective-permute-done((bf16[96,2048]{1,0:T(8,128)(2,1)S(1)}, bf16[96,2048]{1,0:T(8,128)(2,1)S(1)}, u32[]{:S(2)}, u32[]{:S(2)}) %collective-permute-start.1) | collective-permute-done | bytes 393248 | tf_op jit(solution)/shard_map/ppermute | solution.py:290
  14.0 5.7 %collective-permute-start.2 = (bf16[96,2048]{1,0:T(8,128)(2,1)S(1)}, bf16[96,2048]{1,0:T(8,128)(2,1)S(1)}, u32[]{:S(2)}, u32[]{:S(2)}) collective-permute-start(bf16[96,2048]{1,0:T(8,128)(2,1)S(1)} %transpose_tile.1.refs_2_), channel_id=1, source_target_pairs={{0,24},{2,26},{4,28},{6,30},{24,0},{26,2},{28,4},{30,6},{1,25},{3,... | collective-permute-start | bytes 1179656 | tf_op jit(solution)/shard_map/ppermute | solution.py:290
  19.7 1.6 %collective-permute-start.9 = (bf16[96,2048]{1,0:T(8,128)(2,1)S(1)}, bf16[96,2048]{1,0:T(8,128)(2,1)S(1)}, u32[]{:S(2)}, u32[]{:S(2)}) collective-permute-start(bf16[96,2048]{1,0:T(8,128)(2,1)S(1)} %collective-permute-done.3.refs_4_), channel_id=1, source_target_pairs={{0,2},{2,0},{4,6},{6,4},{8,10},{10,8},{12,14},{14,12},{16,18},{18,... | collective-permute-start | bytes 1179656 | tf_op jit(solution)/shard_map/ppermute | solution.py:290
  21.3 1.5 %collective-permute-start.8 = (bf16[96,2048]{1,0:T(8,128)(2,1)S(1)}, bf16[96,2048]{1,0:T(8,128)(2,1)S(1)}, u32[]{:S(2)}, u32[]{:S(2)}) collective-permute-start(bf16[96,2048]{1,0:T(8,128)(2,1)S(1)} %collective-permute-done.1.refs_3_), channel_id=1, source_target_pairs={{0,4},{2,6},{4,0},{6,2},{8,12},{10,14},{12,8},{14,10},{16,20},{18,... | collective-permute-start | bytes 1179656 | tf_op jit(solution)/shard_map/ppermute | solution.py:290
  22.8 3.9 %work.7 = (bf16[256,6144]{1,0:T(8,128)(2,1)S(1)}, bf16[256,6144]{1,0:T(8,128)(2,1)S(1)}, f32[256,96]{1,0:T(8,128)S(1)}, f32[8,128]{1,0:T(8,128)S(1)}) custom-call(f32[8,128]{1,0:T(8,128)S(1)} %mark_step.1.mark_ref, bf16[256,32768]{1,0:T(8,128)(2,1)} %refs_0_.5, bf16[256,8192]{1,0:T(8,128)(2,1)S(1)} %get-tuple-element.77.refs_1_, ...), custom_call_target="tpu_custom_call", output_to_operand_aliasing={{3}: (0, {})} | custom-call | flops 1 | bytes 4000000 | tf_op jit(solution)/shard_map/work/pallas_call | solution.py:188
  26.7 1.3 %collective-permute-done.2.outer_ref = bf16[96,2048]{1,0:T(8,128)(2,1)S(1)} collective-permute-done((bf16[96,2048]{1,0:T(8,128)(2,1)S(1)}, bf16[96,2048]{1,0:T(8,128)(2,1)S(1)}, u32[]{:S(2)}, u32[]{:S(2)}) %collective-permute-start.2) | collective-permute-done | bytes 393248 | tf_op jit(solution)/shard_map/ppermute | solution.py:290
  28.0 1.5 %collective-permute-start.7 = (bf16[96,2048]{1,0:T(8,128)(2,1)S(1)}, bf16[96,2048]{1,0:T(8,128)(2,1)S(1)}, u32[]{:S(2)}, u32[]{:S(2)}) collective-permute-start(bf16[96,2048]{1,0:T(8,128)(2,1)S(1)} %get-tuple-element.80.refs_2_), channel_id=1, source_target_pairs={{0,2},{2,0},{4,6},{6,4},{8,10},{10,8},{12,14},{14,12},{16,18},{18,... | collective-permute-start | bytes 1179656 | tf_op jit(solution)/shard_map/ppermute | solution.py:290
  29.5 1.5 %collective-permute-start.5 = (bf16[96,2048]{1,0:T(8,128)(2,1)S(1)}, bf16[96,2048]{1,0:T(8,128)(2,1)S(1)}, u32[]{:S(2)}, u32[]{:S(2)}) collective-permute-start(bf16[96,2048]{1,0:T(8,128)(2,1)S(1)} %get-tuple-element.80.refs_2_), channel_id=1, source_target_pairs={{0,4},{2,6},{4,0},{6,2},{8,12},{10,14},{12,8},{14,10},{16,20},{18,... | collective-permute-start | bytes 1179656 | tf_op jit(solution)/shard_map/ppermute | solution.py:290
  31.4 3.7 %work.8 = (bf16[256,6144]{1,0:T(8,128)(2,1)S(1)}, bf16[256,6144]{1,0:T(8,128)(2,1)S(1)}, f32[256,96]{1,0:T(8,128)S(1)}, f32[8,128]{1,0:T(8,128)S(1)}) custom-call(f32[8,128]{1,0:T(8,128)S(1)} %get-tuple-element.89.mark_ref, bf16[256,32768]{1,0:T(8,128)(2,1)} %refs_0_.5, ...), custom_call_target="tpu_custom_call", output_to_operand_aliasing={{3}: (0, {})} | custom-call | flops 1 | bytes 4000000 | tf_op jit(solution)/shard_map/work/pallas_call | solution.py:188
  35.1 2.8 %collective-permute-done.7.refs_5_ = bf16[96,2048]{1,0:T(8,128)(2,1)S(1)} collective-permute-done((bf16[96,2048]{1,0:T(8,128)(2,1)S(1)}, bf16[96,2048]{1,0:T(8,128)(2,1)S(1)}, u32[]{:S(2)}, u32[]{:S(2)}) %collective-permute-start.7) | collective-permute-done | bytes 393248 | tf_op jit(solution)/shard_map/ppermute | solution.py:290
  37.9 1.2 %collective-permute-start.10 = (bf16[96,2048]{1,0:T(8,128)(2,1)S(1)}, bf16[96,2048]{1,0:T(8,128)(2,1)S(1)}, u32[]{:S(2)}, u32[]{:S(2)}) collective-permute-start(bf16[96,2048]{1,0:T(8,128)(2,1)S(1)} %collective-permute-done.7.refs_5_), channel_id=1, source_target_pairs={{0,8},{2,10},{4,12},{6,14},{8,0},{10,2},{12,4},{14,6},{16,24},{18,... | collective-permute-start | bytes 1179656 | tf_op jit(solution)/shard_map/ppermute | solution.py:290
  39.1 1.5 %collective-permute-start.12 = (bf16[96,2048]{1,0:T(8,128)(2,1)S(1)}, bf16[96,2048]{1,0:T(8,128)(2,1)S(1)}, u32[]{:S(2)}, u32[]{:S(2)}) collective-permute-start(bf16[96,2048]{1,0:T(8,128)(2,1)S(1)} %collective-permute-done.1.refs_3_), channel_id=1, source_target_pairs={{0,2},{2,0},{4,6},{6,4},{8,10},{10,8},{12,14},{14,12},{16,18},{18,... | collective-permute-start | bytes 1179656 | tf_op jit(solution)/shard_map/ppermute | solution.py:290
  40.6 0.6 %collective-permute-start.11 = (bf16[96,2048]{1,0:T(8,128)(2,1)S(1)}, bf16[96,2048]{1,0:T(8,128)(2,1)S(1)}, u32[]{:S(2)}, u32[]{:S(2)}) collective-permute-start(bf16[96,2048]{1,0:T(8,128)(2,1)S(1)} %collective-permute-done.6.refs_6_), channel_id=1, source_target_pairs={{0,4},{2,6},{4,0},{6,2},{8,12},{10,14},{12,8},{14,10},{16,20},{18,... | collective-permute-start | bytes 1179656 | tf_op jit(solution)/shard_map/ppermute | solution.py:290
  41.2 1.5 %collective-permute-start.14 = (bf16[96,2048]{1,0:T(8,128)(2,1)S(1)}, bf16[96,2048]{1,0:T(8,128)(2,1)S(1)}, u32[]{:S(2)}, u32[]{:S(2)}) collective-permute-start(bf16[96,2048]{1,0:T(8,128)(2,1)S(1)} %collective-permute-done.5.refs_7_), channel_id=1, source_target_pairs={{0,2},{2,0},{4,6},{6,4},{8,10},{10,8},{12,14},{14,12},{16,18},{18,... | collective-permute-start | bytes 1179656 | tf_op jit(solution)/shard_map/ppermute | solution.py:290
  42.7 1.6 %work.9 = (f32[96,128]{1,0:T(8,128)S(1)}, f32[256,96]{1,0:T(8,128)S(1)}, f32[8,128]{1,0:T(8,128)S(1)}) custom-call(f32[8,128]{1,0:T(8,128)S(1)} %get-tuple-element.97.mark_ref, s32[2,256]{1,0:T(2,128)S(1)} %bitcast.5, s32[2,96]{1,0:T(2,128)S(1)} %bitcast.7, s32[4,128]{1,0:T(4,128)S(1)} %bitcast.6, s32[16]{0:T(128)S(1)} %copy-done.4, ...), custom_call_target="tpu_custom_call", output_to_operand_aliasing={{2}: (0, {})} | custom-call | flops 1 | bytes 4000000 | tf_op jit(solution)/shard_map/work/pallas_call | solution.py:188
  44.2 3.0 %collective-permute-done.10.refs_1_ = bf16[96,2048]{1,0:T(8,128)(2,1)S(1)} collective-permute-done((bf16[96,2048]{1,0:T(8,128)(2,1)S(1)}, bf16[96,2048]{1,0:T(8,128)(2,1)S(1)}, u32[]{:S(2)}, u32[]{:S(2)}) %collective-permute-start.10) | collective-permute-done | bytes 393248 | tf_op jit(solution)/shard_map/ppermute | solution.py:290
  47.2 0.9 %collective-permute-start.13 = (bf16[96,2048]{1,0:T(8,128)(2,1)S(1)}, bf16[96,2048]{1,0:T(8,128)(2,1)S(1)}, u32[]{:S(2)}, u32[]{:S(2)}) collective-permute-start(bf16[96,2048]{1,0:T(8,128)(2,1)S(1)} %collective-permute-done.9.refs_4_), channel_id=1, source_target_pairs={{0,8},{2,10},{4,12},{6,14},{8,0},{10,2},{12,4},{14,6},{16,24},{18,... | collective-permute-start | bytes 1179656 | tf_op jit(solution)/shard_map/ppermute | solution.py:290
  48.1 0.8 %collective-permute-start.15 = (bf16[96,2048]{1,0:T(8,128)(2,1)S(1)}, bf16[96,2048]{1,0:T(8,128)(2,1)S(1)}, u32[]{:S(2)}, u32[]{:S(2)}) collective-permute-start(bf16[96,2048]{1,0:T(8,128)(2,1)S(1)} %collective-permute-done.10.refs_1_), channel_id=1, source_target_pairs={{0,4},{2,6},{4,0},{6,2},{8,12},{10,14},{12,8},{14,10},{16,20},{18,... | collective-permute-start | bytes 1179656 | tf_op jit(solution)/shard_map/ppermute | solution.py:290
  48.9 2.2 %collective-permute-done.12.refs_3_ = bf16[96,2048]{1,0:T(8,128)(2,1)S(1)} collective-permute-done((bf16[96,2048]{1,0:T(8,128)(2,1)S(1)}, bf16[96,2048]{1,0:T(8,128)(2,1)S(1)}, u32[]{:S(2)}, u32[]{:S(2)}) %collective-permute-start.12) | collective-permute-done | bytes 393248 | tf_op jit(solution)/shard_map/ppermute | solution.py:290
  51.2 1.0 %work.10 = (f32[256,96]{1,0:T(8,128)S(1)}, f32[8,128]{1,0:T(8,128)S(1)}) custom-call(f32[8,128]{1,0:T(8,128)S(1)} %get-tuple-element.107.mark_ref, bf16[256,6144]{1,0:T(8,128)(2,1)S(1)} %get-tuple-element.108.refs_0_, bf16[96,2048]{1,0:T(8,128)(2,1)S(1)} %collective-permute-done.10.refs_1_, ...), custom_call_target="tpu_custom_call", output_to_operand_aliasing={{1}: (0, {})} | custom-call | flops 1 | bytes 4000000 | tf_op jit(solution)/shard_map/work/pallas_call | solution.py:188
  52.2 4.1 %collective-permute-done.14.refs_2_ = bf16[96,2048]{1,0:T(8,128)(2,1)S(1)} collective-permute-done((bf16[96,2048]{1,0:T(8,128)(2,1)S(1)}, bf16[96,2048]{1,0:T(8,128)(2,1)S(1)}, u32[]{:S(2)}, u32[]{:S(2)}) %collective-permute-start.14) | collective-permute-done | bytes 393248 | tf_op jit(solution)/shard_map/ppermute | solution.py:290
  56.2 0.5 collective-permute-done.15.refs_3_
  56.8 1.0 %work.11 = (f32[96,128]{1,0:T(8,128)S(1)}, f32[96,128]{1,0:T(8,128)S(1)}, f32[8,128]{1,0:T(8,128)S(1)}) custom-call(f32[8,128]{1,0:T(8,128)S(1)} %get-tuple-element.114.mark_ref, bf16[256,6144]{1,0:T(8,128)(2,1)S(1)} %get-tuple-element.115.refs_0_, bf16[96,2048]{1,0:T(8,128)(2,1)S(1)} %collective-permute-done.13.refs_1_, ...), custom_call_target="tpu_custom_call", output_to_operand_aliasing={{2}: (0, {})} | custom-call | flops 1 | bytes 4000000 | tf_op jit(solution)/shard_map/work/pallas_call | solution.py:188
  57.9 1.2 %collective-permute-done.16 = f32[96,128]{1,0:T(8,128)S(1)} collective-permute-done((f32[96,128]{1,0:T(8,128)S(1)}, f32[96,128]{1,0:T(8,128)S(1)}, u32[]{:S(2)}, u32[]{:S(2)}) %collective-permute-start.16) | collective-permute-done | bytes 49184 | tf_op jit(solution)/shard_map/ppermute | solution.py:314
  59.1 0.6 %select_bitcast_fusion = f32[128,96]{0,1:T(8,128)} fusion(f32[96,128]{1,0:T(8,128)S(1)} %get-tuple-element.117, f32[96,128]{1,0:T(8,128)S(1)} %collective-permute-done.16, f32[96,128]{1,0:T(8,128)S(1)} %get-tuple-element.100), kind=kLoop, calls=%fused_computation | loop fusion | flops 36864 | bytes 196608 | tf_op jit(solution)/shard_map/transpose | solution.py:315
  (23 shorter events, 0.5 us)
Async XLA Ops:
  0.0 1.1 %copy-start = (bf16[1,196608]{1,0:T(2,128)(2,1)S(1)}, bf16[1,196608]{1,0:T(2,128)(2,1)}, u32[]{:S(2)}) copy-start(bf16[1,196608]{1,0:T(2,128)(2,1)} %tile_ref.1) | copy-start | bytes 1179652
  1.8 12.2 %collective-permute-start.1 = (bf16[96,2048]{1,0:T(8,128)(2,1)S(1)}, bf16[96,2048]{1,0:T(8,128)(2,1)S(1)}, u32[]{:S(2)}, u32[]{:S(2)}) collective-permute-start(bf16[96,2048]{1,0:T(8,128)(2,1)S(1)} %transpose_tile.1.refs_2_), channel_id=1, source_target_pairs={{0,8},{2,10},{4,12},{6,14},{8,0},{10,2},{12,4},{14,6},{16,24},{18,... | collective-permute-start | bytes 1179656 | tf_op jit(solution)/shard_map/ppermute | solution.py:290
  4.9 9.1 %collective-permute-start = (bf16[96,2048]{1,0:T(8,128)(2,1)S(1)}, bf16[96,2048]{1,0:T(8,128)(2,1)S(1)}, u32[]{:S(2)}, u32[]{:S(2)}) collective-permute-start(bf16[96,2048]{1,0:T(8,128)(2,1)S(1)} %transpose_tile.1.refs_2_), channel_id=1, source_target_pairs={{8,16},{10,18},{12,20},{14,22},{16,8},{18,10},{20,12},{22,14},{9,1... | collective-permute-start | bytes 1179656 | tf_op jit(solution)/shard_map/ppermute | solution.py:290
  5.6 14.1 %collective-permute-start.3 = (bf16[96,2048]{1,0:T(8,128)(2,1)S(1)}, bf16[96,2048]{1,0:T(8,128)(2,1)S(1)}, u32[]{:S(2)}, u32[]{:S(2)}) collective-permute-start(bf16[96,2048]{1,0:T(8,128)(2,1)S(1)} %transpose_tile.1.refs_2_), channel_id=1, source_target_pairs={{0,4},{2,6},{4,0},{6,2},{8,12},{10,14},{12,8},{14,10},{16,20},{18,... | collective-permute-start | bytes 1179656 | tf_op jit(solution)/shard_map/ppermute | solution.py:290
  7.2 12.5 %collective-permute-start.4 = (bf16[96,2048]{1,0:T(8,128)(2,1)S(1)}, bf16[96,2048]{1,0:T(8,128)(2,1)S(1)}, u32[]{:S(2)}, u32[]{:S(2)}) collective-permute-start(bf16[96,2048]{1,0:T(8,128)(2,1)S(1)} %transpose_tile.1.refs_2_), channel_id=1, source_target_pairs={{0,2},{2,0},{4,6},{6,4},{8,10},{10,8},{12,14},{14,12},{16,18},{18,... | collective-permute-start | bytes 1179656 | tf_op jit(solution)/shard_map/ppermute | solution.py:290
  14.0 14.0 %collective-permute-start.2 = (bf16[96,2048]{1,0:T(8,128)(2,1)S(1)}, bf16[96,2048]{1,0:T(8,128)(2,1)S(1)}, u32[]{:S(2)}, u32[]{:S(2)}) collective-permute-start(bf16[96,2048]{1,0:T(8,128)(2,1)S(1)} %transpose_tile.1.refs_2_), channel_id=1, source_target_pairs={{0,24},{2,26},{4,28},{6,30},{24,0},{26,2},{28,4},{30,6},{1,25},{3,... | collective-permute-start | bytes 1179656 | tf_op jit(solution)/shard_map/ppermute | solution.py:290
  19.7 11.3 %collective-permute-start.9 = (bf16[96,2048]{1,0:T(8,128)(2,1)S(1)}, bf16[96,2048]{1,0:T(8,128)(2,1)S(1)}, u32[]{:S(2)}, u32[]{:S(2)}) collective-permute-start(bf16[96,2048]{1,0:T(8,128)(2,1)S(1)} %collective-permute-done.3.refs_4_), channel_id=1, source_target_pairs={{0,2},{2,0},{4,6},{6,4},{8,10},{10,8},{12,14},{14,12},{16,18},{18,... | collective-permute-start | bytes 1179656 | tf_op jit(solution)/shard_map/ppermute | solution.py:290
  21.3 10.1 %collective-permute-start.8 = (bf16[96,2048]{1,0:T(8,128)(2,1)S(1)}, bf16[96,2048]{1,0:T(8,128)(2,1)S(1)}, u32[]{:S(2)}, u32[]{:S(2)}) collective-permute-start(bf16[96,2048]{1,0:T(8,128)(2,1)S(1)} %collective-permute-done.1.refs_3_), channel_id=1, source_target_pairs={{0,4},{2,6},{4,0},{6,2},{8,12},{10,14},{12,8},{14,10},{16,20},{18,... | collective-permute-start | bytes 1179656 | tf_op jit(solution)/shard_map/ppermute | solution.py:290
  28.0 9.9 %collective-permute-start.7 = (bf16[96,2048]{1,0:T(8,128)(2,1)S(1)}, bf16[96,2048]{1,0:T(8,128)(2,1)S(1)}, u32[]{:S(2)}, u32[]{:S(2)}) collective-permute-start(bf16[96,2048]{1,0:T(8,128)(2,1)S(1)} %get-tuple-element.80.refs_2_), channel_id=1, source_target_pairs={{0,2},{2,0},{4,6},{6,4},{8,10},{10,8},{12,14},{14,12},{16,18},{18,... | collective-permute-start | bytes 1179656 | tf_op jit(solution)/shard_map/ppermute | solution.py:290
  29.5 9.6 %collective-permute-start.6 = (bf16[96,2048]{1,0:T(8,128)(2,1)S(1)}, bf16[96,2048]{1,0:T(8,128)(2,1)S(1)}, u32[]{:S(2)}, u32[]{:S(2)}) collective-permute-start(bf16[96,2048]{1,0:T(8,128)(2,1)S(1)} %get-tuple-element.80.refs_2_), channel_id=1, source_target_pairs={{0,8},{2,10},{4,12},{6,14},{8,0},{10,2},{12,4},{14,6},{16,24},{18,... | collective-permute-start | bytes 1179656 | tf_op jit(solution)/shard_map/ppermute | solution.py:290
  29.5 9.6 %collective-permute-start.5 = (bf16[96,2048]{1,0:T(8,128)(2,1)S(1)}, bf16[96,2048]{1,0:T(8,128)(2,1)S(1)}, u32[]{:S(2)}, u32[]{:S(2)}) collective-permute-start(bf16[96,2048]{1,0:T(8,128)(2,1)S(1)} %get-tuple-element.80.refs_2_), channel_id=1, source_target_pairs={{0,4},{2,6},{4,0},{6,2},{8,12},{10,14},{12,8},{14,10},{16,20},{18,... | collective-permute-start | bytes 1179656 | tf_op jit(solution)/shard_map/ppermute | solution.py:290
  31.4 11.3 %copy-start.1 = (s32[256,2]{0,1:T(2,128)S(1)}, s32[256,2]{0,1:T(2,128)}, u32[]{:S(2)}) copy-start(s32[256,2]{0,1:T(2,128)} %param.8) | copy-start | bytes 6148
  31.4 11.3 %copy-start.2 = (s32[512]{0:T(512)S(1)}, s32[512]{0:T(512)}, u32[]{:S(2)}) copy-start(s32[512]{0:T(512)} %param.9) | copy-start | bytes 6148
  31.4 11.3 %copy-start.3 = (s32[96,2]{0,1:T(2,128)S(1)}, s32[96,2]{0,1:T(2,128)}, u32[]{:S(2)}) copy-start(s32[96,2]{0,1:T(2,128)} %param.10) | copy-start | bytes 2308
  31.4 11.3 %copy-start.4 = (s32[16]{0:T(128)S(1)}, s32[16]{0:T(128)}, u32[]{:S(2)}) copy-start(s32[16]{0:T(128)} %refs_3_.1) | copy-start | bytes 196
  37.9 9.3 %collective-permute-start.10 = (bf16[96,2048]{1,0:T(8,128)(2,1)S(1)}, bf16[96,2048]{1,0:T(8,128)(2,1)S(1)}, u32[]{:S(2)}, u32[]{:S(2)}) collective-permute-start(bf16[96,2048]{1,0:T(8,128)(2,1)S(1)} %collective-permute-done.7.refs_5_), channel_id=1, source_target_pairs={{0,8},{2,10},{4,12},{6,14},{8,0},{10,2},{12,4},{14,6},{16,24},{18,... | collective-permute-start | bytes 1179656 | tf_op jit(solution)/shard_map/ppermute | solution.py:290
  39.1 12.1 %collective-permute-start.12 = (bf16[96,2048]{1,0:T(8,128)(2,1)S(1)}, bf16[96,2048]{1,0:T(8,128)(2,1)S(1)}, u32[]{:S(2)}, u32[]{:S(2)}) collective-permute-start(bf16[96,2048]{1,0:T(8,128)(2,1)S(1)} %collective-permute-done.1.refs_3_), channel_id=1, source_target_pairs={{0,2},{2,0},{4,6},{6,4},{8,10},{10,8},{12,14},{14,12},{16,18},{18,... | collective-permute-start | bytes 1179656 | tf_op jit(solution)/shard_map/ppermute | solution.py:290
  40.6 10.6 %collective-permute-start.11 = (bf16[96,2048]{1,0:T(8,128)(2,1)S(1)}, bf16[96,2048]{1,0:T(8,128)(2,1)S(1)}, u32[]{:S(2)}, u32[]{:S(2)}) collective-permute-start(bf16[96,2048]{1,0:T(8,128)(2,1)S(1)} %collective-permute-done.6.refs_6_), channel_id=1, source_target_pairs={{0,4},{2,6},{4,0},{6,2},{8,12},{10,14},{12,8},{14,10},{16,20},{18,... | collective-permute-start | bytes 1179656 | tf_op jit(solution)/shard_map/ppermute | solution.py:290
  41.2 15.1 %collective-permute-start.14 = (bf16[96,2048]{1,0:T(8,128)(2,1)S(1)}, bf16[96,2048]{1,0:T(8,128)(2,1)S(1)}, u32[]{:S(2)}, u32[]{:S(2)}) collective-permute-start(bf16[96,2048]{1,0:T(8,128)(2,1)S(1)} %collective-permute-done.5.refs_7_), channel_id=1, source_target_pairs={{0,2},{2,0},{4,6},{6,4},{8,10},{10,8},{12,14},{14,12},{16,18},{18,... | collective-permute-start | bytes 1179656 | tf_op jit(solution)/shard_map/ppermute | solution.py:290
  47.2 9.0 %collective-permute-start.13 = (bf16[96,2048]{1,0:T(8,128)(2,1)S(1)}, bf16[96,2048]{1,0:T(8,128)(2,1)S(1)}, u32[]{:S(2)}, u32[]{:S(2)}) collective-permute-start(bf16[96,2048]{1,0:T(8,128)(2,1)S(1)} %collective-permute-done.9.refs_4_), channel_id=1, source_target_pairs={{0,8},{2,10},{4,12},{6,14},{8,0},{10,2},{12,4},{14,6},{16,24},{18,... | collective-permute-start | bytes 1179656 | tf_op jit(solution)/shard_map/ppermute | solution.py:290
  48.1 8.6 %collective-permute-start.15 = (bf16[96,2048]{1,0:T(8,128)(2,1)S(1)}, bf16[96,2048]{1,0:T(8,128)(2,1)S(1)}, u32[]{:S(2)}, u32[]{:S(2)}) collective-permute-start(bf16[96,2048]{1,0:T(8,128)(2,1)S(1)} %collective-permute-done.10.refs_1_), channel_id=1, source_target_pairs={{0,4},{2,6},{4,0},{6,2},{8,12},{10,14},{12,8},{14,10},{16,20},{18,... | collective-permute-start | bytes 1179656 | tf_op jit(solution)/shard_map/ppermute | solution.py:290
  57.8 1.3 %collective-permute-start.16 = (f32[96,128]{1,0:T(8,128)S(1)}, f32[96,128]{1,0:T(8,128)S(1)}, u32[]{:S(2)}, u32[]{:S(2)}) collective-permute-start(f32[96,128]{1,0:T(8,128)S(1)} %get-tuple-element.118), channel_id=1, source_target_pairs={{0,1},{1,0},{2,3},{3,2},{4,5},{5,4},{6,7},{7,6},{8,9},{9,8},{10,11... | collective-permute-start | bytes 147464 | tf_op jit(solution)/shard_map/ppermute | solution.py:314

commit v4 on v3

--- a/solution.py
+++ b/solution.py
@@ -17,7 +17,7 @@
     ("C2", Z3, "O", OUTER), ("YA", Y, "A"), ("YO",), ("DO", X, "YO"), ("XO",), MULTIPLY, ("C2",), (PICK, "C"),
     ("XC", X, "C"), ("B", Z1, "C"), ("YC", Y, "C"), ("YA",), ("DO",), MULTIPLY, ("XC",), ("XB", Z1, "XC"), ("B",),
     ("YB", Y, "B"), ("YC",), ("XA", X, "A"), ("DC", X, "YC"), MULTIPLY, ("XB",), ("DB", Y, "XB"), ("DA", Z1, "DO"),
-    ("YB",), ("XA",), MULTIPLY, ("DA",), ("DC",), ("DB",),
+    ("YB",), ("XA",), MULTIPLY, ("DC",), ("DA",), MULTIPLY, ("DB",),
 )
 LOADS = {0: (1, 3), 1: (3, None)}
 KEEP_AT = 2

time: 60 us -> 59.6 us (level)
    pallas_call x6 -> x7, Pallas kernels: 13.4 us -> 13.6 us  [work(): pl.pallas_call(functools.partial(work_kernel, parts, depth), out_shape=ou...]
  transfers between devices with their start and end apart: 17 -> 17, of which waited for: 9 -> 8; matrix products, arithmetic and copies ran while one was open for 0% -> 0% of each run, Pallas kernels for 21% -> 22%
where the time goes in v4:
time: 59.6 us; the launch traced here: 59.4 us
  starting transfers between devices  25.1 us (42%)
  waiting for transfers between devices  18.1 us (30%)
  Pallas kernels  14.3 us (24%)
  local copies, waits for them, and re-layouts  1.15 us (2%)
  other arithmetic  0.63 us (1%)
    ppermute x16, starting transfers between devices, exchanged_product(): lax.ppermute(value, 'wide', [(i, i ^ step) for i in range(16) if i // 4 i...  25 us
    ppermute x16, waiting for transfers between devices, exchanged_product(): lax.ppermute(value, 'wide', [(i, i ^ step) for i in range(16) if i // 4 i...  16.9 us
    pallas_call x7, Pallas kernels, work(): pl.pallas_call(functools.partial(work_kernel, parts, depth), out_shape=ou...  13.6 us
    ppermute x1, waiting for transfers between devices, shards(): summed = mine + lax.ppermute(other, 'narrow', [(0, 1), (1, 0)])  1.22 us
  transfers between devices with their start and end apart: 17, of which 8 were waited for; matrix products, arithmetic and copies ran while one was open for 0% of the time, Pallas kernels for 22%

profile of v4, /device:TPU:0, one launch (start us, length us, event | category | flops | bytes accessed | tf_op | source)
XLA Modules:
  0.0 59.4 jit_solution(13675634487183401216)
XLA Ops:
  0.0 1.1 %copy-done = bf16[1,196608]{1,0:T(2,128)(2,1)S(1)} copy-done((bf16[1,196608]{1,0:T(2,128)(2,1)S(1)}, bf16[1,196608]{1,0:T(2,128)(2,1)}, u32[]{:S(2)}) %copy-start) | copy-done | bytes 393240
  1.1 0.7 %transpose_tile.1.refs_2_ = bf16[96,2048]{1,0:T(8,128)(2,1)S(1)} custom-call(bf16[1,196608]{1,0:T(2,128)(2,1)S(1)} %copy-done), custom_call_target="tpu_custom_call" | custom-call | tf_op jit(solution)/shard_map/transpose_tile/pallas_call | solution.py:48
  1.8 3.1 %collective-permute-start.1 = (bf16[96,2048]{1,0:T(8,128)(2,1)S(1)}, bf16[96,2048]{1,0:T(8,128)(2,1)S(1)}, u32[]{:S(2)}, u32[]{:S(2)}) collective-permute-start(bf16[96,2048]{1,0:T(8,128)(2,1)S(1)} %transpose_tile.1.refs_2_), channel_id=1, source_target_pairs={{0,8},{2,10},{4,12},{6,14},{8,0},{10,2},{12,4},{14,6},{16,24},{18,... | collective-permute-start | bytes 1179656 | tf_op jit(solution)/shard_map/ppermute | solution.py:290
  4.9 0.7 %collective-permute-start = (bf16[96,2048]{1,0:T(8,128)(2,1)S(1)}, bf16[96,2048]{1,0:T(8,128)(2,1)S(1)}, u32[]{:S(2)}, u32[]{:S(2)}) collective-permute-start(bf16[96,2048]{1,0:T(8,128)(2,1)S(1)} %transpose_tile.1.refs_2_), channel_id=1, source_target_pairs={{8,16},{10,18},{12,20},{14,22},{16,8},{18,10},{20,12},{22,14},{9,1... | collective-permute-start | bytes 1179656 | tf_op jit(solution)/shard_map/ppermute | solution.py:290
  5.6 1.6 %collective-permute-start.3 = (bf16[96,2048]{1,0:T(8,128)(2,1)S(1)}, bf16[96,2048]{1,0:T(8,128)(2,1)S(1)}, u32[]{:S(2)}, u32[]{:S(2)}) collective-permute-start(bf16[96,2048]{1,0:T(8,128)(2,1)S(1)} %transpose_tile.1.refs_2_), channel_id=1, source_target_pairs={{0,4},{2,6},{4,0},{6,2},{8,12},{10,14},{12,8},{14,10},{16,20},{18,... | collective-permute-start | bytes 1179656 | tf_op jit(solution)/shard_map/ppermute | solution.py:290
  7.2 1.5 %collective-permute-start.4 = (bf16[96,2048]{1,0:T(8,128)(2,1)S(1)}, bf16[96,2048]{1,0:T(8,128)(2,1)S(1)}, u32[]{:S(2)}, u32[]{:S(2)}) collective-permute-start(bf16[96,2048]{1,0:T(8,128)(2,1)S(1)} %transpose_tile.1.refs_2_), channel_id=1, source_target_pairs={{0,2},{2,0},{4,6},{6,4},{8,10},{10,8},{12,14},{14,12},{16,18},{18,... | collective-permute-start | bytes 1179656 | tf_op jit(solution)/shard_map/ppermute | solution.py:290
  8.7 2.2 %work.7 = (bf16[256,8192]{1,0:T(8,128)(2,1)S(1)}, f32[8,128]{1,0:T(8,128)S(1)}) custom-call(f32[8,128]{1,0:T(8,128)S(1)} %broadcast_in_dim.3.mark_ref, bf16[256,32768]{1,0:T(8,128)(2,1)} %refs_0_.5), custom_call_target="tpu_custom_call", output_to_operand_aliasing={{1}: (0, {})} | custom-call | flops 1 | bytes 4000000 | tf_op jit(solution)/shard_map/work/pallas_call | solution.py:188
  10.9 3.1 %collective-permute-done.1.refs_3_ = bf16[96,2048]{1,0:T(8,128)(2,1)S(1)} collective-permute-done((bf16[96,2048]{1,0:T(8,128)(2,1)S(1)}, bf16[96,2048]{1,0:T(8,128)(2,1)S(1)}, u32[]{:S(2)}, u32[]{:S(2)}) %collective-permute-start.1) | collective-permute-done | bytes 393248 | tf_op jit(solution)/shard_map/ppermute | solution.py:290
  14.0 5.7 %collective-permute-start.2 = (bf16[96,2048]{1,0:T(8,128)(2,1)S(1)}, bf16[96,2048]{1,0:T(8,128)(2,1)S(1)}, u32[]{:S(2)}, u32[]{:S(2)}) collective-permute-start(bf16[96,2048]{1,0:T(8,128)(2,1)S(1)} %transpose_tile.1.refs_2_), channel_id=1, source_target_pairs={{0,24},{2,26},{4,28},{6,30},{24,0},{26,2},{28,4},{30,6},{1,25},{3,... | collective-permute-start | bytes 1179656 | tf_op jit(solution)/shard_map/ppermute | solution.py:290
  19.7 1.6 %collective-permute-start.9 = (bf16[96,2048]{1,0:T(8,128)(2,1)S(1)}, bf16[96,2048]{1,0:T(8,128)(2,1)S(1)}, u32[]{:S(2)}, u32[]{:S(2)}) collective-permute-start(bf16[96,2048]{1,0:T(8,128)(2,1)S(1)} %collective-permute-done.3.refs_4_), channel_id=1, source_target_pairs={{0,2},{2,0},{4,6},{6,4},{8,10},{10,8},{12,14},{14,12},{16,18},{18,... | collective-permute-start | bytes 1179656 | tf_op jit(solution)/shard_map/ppermute | solution.py:290
  21.3 1.5 %collective-permute-start.8 = (bf16[96,2048]{1,0:T(8,128)(2,1)S(1)}, bf16[96,2048]{1,0:T(8,128)(2,1)S(1)}, u32[]{:S(2)}, u32[]{:S(2)}) collective-permute-start(bf16[96,2048]{1,0:T(8,128)(2,1)S(1)} %collective-permute-done.1.refs_3_), channel_id=1, source_target_pairs={{0,4},{2,6},{4,0},{6,2},{8,12},{10,14},{12,8},{14,10},{16,20},{18,... | collective-permute-start | bytes 1179656 | tf_op jit(solution)/shard_map/ppermute | solution.py:290
  22.8 3.9 %work.8 = (bf16[256,6144]{1,0:T(8,128)(2,1)S(1)}, bf16[256,6144]{1,0:T(8,128)(2,1)S(1)}, f32[256,96]{1,0:T(8,128)S(1)}, f32[8,128]{1,0:T(8,128)S(1)}) custom-call(f32[8,128]{1,0:T(8,128)S(1)} %mark_step.1.mark_ref, bf16[256,32768]{1,0:T(8,128)(2,1)} %refs_0_.5, bf16[256,8192]{1,0:T(8,128)(2,1)S(1)} %get-tuple-element.81.refs_1_, ...), custom_call_target="tpu_custom_call", output_to_operand_aliasing={{3}: (0, {})} | custom-call | flops 1 | bytes 4000000 | tf_op jit(solution)/shard_map/work/pallas_call | solution.py:188
  26.7 1.3 %collective-permute-done.2.outer_ref = bf16[96,2048]{1,0:T(8,128)(2,1)S(1)} collective-permute-done((bf16[96,2048]{1,0:T(8,128)(2,1)S(1)}, bf16[96,2048]{1,0:T(8,128)(2,1)S(1)}, u32[]{:S(2)}, u32[]{:S(2)}) %collective-permute-start.2) | collective-permute-done | bytes 393248 | tf_op jit(solution)/shard_map/ppermute | solution.py:290
  28.0 1.5 %collective-permute-start.7 = (bf16[96,2048]{1,0:T(8,128)(2,1)S(1)}, bf16[96,2048]{1,0:T(8,128)(2,1)S(1)}, u32[]{:S(2)}, u32[]{:S(2)}) collective-permute-start(bf16[96,2048]{1,0:T(8,128)(2,1)S(1)} %get-tuple-element.84.refs_2_), channel_id=1, source_target_pairs={{0,2},{2,0},{4,6},{6,4},{8,10},{10,8},{12,14},{14,12},{16,18},{18,... | collective-permute-start | bytes 1179656 | tf_op jit(solution)/shard_map/ppermute | solution.py:290
  29.5 1.5 %collective-permute-start.5 = (bf16[96,2048]{1,0:T(8,128)(2,1)S(1)}, bf16[96,2048]{1,0:T(8,128)(2,1)S(1)}, u32[]{:S(2)}, u32[]{:S(2)}) collective-permute-start(bf16[96,2048]{1,0:T(8,128)(2,1)S(1)} %get-tuple-element.84.refs_2_), channel_id=1, source_target_pairs={{0,4},{2,6},{4,0},{6,2},{8,12},{10,14},{12,8},{14,10},{16,20},{18,... | collective-permute-start | bytes 1179656 | tf_op jit(solution)/shard_map/ppermute | solution.py:290
  31.4 3.7 %work.9 = (bf16[256,6144]{1,0:T(8,128)(2,1)S(1)}, bf16[256,4096]{1,0:T(8,128)(2,1)S(1)}, bf16[256,2048]{1,0:T(8,128)(2,1)S(1)}, f32[256,96]{1,0:T(8,128)S(1)}, f32[8,128]{1,0:T(8,128)S(1)}) custom-call(f32[8,128]{1,0:T(8,128)S(1)} %get-tuple-element.93.mark_ref, bf16[256,32768]{1,0:T(8,128)(2,1)} %refs_0_.5, ...), custom_call_target="tpu_custom_call", output_to_operand_aliasing={{4}: (0, {})} | custom-call | flops 1 | bytes 4000000 | tf_op jit(solution)/shard_map/work/pallas_call | solution.py:188
  35.1 2.8 %collective-permute-done.7.refs_5_ = bf16[96,2048]{1,0:T(8,128)(2,1)S(1)} collective-permute-done((bf16[96,2048]{1,0:T(8,128)(2,1)S(1)}, bf16[96,2048]{1,0:T(8,128)(2,1)S(1)}, u32[]{:S(2)}, u32[]{:S(2)}) %collective-permute-start.7) | collective-permute-done | bytes 393248 | tf_op jit(solution)/shard_map/ppermute | solution.py:290
  37.9 1.2 %collective-permute-start.10 = (bf16[96,2048]{1,0:T(8,128)(2,1)S(1)}, bf16[96,2048]{1,0:T(8,128)(2,1)S(1)}, u32[]{:S(2)}, u32[]{:S(2)}) collective-permute-start(bf16[96,2048]{1,0:T(8,128)(2,1)S(1)} %collective-permute-done.7.refs_5_), channel_id=1, source_target_pairs={{0,8},{2,10},{4,12},{6,14},{8,0},{10,2},{12,4},{14,6},{16,24},{18,... | collective-permute-start | bytes 1179656 | tf_op jit(solution)/shard_map/ppermute | solution.py:290
  39.1 1.5 %collective-permute-start.12 = (bf16[96,2048]{1,0:T(8,128)(2,1)S(1)}, bf16[96,2048]{1,0:T(8,128)(2,1)S(1)}, u32[]{:S(2)}, u32[]{:S(2)}) collective-permute-start(bf16[96,2048]{1,0:T(8,128)(2,1)S(1)} %collective-permute-done.1.refs_3_), channel_id=1, source_target_pairs={{0,2},{2,0},{4,6},{6,4},{8,10},{10,8},{12,14},{14,12},{16,18},{18,... | collective-permute-start | bytes 1179656 | tf_op jit(solution)/shard_map/ppermute | solution.py:290
  40.6 0.6 %collective-permute-start.11 = (bf16[96,2048]{1,0:T(8,128)(2,1)S(1)}, bf16[96,2048]{1,0:T(8,128)(2,1)S(1)}, u32[]{:S(2)}, u32[]{:S(2)}) collective-permute-start(bf16[96,2048]{1,0:T(8,128)(2,1)S(1)} %collective-permute-done.6.refs_6_), channel_id=1, source_target_pairs={{0,4},{2,6},{4,0},{6,2},{8,12},{10,14},{12,8},{14,10},{16,20},{18,... | collective-permute-start | bytes 1179656 | tf_op jit(solution)/shard_map/ppermute | solution.py:290
  41.2 1.5 %collective-permute-start.13 = (bf16[96,2048]{1,0:T(8,128)(2,1)S(1)}, bf16[96,2048]{1,0:T(8,128)(2,1)S(1)}, u32[]{:S(2)}, u32[]{:S(2)}) collective-permute-start(bf16[96,2048]{1,0:T(8,128)(2,1)S(1)} %collective-permute-done.5.refs_7_), channel_id=1, source_target_pairs={{0,2},{2,0},{4,6},{6,4},{8,10},{10,8},{12,14},{14,12},{16,18},{18,... | collective-permute-start | bytes 1179656 | tf_op jit(solution)/shard_map/ppermute | solution.py:290
  42.7 1.6 %work.10 = (f32[96,128]{1,0:T(8,128)S(1)}, f32[256,96]{1,0:T(8,128)S(1)}, f32[8,128]{1,0:T(8,128)S(1)}) custom-call(f32[8,128]{1,0:T(8,128)S(1)} %get-tuple-element.101.mark_ref, s32[2,256]{1,0:T(2,128)S(1)} %bitcast.5, s32[2,96]{1,0:T(2,128)S(1)} %bitcast.7, s32[4,128]{1,0:T(4,128)S(1)} %bitcast.6, ...), custom_call_target="tpu_custom_call", output_to_operand_aliasing={{2}: (0, {})} | custom-call | flops 1 | bytes 4000000 | tf_op jit(solution)/shard_map/work/pallas_call | solution.py:188
  44.3 2.9 %collective-permute-done.10.refs_1_ = bf16[96,2048]{1,0:T(8,128)(2,1)S(1)} collective-permute-done((bf16[96,2048]{1,0:T(8,128)(2,1)S(1)}, bf16[96,2048]{1,0:T(8,128)(2,1)S(1)}, u32[]{:S(2)}, u32[]{:S(2)}) %collective-permute-start.10) | collective-permute-done | bytes 393248 | tf_op jit(solution)/shard_map/ppermute | solution.py:290
  47.2 0.9 %collective-permute-start.14 = (bf16[96,2048]{1,0:T(8,128)(2,1)S(1)}, bf16[96,2048]{1,0:T(8,128)(2,1)S(1)}, u32[]{:S(2)}, u32[]{:S(2)}) collective-permute-start(bf16[96,2048]{1,0:T(8,128)(2,1)S(1)} %collective-permute-done.9.refs_4_), channel_id=1, source_target_pairs={{0,8},{2,10},{4,12},{6,14},{8,0},{10,2},{12,4},{14,6},{16,24},{18,... | collective-permute-start | bytes 1179656 | tf_op jit(solution)/shard_map/ppermute | solution.py:290
  48.1 0.8 %collective-permute-start.15 = (bf16[96,2048]{1,0:T(8,128)(2,1)S(1)}, bf16[96,2048]{1,0:T(8,128)(2,1)S(1)}, u32[]{:S(2)}, u32[]{:S(2)}) collective-permute-start(bf16[96,2048]{1,0:T(8,128)(2,1)S(1)} %collective-permute-done.10.refs_1_), channel_id=1, source_target_pairs={{0,4},{2,6},{4,0},{6,2},{8,12},{10,14},{12,8},{14,10},{16,20},{18,... | collective-permute-start | bytes 1179656 | tf_op jit(solution)/shard_map/ppermute | solution.py:290
  48.9 2.2 %collective-permute-done.12.refs_3_ = bf16[96,2048]{1,0:T(8,128)(2,1)S(1)} collective-permute-done((bf16[96,2048]{1,0:T(8,128)(2,1)S(1)}, bf16[96,2048]{1,0:T(8,128)(2,1)S(1)}, u32[]{:S(2)}, u32[]{:S(2)}) %collective-permute-start.12) | collective-permute-done | bytes 393248 | tf_op jit(solution)/shard_map/ppermute | solution.py:290
  51.2 1.0 %work.11 = (f32[256,96]{1,0:T(8,128)S(1)}, f32[8,128]{1,0:T(8,128)S(1)}) custom-call(f32[8,128]{1,0:T(8,128)S(1)} %get-tuple-element.111.mark_ref, bf16[256,6144]{1,0:T(8,128)(2,1)S(1)} %get-tuple-element.112.refs_0_, bf16[96,2048]{1,0:T(8,128)(2,1)S(1)} %collective-permute-done.10.refs_1_, ...), custom_call_target="tpu_custom_call", output_to_operand_aliasing={{1}: (0, {})} | custom-call | flops 1 | bytes 4000000 | tf_op jit(solution)/shard_map/work/pallas_call | solution.py:188
  52.2 4.1 %collective-permute-done.13.refs_1_ = bf16[96,2048]{1,0:T(8,128)(2,1)S(1)} collective-permute-done((bf16[96,2048]{1,0:T(8,128)(2,1)S(1)}, bf16[96,2048]{1,0:T(8,128)(2,1)S(1)}, u32[]{:S(2)}, u32[]{:S(2)}) %collective-permute-start.13) | collective-permute-done | bytes 393248 | tf_op jit(solution)/shard_map/ppermute | solution.py:290
  56.2 0.7 %work.12 = (f32[256,96]{1,0:T(8,128)S(1)}, f32[8,128]{1,0:T(8,128)S(1)}) custom-call(f32[8,128]{1,0:T(8,128)S(1)} %get-tuple-element.117.mark_ref, bf16[256,4096]{1,0:T(8,128)(2,1)S(1)} %get-tuple-element.118.refs_0_, bf16[96,2048]{1,0:T(8,128)(2,1)S(1)} %collective-permute-done.13.refs_1_, ...), custom_call_target="tpu_custom_call", output_to_operand_aliasing={{1}: (0, {})} | custom-call | flops 1 | bytes 4000000 | tf_op jit(solution)/shard_map/work/pallas_call | solution.py:188
  57.0 0.5 work.13
  57.6 1.2 %collective-permute-done.16 = f32[96,128]{1,0:T(8,128)S(1)} collective-permute-done((f32[96,128]{1,0:T(8,128)S(1)}, f32[96,128]{1,0:T(8,128)S(1)}, u32[]{:S(2)}, u32[]{:S(2)}) %collective-permute-start.16) | collective-permute-done | bytes 49184 | tf_op jit(solution)/shard_map/ppermute | solution.py:314
  58.8 0.6 %select_bitcast_fusion = f32[128,96]{0,1:T(8,128)} fusion(f32[96,128]{1,0:T(8,128)S(1)} %get-tuple-element.125, f32[96,128]{1,0:T(8,128)S(1)} %collective-permute-done.16, f32[96,128]{1,0:T(8,128)S(1)} %get-tuple-element.104), kind=kLoop, calls=%fused_computation | loop fusion | flops 36864 | bytes 196608 | tf_op jit(solution)/shard_map/transpose | solution.py:315
  (24 shorter events, 0.5 us)
Async XLA Ops:
  0.0 1.1 %copy-start = (bf16[1,196608]{1,0:T(2,128)(2,1)S(1)}, bf16[1,196608]{1,0:T(2,128)(2,1)}, u32[]{:S(2)}) copy-start(bf16[1,196608]{1,0:T(2,128)(2,1)} %tile_ref.1) | copy-start | bytes 1179652
  1.8 12.2 %collective-permute-start.1 = (bf16[96,2048]{1,0:T(8,128)(2,1)S(1)}, bf16[96,2048]{1,0:T(8,128)(2,1)S(1)}, u32[]{:S(2)}, u32[]{:S(2)}) collective-permute-start(bf16[96,2048]{1,0:T(8,128)(2,1)S(1)} %transpose_tile.1.refs_2_), channel_id=1, source_target_pairs={{0,8},{2,10},{4,12},{6,14},{8,0},{10,2},{12,4},{14,6},{16,24},{18,... | collective-permute-start | bytes 1179656 | tf_op jit(solution)/shard_map/ppermute | solution.py:290
  4.9 9.1 %collective-permute-start = (bf16[96,2048]{1,0:T(8,128)(2,1)S(1)}, bf16[96,2048]{1,0:T(8,128)(2,1)S(1)}, u32[]{:S(2)}, u32[]{:S(2)}) collective-permute-start(bf16[96,2048]{1,0:T(8,128)(2,1)S(1)} %transpose_tile.1.refs_2_), channel_id=1, source_target_pairs={{8,16},{10,18},{12,20},{14,22},{16,8},{18,10},{20,12},{22,14},{9,1... | collective-permute-start | bytes 1179656 | tf_op jit(solution)/shard_map/ppermute | solution.py:290
  5.6 14.1 %collective-permute-start.3 = (bf16[96,2048]{1,0:T(8,128)(2,1)S(1)}, bf16[96,2048]{1,0:T(8,128)(2,1)S(1)}, u32[]{:S(2)}, u32[]{:S(2)}) collective-permute-start(bf16[96,2048]{1,0:T(8,128)(2,1)S(1)} %transpose_tile.1.refs_2_), channel_id=1, source_target_pairs={{0,4},{2,6},{4,0},{6,2},{8,12},{10,14},{12,8},{14,10},{16,20},{18,... | collective-permute-start | bytes 1179656 | tf_op jit(solution)/shard_map/ppermute | solution.py:290
  7.2 12.5 %collective-permute-start.4 = (bf16[96,2048]{1,0:T(8,128)(2,1)S(1)}, bf16[96,2048]{1,0:T(8,128)(2,1)S(1)}, u32[]{:S(2)}, u32[]{:S(2)}) collective-permute-start(bf16[96,2048]{1,0:T(8,128)(2,1)S(1)} %transpose_tile.1.refs_2_), channel_id=1, source_target_pairs={{0,2},{2,0},{4,6},{6,4},{8,10},{10,8},{12,14},{14,12},{16,18},{18,... | collective-permute-start | bytes 1179656 | tf_op jit(solution)/shard_map/ppermute | solution.py:290
  14.0 14.0 %collective-permute-start.2 = (bf16[96,2048]{1,0:T(8,128)(2,1)S(1)}, bf16[96,2048]{1,0:T(8,128)(2,1)S(1)}, u32[]{:S(2)}, u32[]{:S(2)}) collective-permute-start(bf16[96,2048]{1,0:T(8,128)(2,1)S(1)} %transpose_tile.1.refs_2_), channel_id=1, source_target_pairs={{0,24},{2,26},{4,28},{6,30},{24,0},{26,2},{28,4},{30,6},{1,25},{3,... | collective-permute-start | bytes 1179656 | tf_op jit(solution)/shard_map/ppermute | solution.py:290
  19.7 11.3 %collective-permute-start.9 = (bf16[96,2048]{1,0:T(8,128)(2,1)S(1)}, bf16[96,2048]{1,0:T(8,128)(2,1)S(1)}, u32[]{:S(2)}, u32[]{:S(2)}) collective-permute-start(bf16[96,2048]{1,0:T(8,128)(2,1)S(1)} %collective-permute-done.3.refs_4_), channel_id=1, source_target_pairs={{0,2},{2,0},{4,6},{6,4},{8,10},{10,8},{12,14},{14,12},{16,18},{18,... | collective-permute-start | bytes 1179656 | tf_op jit(solution)/shard_map/ppermute | solution.py:290
  21.3 10.1 %collective-permute-start.8 = (bf16[96,2048]{1,0:T(8,128)(2,1)S(1)}, bf16[96,2048]{1,0:T(8,128)(2,1)S(1)}, u32[]{:S(2)}, u32[]{:S(2)}) collective-permute-start(bf16[96,2048]{1,0:T(8,128)(2,1)S(1)} %collective-permute-done.1.refs_3_), channel_id=1, source_target_pairs={{0,4},{2,6},{4,0},{6,2},{8,12},{10,14},{12,8},{14,10},{16,20},{18,... | collective-permute-start | bytes 1179656 | tf_op jit(solution)/shard_map/ppermute | solution.py:290
  28.0 9.9 %collective-permute-start.7 = (bf16[96,2048]{1,0:T(8,128)(2,1)S(1)}, bf16[96,2048]{1,0:T(8,128)(2,1)S(1)}, u32[]{:S(2)}, u32[]{:S(2)}) collective-permute-start(bf16[96,2048]{1,0:T(8,128)(2,1)S(1)} %get-tuple-element.84.refs_2_), channel_id=1, source_target_pairs={{0,2},{2,0},{4,6},{6,4},{8,10},{10,8},{12,14},{14,12},{16,18},{18,... | collective-permute-start | bytes 1179656 | tf_op jit(solution)/shard_map/ppermute | solution.py:290
  29.5 9.6 %collective-permute-start.6 = (bf16[96,2048]{1,0:T(8,128)(2,1)S(1)}, bf16[96,2048]{1,0:T(8,128)(2,1)S(1)}, u32[]{:S(2)}, u32[]{:S(2)}) collective-permute-start(bf16[96,2048]{1,0:T(8,128)(2,1)S(1)} %get-tuple-element.84.refs_2_), channel_id=1, source_target_pairs={{0,8},{2,10},{4,12},{6,14},{8,0},{10,2},{12,4},{14,6},{16,24},{18,... | collective-permute-start | bytes 1179656 | tf_op jit(solution)/shard_map/ppermute | solution.py:290
  29.5 9.6 %collective-permute-start.5 = (bf16[96,2048]{1,0:T(8,128)(2,1)S(1)}, bf16[96,2048]{1,0:T(8,128)(2,1)S(1)}, u32[]{:S(2)}, u32[]{:S(2)}) collective-permute-start(bf16[96,2048]{1,0:T(8,128)(2,1)S(1)} %get-tuple-element.84.refs_2_), channel_id=1, source_target_pairs={{0,4},{2,6},{4,0},{6,2},{8,12},{10,14},{12,8},{14,10},{16,20},{18,... | collective-permute-start | bytes 1179656 | tf_op jit(solution)/shard_map/ppermute | solution.py:290
  31.4 11.3 %copy-start.1 = (s32[256,2]{0,1:T(2,128)S(1)}, s32[256,2]{0,1:T(2,128)}, u32[]{:S(2)}) copy-start(s32[256,2]{0,1:T(2,128)} %param.8) | copy-start | bytes 6148
  31.4 11.3 %copy-start.2 = (s32[512]{0:T(512)S(1)}, s32[512]{0:T(512)}, u32[]{:S(2)}) copy-start(s32[512]{0:T(512)} %param.9) | copy-start | bytes 6148
  31.4 11.3 %copy-start.3 = (s32[96,2]{0,1:T(2,128)S(1)}, s32[96,2]{0,1:T(2,128)}, u32[]{:S(2)}) copy-start(s32[96,2]{0,1:T(2,128)} %param.10) | copy-start | bytes 2308
  31.4 11.3 %copy-start.4 = (s32[16]{0:T(128)S(1)}, s32[16]{0:T(128)}, u32[]{:S(2)}) copy-start(s32[16]{0:T(128)} %refs_3_.1) | copy-start | bytes 196
  37.9 9.3 %collective-permute-start.10 = (bf16[96,2048]{1,0:T(8,128)(2,1)S(1)}, bf16[96,2048]{1,0:T(8,128)(2,1)S(1)}, u32[]{:S(2)}, u32[]{:S(2)}) collective-permute-start(bf16[96,2048]{1,0:T(8,128)(2,1)S(1)} %collective-permute-done.7.refs_5_), channel_id=1, source_target_pairs={{0,8},{2,10},{4,12},{6,14},{8,0},{10,2},{12,4},{14,6},{16,24},{18,... | collective-permute-start | bytes 1179656 | tf_op jit(solution)/shard_map/ppermute | solution.py:290
  39.1 12.1 %collective-permute-start.12 = (bf16[96,2048]{1,0:T(8,128)(2,1)S(1)}, bf16[96,2048]{1,0:T(8,128)(2,1)S(1)}, u32[]{:S(2)}, u32[]{:S(2)}) collective-permute-start(bf16[96,2048]{1,0:T(8,128)(2,1)S(1)} %collective-permute-done.1.refs_3_), channel_id=1, source_target_pairs={{0,2},{2,0},{4,6},{6,4},{8,10},{10,8},{12,14},{14,12},{16,18},{18,... | collective-permute-start | bytes 1179656 | tf_op jit(solution)/shard_map/ppermute | solution.py:290
  40.6 10.6 %collective-permute-start.11 = (bf16[96,2048]{1,0:T(8,128)(2,1)S(1)}, bf16[96,2048]{1,0:T(8,128)(2,1)S(1)}, u32[]{:S(2)}, u32[]{:S(2)}) collective-permute-start(bf16[96,2048]{1,0:T(8,128)(2,1)S(1)} %collective-permute-done.6.refs_6_), channel_id=1, source_target_pairs={{0,4},{2,6},{4,0},{6,2},{8,12},{10,14},{12,8},{14,10},{16,20},{18,... | collective-permute-start | bytes 1179656 | tf_op jit(solution)/shard_map/ppermute | solution.py:290
  41.2 15.1 %collective-permute-start.13 = (bf16[96,2048]{1,0:T(8,128)(2,1)S(1)}, bf16[96,2048]{1,0:T(8,128)(2,1)S(1)}, u32[]{:S(2)}, u32[]{:S(2)}) collective-permute-start(bf16[96,2048]{1,0:T(8,128)(2,1)S(1)} %collective-permute-done.5.refs_7_), channel_id=1, source_target_pairs={{0,2},{2,0},{4,6},{6,4},{8,10},{10,8},{12,14},{14,12},{16,18},{18,... | collective-permute-start | bytes 1179656 | tf_op jit(solution)/shard_map/ppermute | solution.py:290
  47.2 9.0 %collective-permute-start.14 = (bf16[96,2048]{1,0:T(8,128)(2,1)S(1)}, bf16[96,2048]{1,0:T(8,128)(2,1)S(1)}, u32[]{:S(2)}, u32[]{:S(2)}) collective-permute-start(bf16[96,2048]{1,0:T(8,128)(2,1)S(1)} %collective-permute-done.9.refs_4_), channel_id=1, source_target_pairs={{0,8},{2,10},{4,12},{6,14},{8,0},{10,2},{12,4},{14,6},{16,24},{18,... | collective-permute-start | bytes 1179656 | tf_op jit(solution)/shard_map/ppermute | solution.py:290
  48.1 8.8 %collective-permute-start.15 = (bf16[96,2048]{1,0:T(8,128)(2,1)S(1)}, bf16[96,2048]{1,0:T(8,128)(2,1)S(1)}, u32[]{:S(2)}, u32[]{:S(2)}) collective-permute-start(bf16[96,2048]{1,0:T(8,128)(2,1)S(1)} %collective-permute-done.10.refs_1_), channel_id=1, source_target_pairs={{0,4},{2,6},{4,0},{6,2},{8,12},{10,14},{12,8},{14,10},{16,20},{18,... | collective-permute-start | bytes 1179656 | tf_op jit(solution)/shard_map/ppermute | solution.py:290
  57.5 1.3 %collective-permute-start.16 = (f32[96,128]{1,0:T(8,128)S(1)}, f32[96,128]{1,0:T(8,128)S(1)}, u32[]{:S(2)}, u32[]{:S(2)}) collective-permute-start(f32[96,128]{1,0:T(8,128)S(1)} %get-tuple-element.126), channel_id=1, source_target_pairs={{0,1},{1,0},{2,3},{3,2},{4,5},{5,4},{6,7},{7,6},{8,9},{9,8},{10,11... | collective-permute-start | bytes 147464 | tf_op jit(solution)/shard_map/ppermute | solution.py:314

commit v5 on v4

--- a/solution.py
+++ b/solution.py
@@ -17,7 +17,7 @@
     ("C2", Z3, "O", OUTER), ("YA", Y, "A"), ("YO",), ("DO", X, "YO"), ("XO",), MULTIPLY, ("C2",), (PICK, "C"),
     ("XC", X, "C"), ("B", Z1, "C"), ("YC", Y, "C"), ("YA",), ("DO",), MULTIPLY, ("XC",), ("XB", Z1, "XC"), ("B",),
     ("YB", Y, "B"), ("YC",), ("XA", X, "A"), ("DC", X, "YC"), MULTIPLY, ("XB",), ("DB", Y, "XB"), ("DA", Z1, "DO"),
-    ("YB",), ("XA",), MULTIPLY, ("DC",), ("DA",), MULTIPLY, ("DB",),
+    ("YB",), STEP, ("XA",), MULTIPLY, ("DB",), ("DA",), MULTIPLY, ("DC",),
 )
 LOADS = {0: (1, 3), 1: (3, None)}
 KEEP_AT = 2

time: 59.6 us -> 59.4 us (level)
  transfers between devices with their start and end apart: 17 -> 17, of which waited for: 8 -> 9; matrix products, arithmetic and copies ran while one was open for 0% -> 0% of each run, Pallas kernels for 22% -> 22%
where the time goes in v5:
time: 59.4 us; the launch traced here: 59.2 us
  starting transfers between devices  25.1 us (42%)
  waiting for transfers between devices  17.9 us (30%)
  Pallas kernels  14.3 us (24%)
  local copies, waits for them, and re-layouts  1.15 us (2%)
  other arithmetic  0.63 us (1%)
    ppermute x16, starting transfers between devices, exchanged_product(): lax.ppermute(value, 'wide', [(i, i ^ step) for i in range(16) if i // 4 i...  25 us
    ppermute x16, waiting for transfers between devices, exchanged_product(): lax.ppermute(value, 'wide', [(i, i ^ step) for i in range(16) if i // 4 i...  16.7 us
    pallas_call x7, Pallas kernels, work(): pl.pallas_call(functools.partial(work_kernel, parts, depth), out_shape=ou...  13.5 us
    ppermute x1, waiting for transfers between devices, shards(): summed = mine + lax.ppermute(other, 'narrow', [(0, 1), (1, 0)])  1.22 us
  transfers between devices with their start and end apart: 17, of which 9 were waited for; matrix products, arithmetic and copies ran while one was open for 0% of the time, Pallas kernels for 22%

profile of v5, /device:TPU:0, one launch (start us, length us, event | category | flops | bytes accessed | tf_op | source)
XLA Modules:
  0.0 59.2 jit_solution(15838996582128729463)
XLA Ops:
  0.0 1.1 %copy-done = bf16[1,196608]{1,0:T(2,128)(2,1)S(1)} copy-done((bf16[1,196608]{1,0:T(2,128)(2,1)S(1)}, bf16[1,196608]{1,0:T(2,128)(2,1)}, u32[]{:S(2)}) %copy-start) | copy-done | bytes 393240
  1.1 0.7 %transpose_tile.1.refs_2_ = bf16[96,2048]{1,0:T(8,128)(2,1)S(1)} custom-call(bf16[1,196608]{1,0:T(2,128)(2,1)S(1)} %copy-done), custom_call_target="tpu_custom_call" | custom-call | tf_op jit(solution)/shard_map/transpose_tile/pallas_call | solution.py:48
  1.8 3.1 %collective-permute-start.1 = (bf16[96,2048]{1,0:T(8,128)(2,1)S(1)}, bf16[96,2048]{1,0:T(8,128)(2,1)S(1)}, u32[]{:S(2)}, u32[]{:S(2)}) collective-permute-start(bf16[96,2048]{1,0:T(8,128)(2,1)S(1)} %transpose_tile.1.refs_2_), channel_id=1, source_target_pairs={{0,8},{2,10},{4,12},{6,14},{8,0},{10,2},{12,4},{14,6},{16,24},{18,... | collective-permute-start | bytes 1179656 | tf_op jit(solution)/shard_map/ppermute | solution.py:290
  4.9 0.7 %collective-permute-start = (bf16[96,2048]{1,0:T(8,128)(2,1)S(1)}, bf16[96,2048]{1,0:T(8,128)(2,1)S(1)}, u32[]{:S(2)}, u32[]{:S(2)}) collective-permute-start(bf16[96,2048]{1,0:T(8,128)(2,1)S(1)} %transpose_tile.1.refs_2_), channel_id=1, source_target_pairs={{8,16},{10,18},{12,20},{14,22},{16,8},{18,10},{20,12},{22,14},{9,1... | collective-permute-start | bytes 1179656 | tf_op jit(solution)/shard_map/ppermute | solution.py:290
  5.6 1.6 %collective-permute-start.3 = (bf16[96,2048]{1,0:T(8,128)(2,1)S(1)}, bf16[96,2048]{1,0:T(8,128)(2,1)S(1)}, u32[]{:S(2)}, u32[]{:S(2)}) collective-permute-start(bf16[96,2048]{1,0:T(8,128)(2,1)S(1)} %transpose_tile.1.refs_2_), channel_id=1, source_target_pairs={{0,4},{2,6},{4,0},{6,2},{8,12},{10,14},{12,8},{14,10},{16,20},{18,... | collective-permute-start | bytes 1179656 | tf_op jit(solution)/shard_map/ppermute | solution.py:290
  7.2 1.5 %collective-permute-start.4 = (bf16[96,2048]{1,0:T(8,128)(2,1)S(1)}, bf16[96,2048]{1,0:T(8,128)(2,1)S(1)}, u32[]{:S(2)}, u32[]{:S(2)}) collective-permute-start(bf16[96,2048]{1,0:T(8,128)(2,1)S(1)} %transpose_tile.1.refs_2_), channel_id=1, source_target_pairs={{0,2},{2,0},{4,6},{6,4},{8,10},{10,8},{12,14},{14,12},{16,18},{18,... | collective-permute-start | bytes 1179656 | tf_op jit(solution)/shard_map/ppermute | solution.py:290
  8.7 2.2 %work.7 = (bf16[256,8192]{1,0:T(8,128)(2,1)S(1)}, f32[8,128]{1,0:T(8,128)S(1)}) custom-call(f32[8,128]{1,0:T(8,128)S(1)} %broadcast_in_dim.3.mark_ref, bf16[256,32768]{1,0:T(8,128)(2,1)} %refs_0_.5), custom_call_target="tpu_custom_call", output_to_operand_aliasing={{1}: (0, {})} | custom-call | flops 1 | bytes 4000000 | tf_op jit(solution)/shard_map/work/pallas_call | solution.py:188
  10.9 3.1 %collective-permute-done.1.refs_3_ = bf16[96,2048]{1,0:T(8,128)(2,1)S(1)} collective-permute-done((bf16[96,2048]{1,0:T(8,128)(2,1)S(1)}, bf16[96,2048]{1,0:T(8,128)(2,1)S(1)}, u32[]{:S(2)}, u32[]{:S(2)}) %collective-permute-start.1) | collective-permute-done | bytes 393248 | tf_op jit(solution)/shard_map/ppermute | solution.py:290
  14.0 5.7 %collective-permute-start.2 = (bf16[96,2048]{1,0:T(8,128)(2,1)S(1)}, bf16[96,2048]{1,0:T(8,128)(2,1)S(1)}, u32[]{:S(2)}, u32[]{:S(2)}) collective-permute-start(bf16[96,2048]{1,0:T(8,128)(2,1)S(1)} %transpose_tile.1.refs_2_), channel_id=1, source_target_pairs={{0,24},{2,26},{4,28},{6,30},{24,0},{26,2},{28,4},{30,6},{1,25},{3,... | collective-permute-start | bytes 1179656 | tf_op jit(solution)/shard_map/ppermute | solution.py:290
  19.7 1.6 %collective-permute-start.9 = (bf16[96,2048]{1,0:T(8,128)(2,1)S(1)}, bf16[96,2048]{1,0:T(8,128)(2,1)S(1)}, u32[]{:S(2)}, u32[]{:S(2)}) collective-permute-start(bf16[96,2048]{1,0:T(8,128)(2,1)S(1)} %collective-permute-done.3.refs_4_), channel_id=1, source_target_pairs={{0,2},{2,0},{4,6},{6,4},{8,10},{10,8},{12,14},{14,12},{16,18},{18,... | collective-permute-start | bytes 1179656 | tf_op jit(solution)/shard_map/ppermute | solution.py:290
  21.3 1.5 %collective-permute-start.8 = (bf16[96,2048]{1,0:T(8,128)(2,1)S(1)}, bf16[96,2048]{1,0:T(8,128)(2,1)S(1)}, u32[]{:S(2)}, u32[]{:S(2)}) collective-permute-start(bf16[96,2048]{1,0:T(8,128)(2,1)S(1)} %collective-permute-done.1.refs_3_), channel_id=1, source_target_pairs={{0,4},{2,6},{4,0},{6,2},{8,12},{10,14},{12,8},{14,10},{16,20},{18,... | collective-permute-start | bytes 1179656 | tf_op jit(solution)/shard_map/ppermute | solution.py:290
  22.8 3.9 %work.8 = (bf16[256,6144]{1,0:T(8,128)(2,1)S(1)}, bf16[256,6144]{1,0:T(8,128)(2,1)S(1)}, f32[256,96]{1,0:T(8,128)S(1)}, f32[8,128]{1,0:T(8,128)S(1)}) custom-call(f32[8,128]{1,0:T(8,128)S(1)} %mark_step.2.mark_ref, bf16[256,32768]{1,0:T(8,128)(2,1)} %refs_0_.5, bf16[256,8192]{1,0:T(8,128)(2,1)S(1)} %get-tuple-element.82.refs_1_, ...), custom_call_target="tpu_custom_call", output_to_operand_aliasing={{3}: (0, {})} | custom-call | flops 1 | bytes 4000000 | tf_op jit(solution)/shard_map/work/pallas_call | solution.py:188
  26.7 1.3 %collective-permute-done.2.outer_ref = bf16[96,2048]{1,0:T(8,128)(2,1)S(1)} collective-permute-done((bf16[96,2048]{1,0:T(8,128)(2,1)S(1)}, bf16[96,2048]{1,0:T(8,128)(2,1)S(1)}, u32[]{:S(2)}, u32[]{:S(2)}) %collective-permute-start.2) | collective-permute-done | bytes 393248 | tf_op jit(solution)/shard_map/ppermute | solution.py:290
  28.0 1.5 %collective-permute-start.7 = (bf16[96,2048]{1,0:T(8,128)(2,1)S(1)}, bf16[96,2048]{1,0:T(8,128)(2,1)S(1)}, u32[]{:S(2)}, u32[]{:S(2)}) collective-permute-start(bf16[96,2048]{1,0:T(8,128)(2,1)S(1)} %get-tuple-element.85.refs_2_), channel_id=1, source_target_pairs={{0,2},{2,0},{4,6},{6,4},{8,10},{10,8},{12,14},{14,12},{16,18},{18,... | collective-permute-start | bytes 1179656 | tf_op jit(solution)/shard_map/ppermute | solution.py:290
  29.5 1.5 %collective-permute-start.5 = (bf16[96,2048]{1,0:T(8,128)(2,1)S(1)}, bf16[96,2048]{1,0:T(8,128)(2,1)S(1)}, u32[]{:S(2)}, u32[]{:S(2)}) collective-permute-start(bf16[96,2048]{1,0:T(8,128)(2,1)S(1)} %get-tuple-element.85.refs_2_), channel_id=1, source_target_pairs={{0,4},{2,6},{4,0},{6,2},{8,12},{10,14},{12,8},{14,10},{16,20},{18,... | collective-permute-start | bytes 1179656 | tf_op jit(solution)/shard_map/ppermute | solution.py:290
  31.4 3.7 %work.9 = (bf16[256,6144]{1,0:T(8,128)(2,1)S(1)}, bf16[256,4096]{1,0:T(8,128)(2,1)S(1)}, bf16[256,2048]{1,0:T(8,128)(2,1)S(1)}, f32[256,96]{1,0:T(8,128)S(1)}, f32[8,128]{1,0:T(8,128)S(1)}) custom-call(f32[8,128]{1,0:T(8,128)S(1)} %get-tuple-element.94.mark_ref, bf16[256,32768]{1,0:T(8,128)(2,1)} %refs_0_.5, ...), custom_call_target="tpu_custom_call", output_to_operand_aliasing={{4}: (0, {})} | custom-call | flops 1 | bytes 4000000 | tf_op jit(solution)/shard_map/work/pallas_call | solution.py:188
  35.1 2.8 %collective-permute-done.7.refs_5_ = bf16[96,2048]{1,0:T(8,128)(2,1)S(1)} collective-permute-done((bf16[96,2048]{1,0:T(8,128)(2,1)S(1)}, bf16[96,2048]{1,0:T(8,128)(2,1)S(1)}, u32[]{:S(2)}, u32[]{:S(2)}) %collective-permute-start.7) | collective-permute-done | bytes 393248 | tf_op jit(solution)/shard_map/ppermute | solution.py:290
  37.9 1.2 %collective-permute-start.10 = (bf16[96,2048]{1,0:T(8,128)(2,1)S(1)}, bf16[96,2048]{1,0:T(8,128)(2,1)S(1)}, u32[]{:S(2)}, u32[]{:S(2)}) collective-permute-start(bf16[96,2048]{1,0:T(8,128)(2,1)S(1)} %collective-permute-done.7.refs_5_), channel_id=1, source_target_pairs={{0,8},{2,10},{4,12},{6,14},{8,0},{10,2},{12,4},{14,6},{16,24},{18,... | collective-permute-start | bytes 1179656 | tf_op jit(solution)/shard_map/ppermute | solution.py:290
  39.1 0.8 %collective-permute-start.11 = (bf16[96,2048]{1,0:T(8,128)(2,1)S(1)}, bf16[96,2048]{1,0:T(8,128)(2,1)S(1)}, u32[]{:S(2)}, u32[]{:S(2)}) collective-permute-start(bf16[96,2048]{1,0:T(8,128)(2,1)S(1)} %collective-permute-done.6.refs_6_), channel_id=1, source_target_pairs={{0,4},{2,6},{4,0},{6,2},{8,12},{10,14},{12,8},{14,10},{16,20},{18,... | collective-permute-start | bytes 1179656 | tf_op jit(solution)/shard_map/ppermute | solution.py:290
  39.9 1.3 %collective-permute-start.12 = (bf16[96,2048]{1,0:T(8,128)(2,1)S(1)}, bf16[96,2048]{1,0:T(8,128)(2,1)S(1)}, u32[]{:S(2)}, u32[]{:S(2)}) collective-permute-start(bf16[96,2048]{1,0:T(8,128)(2,1)S(1)} %collective-permute-done.1.refs_3_), channel_id=1, source_target_pairs={{0,2},{2,0},{4,6},{6,4},{8,10},{10,8},{12,14},{14,12},{16,18},{18,... | collective-permute-start | bytes 1179656 | tf_op jit(solution)/shard_map/ppermute | solution.py:290
  41.2 1.6 %work.10 = (f32[96,128]{1,0:T(8,128)S(1)}, f32[256,96]{1,0:T(8,128)S(1)}, f32[8,128]{1,0:T(8,128)S(1)}) custom-call(f32[8,128]{1,0:T(8,128)S(1)} %get-tuple-element.102.mark_ref, s32[2,256]{1,0:T(2,128)S(1)} %bitcast.5, s32[2,96]{1,0:T(2,128)S(1)} %bitcast.7, s32[4,128]{1,0:T(4,128)S(1)} %bitcast.6, ...), custom_call_target="tpu_custom_call", output_to_operand_aliasing={{2}: (0, {})} | custom-call | flops 1 | bytes 4000000 | tf_op jit(solution)/shard_map/work/pallas_call | solution.py:188
  42.7 4.5 %collective-permute-done.10.refs_1_ = bf16[96,2048]{1,0:T(8,128)(2,1)S(1)} collective-permute-done((bf16[96,2048]{1,0:T(8,128)(2,1)S(1)}, bf16[96,2048]{1,0:T(8,128)(2,1)S(1)}, u32[]{:S(2)}, u32[]{:S(2)}) %collective-permute-start.10) | collective-permute-done | bytes 393248 | tf_op jit(solution)/shard_map/ppermute | solution.py:290
  47.2 0.9 %collective-permute-start.14 = (bf16[96,2048]{1,0:T(8,128)(2,1)S(1)}, bf16[96,2048]{1,0:T(8,128)(2,1)S(1)}, u32[]{:S(2)}, u32[]{:S(2)}) collective-permute-start(bf16[96,2048]{1,0:T(8,128)(2,1)S(1)} %collective-permute-done.9.refs_4_), channel_id=1, source_target_pairs={{0,8},{2,10},{4,12},{6,14},{8,0},{10,2},{12,4},{14,6},{16,24},{18,... | collective-permute-start | bytes 1179656 | tf_op jit(solution)/shard_map/ppermute | solution.py:290
  48.1 0.8 %collective-permute-start.13 = (bf16[96,2048]{1,0:T(8,128)(2,1)S(1)}, bf16[96,2048]{1,0:T(8,128)(2,1)S(1)}, u32[]{:S(2)}, u32[]{:S(2)}) collective-permute-start(bf16[96,2048]{1,0:T(8,128)(2,1)S(1)} %collective-permute-done.10.refs_1_), channel_id=1, source_target_pairs={{0,4},{2,6},{4,0},{6,2},{8,12},{10,14},{12,8},{14,10},{16,20},{18,... | collective-permute-start | bytes 1179656 | tf_op jit(solution)/shard_map/ppermute | solution.py:290
  48.9 1.5 %collective-permute-start.15 = (bf16[96,2048]{1,0:T(8,128)(2,1)S(1)}, bf16[96,2048]{1,0:T(8,128)(2,1)S(1)}, u32[]{:S(2)}, u32[]{:S(2)}) collective-permute-start(bf16[96,2048]{1,0:T(8,128)(2,1)S(1)} %collective-permute-done.5.refs_7_), channel_id=1, source_target_pairs={{0,2},{2,0},{4,6},{6,4},{8,10},{10,8},{12,14},{14,12},{16,18},{18,... | collective-permute-start | bytes 1179656 | tf_op jit(solution)/shard_map/ppermute | solution.py:290
  50.4 1.0 %work.11 = (f32[256,96]{1,0:T(8,128)S(1)}, f32[8,128]{1,0:T(8,128)S(1)}) custom-call(f32[8,128]{1,0:T(8,128)S(1)} %mark_step.3.mark_ref, bf16[256,6144]{1,0:T(8,128)(2,1)S(1)} %get-tuple-element.114.refs_0_, bf16[96,2048]{1,0:T(8,128)(2,1)S(1)} %collective-permute-done.10.refs_1_, ...), custom_call_target="tpu_custom_call", output_to_operand_aliasing={{1}: (0, {})} | custom-call | flops 1 | bytes 4000000 | tf_op jit(solution)/shard_map/work/pallas_call | solution.py:188
  51.4 3.8 %collective-permute-done.14.refs_2_ = bf16[96,2048]{1,0:T(8,128)(2,1)S(1)} collective-permute-done((bf16[96,2048]{1,0:T(8,128)(2,1)S(1)}, bf16[96,2048]{1,0:T(8,128)(2,1)S(1)}, u32[]{:S(2)}, u32[]{:S(2)}) %collective-permute-start.14) | collective-permute-done | bytes 393248 | tf_op jit(solution)/shard_map/ppermute | solution.py:290
  55.2 0.8 %collective-permute-done.13.refs_1_ = bf16[96,2048]{1,0:T(8,128)(2,1)S(1)} collective-permute-done((bf16[96,2048]{1,0:T(8,128)(2,1)S(1)}, bf16[96,2048]{1,0:T(8,128)(2,1)S(1)}, u32[]{:S(2)}, u32[]{:S(2)}) %collective-permute-start.13) | collective-permute-done | bytes 393248 | tf_op jit(solution)/shard_map/ppermute | solution.py:290
  56.0 0.7 %work.12 = (f32[256,96]{1,0:T(8,128)S(1)}, f32[8,128]{1,0:T(8,128)S(1)}) custom-call(f32[8,128]{1,0:T(8,128)S(1)} %get-tuple-element.119.mark_ref, bf16[256,4096]{1,0:T(8,128)(2,1)S(1)} %get-tuple-element.120.refs_0_, bf16[96,2048]{1,0:T(8,128)(2,1)S(1)} %collective-permute-done.13.refs_1_, ...), custom_call_target="tpu_custom_call", output_to_operand_aliasing={{1}: (0, {})} | custom-call | flops 1 | bytes 4000000 | tf_op jit(solution)/shard_map/work/pallas_call | solution.py:188
  56.8 0.5 work.13
  57.3 1.2 %collective-permute-done.16 = f32[96,128]{1,0:T(8,128)S(1)} collective-permute-done((f32[96,128]{1,0:T(8,128)S(1)}, f32[96,128]{1,0:T(8,128)S(1)}, u32[]{:S(2)}, u32[]{:S(2)}) %collective-permute-start.16) | collective-permute-done | bytes 49184 | tf_op jit(solution)/shard_map/ppermute | solution.py:314
  58.6 0.6 %select_bitcast_fusion = f32[128,96]{0,1:T(8,128)} fusion(f32[96,128]{1,0:T(8,128)S(1)} %get-tuple-element.127, f32[96,128]{1,0:T(8,128)S(1)} %collective-permute-done.16, f32[96,128]{1,0:T(8,128)S(1)} %get-tuple-element.105), kind=kLoop, calls=%fused_computation | loop fusion | flops 36864 | bytes 196608 | tf_op jit(solution)/shard_map/transpose | solution.py:315
  (25 shorter events, 0.6 us)
Async XLA Ops:
  0.0 1.1 %copy-start = (bf16[1,196608]{1,0:T(2,128)(2,1)S(1)}, bf16[1,196608]{1,0:T(2,128)(2,1)}, u32[]{:S(2)}) copy-start(bf16[1,196608]{1,0:T(2,128)(2,1)} %tile_ref.1) | copy-start | bytes 1179652
  1.8 12.2 %collective-permute-start.1 = (bf16[96,2048]{1,0:T(8,128)(2,1)S(1)}, bf16[96,2048]{1,0:T(8,128)(2,1)S(1)}, u32[]{:S(2)}, u32[]{:S(2)}) collective-permute-start(bf16[96,2048]{1,0:T(8,128)(2,1)S(1)} %transpose_tile.1.refs_2_), channel_id=1, source_target_pairs={{0,8},{2,10},{4,12},{6,14},{8,0},{10,2},{12,4},{14,6},{16,24},{18,... | collective-permute-start | bytes 1179656 | tf_op jit(solution)/shard_map/ppermute | solution.py:290
  4.9 9.1 %collective-permute-start = (bf16[96,2048]{1,0:T(8,128)(2,1)S(1)}, bf16[96,2048]{1,0:T(8,128)(2,1)S(1)}, u32[]{:S(2)}, u32[]{:S(2)}) collective-permute-start(bf16[96,2048]{1,0:T(8,128)(2,1)S(1)} %transpose_tile.1.refs_2_), channel_id=1, source_target_pairs={{8,16},{10,18},{12,20},{14,22},{16,8},{18,10},{20,12},{22,14},{9,1... | collective-permute-start | bytes 1179656 | tf_op jit(solution)/shard_map/ppermute | solution.py:290
  5.6 14.1 %collective-permute-start.3 = (bf16[96,2048]{1,0:T(8,128)(2,1)S(1)}, bf16[96,2048]{1,0:T(8,128)(2,1)S(1)}, u32[]{:S(2)}, u32[]{:S(2)}) collective-permute-start(bf16[96,2048]{1,0:T(8,128)(2,1)S(1)} %transpose_tile.1.refs_2_), channel_id=1, source_target_pairs={{0,4},{2,6},{4,0},{6,2},{8,12},{10,14},{12,8},{14,10},{16,20},{18,... | collective-permute-start | bytes 1179656 | tf_op jit(solution)/shard_map/ppermute | solution.py:290
  7.2 12.5 %collective-permute-start.4 = (bf16[96,2048]{1,0:T(8,128)(2,1)S(1)}, bf16[96,2048]{1,0:T(8,128)(2,1)S(1)}, u32[]{:S(2)}, u32[]{:S(2)}) collective-permute-start(bf16[96,2048]{1,0:T(8,128)(2,1)S(1)} %transpose_tile.1.refs_2_), channel_id=1, source_target_pairs={{0,2},{2,0},{4,6},{6,4},{8,10},{10,8},{12,14},{14,12},{16,18},{18,... | collective-permute-start | bytes 1179656 | tf_op jit(solution)/shard_map/ppermute | solution.py:290
  14.0 14.0 %collective-permute-start.2 = (bf16[96,2048]{1,0:T(8,128)(2,1)S(1)}, bf16[96,2048]{1,0:T(8,128)(2,1)S(1)}, u32[]{:S(2)}, u32[]{:S(2)}) collective-permute-start(bf16[96,2048]{1,0:T(8,128)(2,1)S(1)} %transpose_tile.1.refs_2_), channel_id=1, source_target_pairs={{0,24},{2,26},{4,28},{6,30},{24,0},{26,2},{28,4},{30,6},{1,25},{3,... | collective-permute-start | bytes 1179656 | tf_op jit(solution)/shard_map/ppermute | solution.py:290
  19.7 11.3 %collective-permute-start.9 = (bf16[96,2048]{1,0:T(8,128)(2,1)S(1)}, bf16[96,2048]{1,0:T(8,128)(2,1)S(1)}, u32[]{:S(2)}, u32[]{:S(2)}) collective-permute-start(bf16[96,2048]{1,0:T(8,128)(2,1)S(1)} %collective-permute-done.3.refs_4_), channel_id=1, source_target_pairs={{0,2},{2,0},{4,6},{6,4},{8,10},{10,8},{12,14},{14,12},{16,18},{18,... | collective-permute-start | bytes 1179656 | tf_op jit(solution)/shard_map/ppermute | solution.py:290
  21.3 10.1 %collective-permute-start.8 = (bf16[96,2048]{1,0:T(8,128)(2,1)S(1)}, bf16[96,2048]{1,0:T(8,128)(2,1)S(1)}, u32[]{:S(2)}, u32[]{:S(2)}) collective-permute-start(bf16[96,2048]{1,0:T(8,128)(2,1)S(1)} %collective-permute-done.1.refs_3_), channel_id=1, source_target_pairs={{0,4},{2,6},{4,0},{6,2},{8,12},{10,14},{12,8},{14,10},{16,20},{18,... | collective-permute-start | bytes 1179656 | tf_op jit(solution)/shard_map/ppermute | solution.py:290
  28.0 9.9 %collective-permute-start.7 = (bf16[96,2048]{1,0:T(8,128)(2,1)S(1)}, bf16[96,2048]{1,0:T(8,128)(2,1)S(1)}, u32[]{:S(2)}, u32[]{:S(2)}) collective-permute-start(bf16[96,2048]{1,0:T(8,128)(2,1)S(1)} %get-tuple-element.85.refs_2_), channel_id=1, source_target_pairs={{0,2},{2,0},{4,6},{6,4},{8,10},{10,8},{12,14},{14,12},{16,18},{18,... | collective-permute-start | bytes 1179656 | tf_op jit(solution)/shard_map/ppermute | solution.py:290
  29.5 9.6 %collective-permute-start.6 = (bf16[96,2048]{1,0:T(8,128)(2,1)S(1)}, bf16[96,2048]{1,0:T(8,128)(2,1)S(1)}, u32[]{:S(2)}, u32[]{:S(2)}) collective-permute-start(bf16[96,2048]{1,0:T(8,128)(2,1)S(1)} %get-tuple-element.85.refs_2_), channel_id=1, source_target_pairs={{0,8},{2,10},{4,12},{6,14},{8,0},{10,2},{12,4},{14,6},{16,24},{18,... | collective-permute-start | bytes 1179656 | tf_op jit(solution)/shard_map/ppermute | solution.py:290
  29.5 10.4 %collective-permute-start.5 = (bf16[96,2048]{1,0:T(8,128)(2,1)S(1)}, bf16[96,2048]{1,0:T(8,128)(2,1)S(1)}, u32[]{:S(2)}, u32[]{:S(2)}) collective-permute-start(bf16[96,2048]{1,0:T(8,128)(2,1)S(1)} %get-tuple-element.85.refs_2_), channel_id=1, source_target_pairs={{0,4},{2,6},{4,0},{6,2},{8,12},{10,14},{12,8},{14,10},{16,20},{18,... | collective-permute-start | bytes 1179656 | tf_op jit(solution)/shard_map/ppermute | solution.py:290
  31.4 9.8 %copy-start.1 = (s32[256,2]{0,1:T(2,128)S(1)}, s32[256,2]{0,1:T(2,128)}, u32[]{:S(2)}) copy-start(s32[256,2]{0,1:T(2,128)} %param.8) | copy-start | bytes 6148
  31.4 9.8 %copy-start.2 = (s32[512]{0:T(512)S(1)}, s32[512]{0:T(512)}, u32[]{:S(2)}) copy-start(s32[512]{0:T(512)} %param.9) | copy-start | bytes 6148
  31.4 9.8 %copy-start.3 = (s32[96,2]{0,1:T(2,128)S(1)}, s32[96,2]{0,1:T(2,128)}, u32[]{:S(2)}) copy-start(s32[96,2]{0,1:T(2,128)} %param.10) | copy-start | bytes 2308
  31.4 9.8 %copy-start.4 = (s32[16]{0:T(128)S(1)}, s32[16]{0:T(128)}, u32[]{:S(2)}) copy-start(s32[16]{0:T(128)} %refs_3_.1) | copy-start | bytes 196
  37.9 9.3 %collective-permute-start.10 = (bf16[96,2048]{1,0:T(8,128)(2,1)S(1)}, bf16[96,2048]{1,0:T(8,128)(2,1)S(1)}, u32[]{:S(2)}, u32[]{:S(2)}) collective-permute-start(bf16[96,2048]{1,0:T(8,128)(2,1)S(1)} %collective-permute-done.7.refs_5_), channel_id=1, source_target_pairs={{0,8},{2,10},{4,12},{6,14},{8,0},{10,2},{12,4},{14,6},{16,24},{18,... | collective-permute-start | bytes 1179656 | tf_op jit(solution)/shard_map/ppermute | solution.py:290
  39.1 11.3 %collective-permute-start.11 = (bf16[96,2048]{1,0:T(8,128)(2,1)S(1)}, bf16[96,2048]{1,0:T(8,128)(2,1)S(1)}, u32[]{:S(2)}, u32[]{:S(2)}) collective-permute-start(bf16[96,2048]{1,0:T(8,128)(2,1)S(1)} %collective-permute-done.6.refs_6_), channel_id=1, source_target_pairs={{0,4},{2,6},{4,0},{6,2},{8,12},{10,14},{12,8},{14,10},{16,20},{18,... | collective-permute-start | bytes 1179656 | tf_op jit(solution)/shard_map/ppermute | solution.py:290
  39.9 10.5 %collective-permute-start.12 = (bf16[96,2048]{1,0:T(8,128)(2,1)S(1)}, bf16[96,2048]{1,0:T(8,128)(2,1)S(1)}, u32[]{:S(2)}, u32[]{:S(2)}) collective-permute-start(bf16[96,2048]{1,0:T(8,128)(2,1)S(1)} %collective-permute-done.1.refs_3_), channel_id=1, source_target_pairs={{0,2},{2,0},{4,6},{6,4},{8,10},{10,8},{12,14},{14,12},{16,18},{18,... | collective-permute-start | bytes 1179656 | tf_op jit(solution)/shard_map/ppermute | solution.py:290
  47.2 8.0 %collective-permute-start.14 = (bf16[96,2048]{1,0:T(8,128)(2,1)S(1)}, bf16[96,2048]{1,0:T(8,128)(2,1)S(1)}, u32[]{:S(2)}, u32[]{:S(2)}) collective-permute-start(bf16[96,2048]{1,0:T(8,128)(2,1)S(1)} %collective-permute-done.9.refs_4_), channel_id=1, source_target_pairs={{0,8},{2,10},{4,12},{6,14},{8,0},{10,2},{12,4},{14,6},{16,24},{18,... | collective-permute-start | bytes 1179656 | tf_op jit(solution)/shard_map/ppermute | solution.py:290
  48.1 7.8 %collective-permute-start.13 = (bf16[96,2048]{1,0:T(8,128)(2,1)S(1)}, bf16[96,2048]{1,0:T(8,128)(2,1)S(1)}, u32[]{:S(2)}, u32[]{:S(2)}) collective-permute-start(bf16[96,2048]{1,0:T(8,128)(2,1)S(1)} %collective-permute-done.10.refs_1_), channel_id=1, source_target_pairs={{0,4},{2,6},{4,0},{6,2},{8,12},{10,14},{12,8},{14,10},{16,20},{18,... | collective-permute-start | bytes 1179656 | tf_op jit(solution)/shard_map/ppermute | solution.py:290
  48.9 7.8 %collective-permute-start.15 = (bf16[96,2048]{1,0:T(8,128)(2,1)S(1)}, bf16[96,2048]{1,0:T(8,128)(2,1)S(1)}, u32[]{:S(2)}, u32[]{:S(2)}) collective-permute-start(bf16[96,2048]{1,0:T(8,128)(2,1)S(1)} %collective-permute-done.5.refs_7_), channel_id=1, source_target_pairs={{0,2},{2,0},{4,6},{6,4},{8,10},{10,8},{12,14},{14,12},{16,18},{18,... | collective-permute-start | bytes 1179656 | tf_op jit(solution)/shard_map/ppermute | solution.py:290
  57.3 1.3 %collective-permute-start.16 = (f32[96,128]{1,0:T(8,128)S(1)}, f32[96,128]{1,0:T(8,128)S(1)}, u32[]{:S(2)}, u32[]{:S(2)}) collective-permute-start(f32[96,128]{1,0:T(8,128)S(1)} %get-tuple-element.128), channel_id=1, source_target_pairs={{0,1},{1,0},{2,3},{3,2},{4,5},{5,4},{6,7},{7,6},{8,9},{9,8},{10,11... | collective-permute-start | bytes 147464 | tf_op jit(solution)/shard_map/ppermute | solution.py:314
